TPU v7x, 32 devices: a whole 2x2x4 slice. The times are simulated.
32 devices in a mesh: grp: 2 (over y), tr: 4 (over z), cache: 2 (over x), sub: 2 (over core).
Axes of the slice: x: 2, y: 2, z: 4, core: 2. Of those that a mesh axis runs over, the one named last changes fastest.
Arguments:
- table: bfloat16 [32768, 768], P(('grp', 'tr', 'cache', 'sub')), parts along dimension 0, may hold values from -6 to 6
- requests: int32 [512, 64], P(('grp', 'tr', 'cache', 'sub')), parts along dimension 0, may hold values from 0 to 1023
- counts: int32 [512], P(('grp', 'tr', 'cache', 'sub')), parts along dimension 0, may hold values from 0 to 64, as said below
- nbr_low: int32 [16384, 10], P(('grp', 'tr', 'cache', 'sub')), parts along dimension 0, may hold values from 0 to 1023, as said below
- fan_low: int32 [16384], P(('grp', 'tr', 'cache', 'sub')), parts along dimension 0, may hold values from 1 to 10
- nbr_top: int32 [8192, 25], P(('grp', 'tr', 'cache', 'sub')), parts along dimension 0, may hold values from 0 to 511, as said below
- fan_top: int32 [8192], P(('grp', 'tr', 'cache', 'sub')), parts along dimension 0, may hold values from 1 to 25
- grad_logits: bfloat16 [8192, 153], P(('grp', 'tr', 'cache', 'sub')), parts along dimension 0, may hold values from -0.09375 to 0.09375
- w1_self: bfloat16 [768, 1024], replicated, may hold values from -0.21875 to 0.21875
- w1_neigh: bfloat16 [768, 1024], replicated, may hold values from -0.21875 to 0.21875
- w2_self: bfloat16 [1024, 153], replicated, may hold values from -0.1875 to 0.1875
- w2_neigh: bfloat16 [1024, 153], replicated, may hold values from -0.1875 to 0.1875
Outputs:
- logits: float32 [8192, 153], P(('grp', 'tr', 'cache', 'sub')), parts along dimension 0
- grad_w1_self: bfloat16 [1536, 1024], P('grp'), parts along dimension 0
- grad_w1_neigh: bfloat16 [1536, 1024], P('grp'), parts along dimension 0
- grad_w2_self: bfloat16 [2048, 153], P('grp'), parts along dimension 0
- grad_w2_neigh: bfloat16 [2048, 153], P('grp'), parts along dimension 0
There are 2 independent parts, one for each index of `grp`. A program takes and returns all parts, laid end to end along the dimension named above; an argument that names none is the same for every part. Nothing has to cross between parts.
Inputs may be any that keep to these rules, and one draw needn't show every extreme that they name: `counts`: the live slots are the first ones of each trainer and owner. `nbr_low`: input node indices; entries at k >= fan_low are unused. `nbr_top`: middle node indices; entries at k >= fan_top are unused.
All inputs are finite; a program needn't handle non-finite values.
Results may differ from a plain program's by a relative error of at most 0.0059.
Values may be sent and summed in bfloat16 or wider, within the bound.
No kernel may reach another device: no remote copies, remote signals or barrier semaphores. Data moves between devices by JAX's collectives and lax.ppermute only.
A program may use at most 64 MiB of HBM per device.

v0:
```python
import jax
import jax.numpy as jnp
from jax import lax
from jax.sharding import PartitionSpec as P


def count_tile(neighbours, used, width):
    valid = lax.broadcasted_iota(jnp.int32, neighbours.shape, 1) < used[:, None]
    columns = lax.broadcasted_iota(jnp.int32, (neighbours.shape[0], width), 1)
    total = jnp.zeros((neighbours.shape[0], width), jnp.float32)
    for column in range(neighbours.shape[1]):
        hit = valid[:, column : column + 1] & (neighbours[:, column : column + 1] == columns)
        total = total + jnp.where(hit, 1.0, 0.0).astype(jnp.float32)
    return total.astype(jnp.bfloat16)


def on_device(
    table,
    requests,
    counts,
    nbr_low,
    fan_low,
    nbr_top,
    fan_top,
    grad_logits,
    w1_self,
    w1_neigh,
    w2_self,
    w2_neigh,
):
    peer_count, slot_count = requests.shape
    feat_width = table.shape[1]
    asked = lax.all_to_all(
        requests, ("tr", "cache", "sub"), split_axis=0, concat_axis=0, tiled=True
    )
    picked = jnp.take(table, asked.reshape(-1), axis=0)
    fetched = lax.all_to_all(
        picked.reshape(peer_count, slot_count, feat_width),
        ("tr", "cache", "sub"),
        split_axis=0,
        concat_axis=0,
        tiled=True,
    )
    fetched = fetched.reshape(peer_count * slot_count, feat_width)
    live_slot = (
        lax.broadcasted_iota(jnp.int32, (peer_count, slot_count), 1) < counts[:, None]
    ).reshape(-1)
    inputs = jnp.where(live_slot[:, None], fetched, jnp.zeros((), jnp.bfloat16))
    middle = nbr_low.shape[0]
    seeds = nbr_top.shape[0]
    adj_low = count_tile(nbr_low, fan_low, inputs.shape[0])
    self_low = inputs[:middle]
    div_low = fan_low[:, None].astype(jnp.float32) + 1.0
    mean_low = (
        (
            jnp.dot(adj_low, inputs, preferred_element_type=jnp.float32)
            + self_low.astype(jnp.float32)
        )
        / div_low
    ).astype(jnp.bfloat16)
    pre_act = jnp.dot(self_low, w1_self, preferred_element_type=jnp.float32) + jnp.dot(
        mean_low, w1_neigh, preferred_element_type=jnp.float32
    )
    hidden = jax.nn.silu(pre_act).astype(jnp.bfloat16)
    adj_top = count_tile(nbr_top, fan_top, middle)
    self_top = hidden[:seeds]
    div_top = fan_top[:, None].astype(jnp.float32) + 1.0
    mean_top = (
        (
            jnp.dot(adj_top, hidden, preferred_element_type=jnp.float32)
            + self_top.astype(jnp.float32)
        )
        / div_top
    ).astype(jnp.bfloat16)
    logits = jnp.dot(self_top, w2_self, preferred_element_type=jnp.float32) + jnp.dot(
        mean_top, w2_neigh, preferred_element_type=jnp.float32
    )
    back_top = (
        jnp.dot(grad_logits, w2_neigh.T, preferred_element_type=jnp.float32) / div_top
    ).astype(jnp.bfloat16)
    grad_w2s = jnp.dot(self_top.T, grad_logits, preferred_element_type=jnp.float32)
    grad_w2n = jnp.dot(mean_top.T, grad_logits, preferred_element_type=jnp.float32)
    direct_top = jnp.dot(
        grad_logits, w2_self.T, preferred_element_type=jnp.float32
    ) + back_top.astype(jnp.float32)
    grad_hidden = jnp.dot(adj_top.T, back_top, preferred_element_type=jnp.float32) + jnp.pad(
        direct_top, ((0, middle - seeds), (0, 0))
    )
    sigma = jax.nn.sigmoid(pre_act)
    grad_pre = (grad_hidden * sigma * (1.0 + pre_act * (1.0 - sigma))).astype(jnp.bfloat16)
    grad_w1s = jnp.dot(self_low.T, grad_pre, preferred_element_type=jnp.float32)
    grad_w1n = jnp.dot(mean_low.T, grad_pre, preferred_element_type=jnp.float32)
    sum_w1s, sum_w1n, sum_w2s, sum_w2n = lax.psum(
        (grad_w1s, grad_w1n, grad_w2s, grad_w2n), ("tr", "cache", "sub")
    )
    out_w1s = sum_w1s.astype(jnp.bfloat16)
    out_w1n = sum_w1n.astype(jnp.bfloat16)
    out_w2s = sum_w2s.astype(jnp.bfloat16)
    out_w2n = sum_w2n.astype(jnp.bfloat16)
    return (logits, out_w1s, out_w1n, out_w2s, out_w2n)


def solution(mesh):
    in_specs = (
        P(("grp", "tr", "cache", "sub"), None),
        P(("grp", "tr", "cache", "sub"), None),
        P(("grp", "tr", "cache", "sub")),
        P(("grp", "tr", "cache", "sub"), None),
        P(("grp", "tr", "cache", "sub")),
        P(("grp", "tr", "cache", "sub"), None),
        P(("grp", "tr", "cache", "sub")),
        P(("grp", "tr", "cache", "sub"), None),
        P(),
        P(),
        P(),
        P(),
    )
    out_specs = (
        P(("grp", "tr", "cache", "sub"), None),
        P("grp", None),
        P("grp", None),
        P("grp", None),
        P("grp", None),
    )
    return jax.shard_map(
        on_device, mesh=mesh, in_specs=in_specs, out_specs=out_specs, check_vma=False
    )
```

profile of v0, /device:TPU:9, one launch (start us, length us, event | category | flops | bytes accessed | tf_op | source)
XLA Modules:
  0.0 262.9 jit_solution(9380446450472056043)
XLA Ops:
  0.6 0.0 copy-start
  0.6 11.3 %all_to_all.14 = s32[16,1,64]{2,1,0:T(1,128)S(1)} all-to-all(s32[16,1,64]{2,1,0:T(1,128)} %bitcast.63), channel_id=1, replica_groups=mesh['grp'=2,'tr'=4,'cache'=2,'sub'=2] {'tr','cache','sub'}, dimensions={0} | all-to-all | bytes 8192 | tf_op jit(solution)/shard_map/all_to_all | solution.py:33
  12.0 0.5 broadcast.90
  12.5 0.7 reduce.73
  13.2 0.1 reshape.87
  13.3 6.1 %gather_fusion = bf16[1024,768]{1,0:T(8,128)(2,1)S(1)} fusion(bf16[1024,768]{1,0:T(8,128)(2,1)} %param.12, s32[1024]{0:T(1024)S(1)} %broadcast_clamp_fusion), kind=kCustom, calls=%fused_computation | custom fusion | bytes 3149824 | tf_op jit(solution)/shard_map/jit(_take)/gather | solution.py:36
  19.4 1.4 broadcast_select_fusion
  20.7 5.5 %all-to-all-start.1 = ((bf16[16,64,768]{2,1,0:T(8,128)(2,1)}), bf16[16,64,768]{2,1,0:T(8,128)(2,1)S(1)}, u32[]{:S(2)}, u32[]{:S(2)}) async-start(bf16[16,64,768]{2,1,0:T(8,128)(2,1)} %broadcast_select_fusion), calls=%async_computation.1 | async-start | bytes 3145728 | tf_op jit(solution)/shard_map/all_to_all | solution.py:37
  26.2 1.3 iota_compare_fusion.37
  27.5 1.3 lt.55
  28.8 0.7 iota_compare_fusion.35
  29.5 0.6 slice_reduce_fusion.33
  30.1 0.7 slice_reduce_fusion.34
  30.8 0.7 iota_compare_fusion.36
  31.5 0.7 slice_reduce_fusion.9
  32.2 0.7 convert_add_fusion.1
  32.9 1.3 convert_add_fusion
  34.2 1.5 fusion.71
  35.6 1.8 fusion.70
  37.4 0.0 copy-start.6
  37.4 1.6 fusion.72
  39.1 0.3 fusion.12
  39.4 0.0 copy-done.44
  39.4 0.0 copy-start.3
  39.5 0.8 copy-done.3
  40.2 0.0 copy-done.6
  40.2 1.3 convolution_add_fusion.1
  41.5 20.2 %all-to-all-done.1 = bf16[16,64,768]{2,1,0:T(8,128)(2,1)S(1)} async-done(((bf16[16,64,768]{2,1,0:T(8,128)(2,1)}), bf16[16,64,768]{2,1,0:T(8,128)(2,1)S(1)}, u32[]{:S(2)}, u32[]{:S(2)}) %all-to-all-start.1) | async-done | bytes 1572896 | tf_op jit(solution)/shard_map/all_to_all | solution.py:37
  61.7 1.0 bitcast_select_fusion
  62.7 0.4 copy-done.68
  63.3 1.0 fusion.37
  64.3 0.0 copy-done.8
  64.3 0.0 copy-done.9
  64.3 0.0 copy-done.10
  64.3 0.0 copy-done.11
  64.5 6.6 %divide_convert_fusion = bf16[512,768]{1,0:T(8,128)(2,1)S(1)} fusion(bf16[1024,768]{1,0:T(8,128)(2,1)S(1)} %bitcast_select_fusion, s32[512]{0:T(512)S(1)} %bitcast.72, s32[512]{0:T(512)S(1)} %bitcast.73, s32[512]{0:T(512)S(1)} %bitcast.65, s32[512]{0:T(512)S(1)} %bitcast.66, s32[512]{0:T(512)S(1)} %bitcast.67, s32[512]{0:T(512)S(1)} %bitcast.68, ...), kind=kOutput, calls=%fused_computation.27 | convolution fusion | flops 827850752 | bytes 3173376 | tf_op jit(solution)/shard_map/dot_general | solution.py:56
  71.1 0.0 copy-start.7
  71.1 1.3 multiply_convert_fusion.1
  72.8 0.3 fusion.66
  73.1 0.3 fusion.64
  73.7 0.0 copy-start.1
  73.8 5.9 %fusion.11 = bf16[256,1024]{1,0:T(8,128)(2,1)S(1)} fusion(bf16[512,1024]{1,0:T(8,128)(2,1)S(1)} %get-tuple-element.79, f32[256]{0:T(256)S(1)} %copy-done.45, s32[256]{0:T(256)S(1)} %bitcast.82, s32[256]{0:T(256)S(1)} %bitcast.84, s32[256]{0:T(256)S(1)} %bitcast.88, s32[256]{0:T(256)S(1)} %bitcast.90, s32[256]{0:T(256)S(1)} %bitcast.92, ...), kind=kOutput, calls=%fused_computation.33 | convolution fusion | flops 282591232 | bytes 2132992 | tf_op jit(solution)/shard_map/dot_general | solution.py:70
  79.7 4.9 %multiply_convert_fusion = bf16[512,1024]{1,0:T(8,128)(2,1)S(1)} fusion(f32[512,1024]{1,0:T(8,128)S(1)} %get-tuple-element.80, f32[256,1024]{1,0:T(8,128)S(1)} %copy-done.1, bf16[256,1024]{1,0:T(8,128)(2,1)S(1)} %copy-done.4, s32[256]{0:T(256)S(1)} %bitcast.83, s32[256]{0:T(256)S(1)} %bitcast.85, s32[256]{0:T(256)S(1)} %bitcast.89, s32[256]{0:T(256)S(1)} %bitcast.91, ...), kind=kOutput, calls=%fused_computation.1 | convolution fusion | flops 286785536 | bytes 4750592 | tf_op jit(solution)/shard_map/dot_general | solution.py:86
  84.6 2.7 %fusion.35 = f32[768,1024]{1,0:T(8,128)} fusion(bf16[512,1024]{1,0:T(8,128)(2,1)S(1)} %multiply_convert_fusion, bf16[1024,768]{1,0:T(8,128)(2,1)S(1)} %bitcast_select_fusion), kind=kOutput, calls=%fused_computation.58 | convolution fusion | flops 805306368 | bytes 4980736 | tf_op jit(solution)/shard_map/dot_general | solution.py:91
  87.2 2.7 %fusion.73 = f32[768,1024]{1,0:T(8,128)} fusion(bf16[512,768]{1,0:T(8,128)(2,1)S(1)} %divide_convert_fusion, bf16[512,1024]{1,0:T(8,128)(2,1)S(1)} %multiply_convert_fusion), kind=kOutput, calls=%fused_computation.166 | convolution fusion | flops 805306368 | bytes 4980736 | tf_op jit(solution)/shard_map/dot_general | solution.py:92
  90.0 0.3 fusion.74
  90.2 1.0 convolution_add_fusion.3
  91.2 171.7 %all-reduce.3 = (bf16[768,1024]{1,0:T(8,128)(2,1)}, bf16[768,1024]{1,0:T(8,128)(2,1)}, bf16[1024,153]{0,1:T(8,128)(2,1)}, bf16[1024,153]{0,1:T(8,128)(2,1)}) all-reduce(f32[768,1024]{1,0:T(8,128)} %fusion.35, f32[768,1024]{1,0:T(8,128)} %fusion.73, ...), channel_id=1, replica_groups=mesh['grp'=2,'tr'=4,'cache'=2,'sub'=2] {'tr','cache','sub'}, use_global_device_ids=true, to_apply=%region_0.1 | all-reduce | flops 1886208 | bytes 11317248 | tf_op jit(solution)/shard_map/psum | solution.py:93
  (128 shorter events, 0.3 us)
Async XLA Ops:
  0.6 70.4 %copy-start = (bf16[768,1024]{1,0:T(8,128)(2,1)S(1)}, bf16[768,1024]{1,0:T(8,128)(2,1)}, u32[]{:S(2)}) copy-start(bf16[768,1024]{1,0:T(8,128)(2,1)} %param.21) | copy-start | bytes 4718596
  20.7 18.4 %copy-start.2 = (bf16[256,153]{0,1:T(8,128)(2,1)S(1)}, bf16[256,153]{0,1:T(8,128)(2,1)}, u32[]{:S(2)}) copy-start(bf16[256,153]{0,1:T(8,128)(2,1)} %param.19) | copy-start | bytes 235012
  20.7 18.4 %copy-start.5 = (bf16[1024,153]{0,1:T(8,128)(2,1)S(1)}, bf16[1024,153]{0,1:T(8,128)(2,1)}, u32[]{:S(2)}) copy-start(bf16[1024,153]{0,1:T(8,128)(2,1)} %param.23) | copy-start | bytes 940036
  20.7 40.9 %all-to-all-start.1 = ((bf16[16,64,768]{2,1,0:T(8,128)(2,1)}), bf16[16,64,768]{2,1,0:T(8,128)(2,1)S(1)}, u32[]{:S(2)}, u32[]{:S(2)}) async-start(bf16[16,64,768]{2,1,0:T(8,128)(2,1)} %broadcast_select_fusion), calls=%async_computation.1 | async-start | bytes 3145728 | tf_op jit(solution)/shard_map/all_to_all | solution.py:37
  32.9 6.6 %copy-start.44 = (f32[256]{0:T(256)}, f32[256]{0:T(256)S(1)}, u32[]{:S(2)}) copy-start(f32[256]{0:T(256)S(1)} %convert_add_fusion.1) | copy-start | bytes 3076
  37.4 2.8 %copy-start.6 = (bf16[1024,153]{0,1:T(8,128)(2,1)S(1)}, bf16[1024,153]{0,1:T(8,128)(2,1)}, u32[]{:S(2)}) copy-start(bf16[1024,153]{0,1:T(8,128)(2,1)} %param.22) | copy-start | bytes 940036
  61.7 1.4 copy-start.68
  63.1 1.2 copy-start.8
  63.1 1.2 copy-start.9
  63.1 1.2 copy-start.10
  63.1 1.2 copy-start.11
  63.1 1.2 copy-start.12
  63.1 1.2 copy-start.13
  63.1 1.2 copy-start.14
  63.1 1.2 copy-start.15
  63.1 1.2 copy-start.16
  63.2 1.2 copy-start.17
  63.2 1.2 copy-start.18
  63.2 1.2 copy-start.58
  63.2 1.2 copy-start.59
  63.2 1.2 copy-start.60
  63.2 1.2 copy-start.61
  63.2 1.2 copy-start.62
  63.2 1.2 copy-start.63
  63.2 1.2 copy-start.64
  63.2 1.2 copy-start.65
  63.3 1.2 copy-start.66
  63.3 1.2 copy-start.67
  71.1 1.7 copy-start.7
  72.4 1.0 copy-start.19
  72.4 1.0 copy-start.20
  72.4 1.0 copy-start.21
  72.4 1.0 copy-start.22
  72.4 1.0 copy-start.23
  72.4 1.0 copy-start.24
  72.4 1.0 copy-start.25
  72.5 1.0 copy-start.26
  72.5 1.0 copy-start.27
  72.5 1.0 copy-start.28
  72.5 1.0 copy-start.29
  72.5 1.0 copy-start.30
  72.5 1.0 copy-start.31
  72.5 1.0 copy-start.32
  72.5 1.0 copy-start.33
  72.5 1.0 copy-start.34
  73.7 5.9 %copy-start.1 = (f32[256,1024]{1,0:T(8,128)S(1)}, f32[256,1024]{1,0:T(8,128)}, u32[]{:S(2)}) copy-start(f32[256,1024]{1,0:T(8,128)} %convolution_add_fusion.1) | copy-start | bytes 3145732
  73.7 5.9 %copy-start.4 = (bf16[256,1024]{1,0:T(8,128)(2,1)S(1)}, bf16[256,1024]{1,0:T(8,128)(2,1)}, u32[]{:S(2)}) copy-start(bf16[256,1024]{1,0:T(8,128)(2,1)} %copy-done.3) | copy-start | bytes 1572868
  73.7 5.9 %copy-start.57 = (pred[256]{0:T(512)(128)(4,1)S(1)}, pred[256]{0:T(512)(128)(4,1)}, u32[]{:S(2)}) copy-start(pred[256]{0:T(512)(128)(4,1)} %get-tuple-element.16) | copy-start | bytes 772
  (22 other events, 21.1 us)
where the time goes:
time: 264 us; the launch traced here: 263 us
  blocking collectives  183 us (69%)
  matrix products  28.5 us (11%)
  waiting for transfers between devices  20.2 us (8%)
  local copies, waits for them, and re-layouts  16.4 us (6%)
  other arithmetic  7.68 us (3%)
  starting transfers between devices  5.46 us (2%)
    psum x1, blocking collectives, on_device(): lax.psum((grad_w1s, grad_w1n, grad_w2s, grad_w2n), ('tr', 'cache', 'sub'))  172 us
    all_to_all x1, waiting for transfers between devices, on_device(): lax.all_to_all(picked.reshape(peer_count, slot_count, feat_width), ('tr',...  20.2 us
    all_to_all x1, blocking collectives, on_device(): lax.all_to_all(requests, ('tr', 'cache', 'sub'), split_axis=0, concat_axi...  11.3 us
    dot_general x1, matrix products, on_device(): jnp.dot(adj_low, inputs, preferred_element_type=jnp.float32)  6.58 us
    gather x1, local copies, waits for them, and re-layouts, on_device(): picked = jnp.take(table, asked.reshape(-1), axis=0)  6.09 us
    dot_general x1, matrix products, on_device(): jnp.dot(adj_top, hidden, preferred_element_type=jnp.float32)  5.89 us
    all_to_all x1, starting transfers between devices, on_device(): lax.all_to_all(picked.reshape(peer_count, slot_count, feat_width), ('tr',...  5.46 us
  transfers between devices with their start and end apart: 1, of which 1 were waited for; matrix products, arithmetic and copies ran while one was open for 6% of the time, Pallas kernels for 0%

commit v1 on v0

v1 whole, which is shorter than its diff:
```python
import functools

import jax
import jax.numpy as jnp
from jax import lax
from jax.experimental import pallas as pl
from jax.experimental.pallas import tpu as pltpu
from jax.sharding import PartitionSpec as P

LANES = 128
BLOCKS = 8
TRAINERS = ("tr", "cache", "sub")
F32, BF16 = jnp.float32, jnp.bfloat16
VMEM = pl.BlockSpec(memory_space=pltpu.VMEM)
SMEM = pl.BlockSpec(memory_space=pltpu.SMEM)


def params(mebibytes):
    return pltpu.CompilerParams(vmem_limit_bytes=mebibytes * 1024 * 1024)


def tdot(lhs, rhs):
    return lax.dot_general(lhs, rhs, (((0,), (0,)), ((), ())), preferred_element_type=F32)


def count_tile(neighbours, used, width):
    valid = lax.broadcasted_iota(jnp.int32, neighbours.shape, 1) < used[:, None]
    columns = lax.broadcasted_iota(jnp.int32, (neighbours.shape[0], width), 1)
    total = jnp.zeros((neighbours.shape[0], width), jnp.float32)
    for column in range(neighbours.shape[1]):
        hit = valid[:, column : column + 1] & (neighbours[:, column : column + 1] == columns)
        total = total + jnp.where(hit, 1.0, 0.0).astype(jnp.float32)
    return total.astype(jnp.bfloat16)


def swap(array, axis, size, distance):
    return lax.ppermute(array, axis, [(i, i ^ distance) for i in range(size)])


def axis_bits(axis, size):
    return [(axis, size, 1 << k) for k in range(size.bit_length() - 1)]


def bit_of(step):
    axis, _, distance = step
    return lax.rem(lax.div(lax.axis_index(axis), distance), 2)


def place_of(order):
    place = jnp.int32(0)
    for step in order[:3]:
        place = 2 * place + bit_of(step)
    return place


def scatter_blocks(send, keep, order):
    for step in order[:3]:
        got = swap(send, *step)
        half = keep.shape[0] // 2
        if half:
            send = (keep[half:] + got[half:].astype(F32)).astype(BF16)
            keep = keep[:half] + got[:half].astype(F32)
        else:
            keep = keep + got.astype(F32)
    for step in order[3:]:
        half = keep.shape[1] // 2
        bit = bit_of(step)
        other = lax.dynamic_slice_in_dim(keep, (1 - bit) * half, half, 1).astype(BF16)
        keep = lax.dynamic_slice_in_dim(keep, bit * half, half, 1)
        keep = keep + swap(other, *step).astype(F32)
    return keep.astype(BF16)


def gather_blocks(share, order):
    for step in order[3:][::-1]:
        got = swap(share, *step)
        low = bit_of(step) == 0
        share = jnp.concatenate([jnp.where(low, share, got), jnp.where(low, got, share)], 1)
    for step in order[:3][::-1]:
        share = jnp.concatenate([share, swap(share, *step)], 0)
    return share


def product_kernel(rows, first, place, mine, got, grad, grad_got, *outs):
    base = 0
    for which, out in enumerate(outs):
        at = place[which]
        low = lax.rem(at, 2)
        span = slice(base, base + rows[which])
        for pair in range(BLOCKS // 4):
            column = jnp.bitwise_xor(first // 2 + pair, at // 2)
            where = pl.ds(pl.multiple_of(column * 2 * LANES, 2 * LANES), 2 * LANES)
            value = tdot(mine[:, span], grad[:, where]) + tdot(got[:, span], grad_got[:, where])
            value = value.astype(out.dtype)
            out[2 * pair + low] = value[:, :LANES]
            out[2 * pair + 1 - low] = value[:, LANES:]
        base += rows[which]


def products(rows, first, dtype, place, mine, got, grad, grad_got):
    return pl.pallas_call(
        functools.partial(product_kernel, rows, first),
        out_shape=[jax.ShapeDtypeStruct((BLOCKS // 2, r, LANES), dtype) for r in rows],
        in_specs=[SMEM, VMEM, VMEM, VMEM, VMEM],
        out_specs=[VMEM] * len(rows),
        compiler_params=params(32),
        name="grad_send" if first else "grad_keep",
    )(place, mine, got, grad, grad_got)


def place_kernel(info, *refs):
    pieces, outs = refs[:-4], refs[-4:]
    core = info[0]
    base = 0
    for which in range(len(pieces) // 2):
        own, other = pieces[2 * which], pieces[2 * which + 1]
        last = which == len(pieces) // 2 - 1
        first_out, second_out = (outs[2], outs[3]) if last else (outs[0], outs[1])
        height = first_out.shape[0] if last else own.shape[1]
        base = 0 if last else base
        span = slice(base, base + height)
        for position in range(BLOCKS):
            column = jnp.bitwise_xor(info[1 + which], position)
            where = pl.ds(pl.multiple_of(column * LANES, LANES), LANES)
            a, b = own[position, :height], other[position, :height]
            first_out[span, where] = jnp.where(core == 0, a, b)
            second_out[span, where] = jnp.where(core == 0, b, a)
        base += height


def place_blocks(info, pieces, shapes):
    return pl.pallas_call(
        place_kernel,
        out_shape=[jax.ShapeDtypeStruct(s, BF16) for s in shapes],
        in_specs=[SMEM] + [VMEM] * len(pieces),
        out_specs=[VMEM] * 4,
        compiler_params=params(32),
        name="place_blocks",
    )(info, *pieces)


def on_device(sizes, table, requests, counts, nbr_low, fan_low, nbr_top, fan_top, grad_logits,
              w1_self, w1_neigh, w2_self, w2_neigh):
    peer_count, slot_count = requests.shape
    feat_width = table.shape[1]
    middle, seeds, classes = nbr_low.shape[0], nbr_top.shape[0], grad_logits.shape[1]
    cache_bits, tr_bits = axis_bits("cache", sizes["cache"]), axis_bits("tr", sizes["tr"])
    across, along = cache_bits + tr_bits, tr_bits + cache_bits
    core = lax.axis_index("sub")
    core_step = ("sub", 2, 1)

    asked = lax.all_to_all(requests, TRAINERS, split_axis=0, concat_axis=0, tiled=True)
    picked = jnp.take(table, asked.reshape(-1), axis=0, mode="clip")
    fetched = lax.all_to_all(
        picked.reshape(peer_count, slot_count, feat_width), TRAINERS,
        split_axis=0, concat_axis=0, tiled=True,
    ).reshape(peer_count * slot_count, feat_width)

    adj_low = count_tile(nbr_low, fan_low, peer_count * slot_count)
    adj_top = count_tile(nbr_top, fan_top, middle)
    div_low = fan_low[:, None].astype(F32) + 1.0
    div_top = fan_top[:, None].astype(F32) + 1.0
    adj_low, adj_top = lax.optimization_barrier((adj_low, adj_top))
    back_top = (
        jnp.dot(grad_logits, w2_neigh.T, preferred_element_type=F32) / div_top
    ).astype(BF16)
    direct_top = jnp.dot(grad_logits, w2_self.T, preferred_element_type=F32) + back_top.astype(F32)
    grad_hidden = jnp.dot(adj_top.T, back_top, preferred_element_type=F32) + jnp.pad(
        direct_top, ((0, middle - seeds), (0, 0))
    )
    padded = -(-classes // 32) * 32
    cotangent = jnp.pad(grad_logits, ((0, 0), (0, padded - classes)))
    cotangent_got = swap(cotangent, *core_step)
    grad_hidden, cotangent, cotangent_got = lax.optimization_barrier(
        (grad_hidden, cotangent, cotangent_got)
    )

    live_slot = (
        lax.broadcasted_iota(jnp.int32, (peer_count, slot_count), 1) < counts[:, None]
    ).reshape(-1)
    inputs = jnp.where(live_slot[:, None], fetched, jnp.zeros((), BF16))
    self_low = inputs[:middle]
    mean_low = (
        (jnp.dot(adj_low, inputs, preferred_element_type=F32) + self_low.astype(F32)) / div_low
    ).astype(BF16)
    low_mine = jnp.where(core == 0, self_low, mean_low)
    low_got = swap(jnp.where(core == 0, mean_low, self_low), *core_step)
    pre_act = jnp.dot(self_low, w1_self, preferred_element_type=F32) + jnp.dot(
        mean_low, w1_neigh, preferred_element_type=F32
    )
    hidden = jax.nn.silu(pre_act).astype(BF16)
    sigma = jax.nn.sigmoid(pre_act)
    grad_pre = (grad_hidden * sigma * (1.0 + pre_act * (1.0 - sigma))).astype(BF16)
    grad_pre_got = swap(grad_pre, *core_step)

    place = jnp.stack([place_of(across), place_of(along)])
    rows = (feat_width // 2, feat_width // 2)
    sends = products(rows, BLOCKS // 2, BF16, place, low_mine, low_got, grad_pre, grad_pre_got)
    keeps = products(rows, 0, F32, place, low_mine, low_got, grad_pre, grad_pre_got)

    self_top = hidden[:seeds]
    mean_top = (
        (jnp.dot(adj_top, hidden, preferred_element_type=F32) + self_top.astype(F32)) / div_top
    ).astype(BF16)
    logits = jnp.dot(self_top, w2_self, preferred_element_type=F32) + jnp.dot(
        mean_top, w2_neigh, preferred_element_type=F32
    )
    top_mine = jnp.where(core == 0, self_top, mean_top)
    top_got = swap(jnp.where(core == 0, mean_top, self_top), *core_step)
    top_place = place[:1]
    top_send = products(
        (padded,), BLOCKS // 2, BF16, top_place, cotangent, cotangent_got, top_mine, top_got
    )
    top_keep = products((padded,), 0, F32, top_place, cotangent, cotangent_got, top_mine, top_got)

    orders = (across, along, across)
    pieces = []
    for send, keep, order in zip(list(sends) + list(top_send), list(keeps) + list(top_keep), orders):
        whole = gather_blocks(scatter_blocks(send, keep, order), order)
        pieces += [whole, swap(whole, *core_step)]
    info = jnp.concatenate([core[None].astype(jnp.int32), place, top_place])
    hidden_width = w1_self.shape[1]
    w1_shape, w2_shape = (feat_width, hidden_width), (classes, hidden_width)
    out = place_blocks(info, pieces, (w1_shape, w1_shape, w2_shape, w2_shape))
    return (logits, out[0], out[1], out[2].T, out[3].T)


def solution(mesh):
    split, whole = P(("grp", "tr", "cache", "sub"), None), P(("grp", "tr", "cache", "sub"))
    in_specs = (split, split, whole, split, whole, split, whole, split, P(), P(), P(), P())
    out_specs = (split, P("grp", None), P("grp", None), P("grp", None), P("grp", None))
    return jax.shard_map(
        functools.partial(on_device, dict(mesh.shape)),
        mesh=mesh,
        in_specs=in_specs,
        out_specs=out_specs,
        check_vma=False,
    )
```

time: 264 us -> 156 us (0.59)
  the two profiles are of different devices: /device:TPU:9 before, /device:TPU:0 now
where the time goes in v1:
time: 156 us; the launch traced here: 155 us
  waiting for transfers between devices  53.5 us (34%)
  starting transfers between devices  43.3 us (28%)
  local copies, waits for them, and re-layouts  18.2 us (12%)
  other arithmetic  17.4 us (11%)
  Pallas kernels  11.6 us (7%)
  matrix products  10.3 us (7%)
    ppermute x25, waiting for transfers between devices, swap(): return lax.ppermute(array, axis, [(i, i ^ distance) for i in range(size)])  38.3 us
    ppermute x25, starting transfers between devices, swap(): return lax.ppermute(array, axis, [(i, i ^ distance) for i in range(size)])  29.9 us
    all_to_all x1, waiting for transfers between devices, on_device(): lax.all_to_all(picked.reshape(peer_count, slot_count, feat_width), TRAINE...  15.2 us
    convert_element_type x2, other arithmetic, count_tile(): return total.astype(jnp.bfloat16)  11.5 us
    pallas_call x4, Pallas kernels, products(): pl.pallas_call(functools.partial(product_kernel, rows, first), out_shape=...  8.35 us
    all_to_all x1, starting transfers between devices, on_device(): lax.all_to_all(requests, TRAINERS, split_axis=0, concat_axis=0, tiled=True)  7.5 us
    unnamed x43, local copies, waits for them, and re-layouts  6.89 us
    all_to_all x1, starting transfers between devices, on_device(): lax.all_to_all(picked.reshape(peer_count, slot_count, feat_width), TRAINE...  5.89 us
  transfers between devices with their start and end apart: 27, of which 15 were waited for; matrix products, arithmetic and copies ran while one was open for 22% of the time, Pallas kernels for 5%

profile of v1, /device:TPU:0, one launch (start us, length us, event | category | flops | bytes accessed | tf_op | source)
XLA Modules:
  0.0 155.4 jit_solution(13516948508262173590)
XLA Ops:
  0.6 7.5 %all-to-all-start = ((s32[16,1,64]{2,1,0:T(1,128)}), s32[16,1,64]{2,1,0:T(1,128)S(1)}, u32[]{:S(2)}, u32[]{:S(2)}) async-start(s32[16,1,64]{2,1,0:T(1,128)} %bitcast.71), calls=%async_computation | async-start | bytes 16384 | tf_op jit(solution)/shard_map/all_to_all | solution.py:152
  8.2 1.0 copy.19
  9.7 1.0 fusion.54
  12.1 1.6 %fusion.52 = (s32[256,1]{0,1:T(1,128)S(1)}, s32[256,1]{0,1:T(1,128)S(1)}, s32[256,1]{0,1:T(1,128)S(1)}, s32[256,1]{0,1:T(1,128)S(1)}, s32[256,1]{0,1:T(1,128)S(1...) fusion(s32[256,25]{0,1:T(8,128)} %param.17), kind=kLoop, calls=%fused_computation.169 | loop fusion | bytes 38912 | tf_op jit(solution)/shard_map/slice | solution.py:31
  16.9 5.2 %gather_fusion = bf16[1024,768]{1,0:T(8,128)(2,1)} fusion(bf16[1024,768]{1,0:T(8,128)(2,1)S(1)} %copy-done, s32[1024]{0:T(1024)S(1)} %broadcast_clamp_fusion), kind=kCustom, calls=%fused_computation | custom fusion | bytes 3149824 | tf_op jit(solution)/shard_map/jit(_take)/gather | solution.py:153
  22.1 5.9 %all-to-all-start.1 = ((bf16[16,64,768]{2,1,0:T(8,128)(2,1)}), bf16[16,64,768]{2,1,0:T(8,128)(2,1)S(1)}, u32[]{:S(2)}, u32[]{:S(2)}) async-start(bf16[16,64,768]{2,1,0:T(8,128)(2,1)} %bitcast.60), calls=%async_computation.1 | async-start | bytes 3145728 | tf_op jit(solution)/shard_map/all_to_all | solution.py:154
  28.9 4.8 %add_convert_fusion.1 = bf16[256,512]{1,0:T(8,128)(2,1)S(1)} fusion(s32[256]{0:T(256)S(1)} %bitcast.95, s32[256]{0:T(256)S(1)} %bitcast.96, s32[256]{0:T(256)S(1)} %bitcast.73, s32[256]{0:T(256)S(1)} %bitcast.74, s32[256]{0:T(256)S(1)} %bitcast.75, s32[256]{0:T(256)S(1)} %bitcast.76, s32[256]{0:T(256)} %bitcast.77, s32[256]{0:T(256)} %bitcast.78, ...), kind=kLoop, calls=%fused_computation.40 | loop fusion | flops 13107200 | bytes 294144 | tf_op jit(solution)/shard_map/convert_element_type | solution.py:33
  33.7 6.8 %add_convert_fusion = bf16[512,1024]{1,0:T(8,128)(2,1)} fusion(s32[512]{0:T(512)S(1)} %bitcast.69, s32[512]{0:T(512)S(1)} %bitcast.70, s32[512]{0:T(512)S(1)} %bitcast.62, s32[512]{0:T(512)S(1)} %bitcast.63, s32[512]{0:T(512)S(1)} %bitcast.64, s32[512]{0:T(512)S(1)} %bitcast.65, s32[512]{0:T(512)S(1)} %bitcast.66, s32[512]{0:T(512)S(1)} %bitcast.67, ...), kind=kLoop, calls=%fused_computation.5 | loop fusion | flops 20971520 | bytes 1074176 | tf_op jit(solution)/shard_map/convert_element_type | solution.py:33
  41.2 1.3 fusion.12
  42.9 1.8 %pad_add_fusion = f32[512,1024]{1,0:T(8,128)} fusion(f32[256,1024]{1,0:T(8,128)S(1)} %convolution_add_fusion.1, bf16[256,512]{1,0:T(8,128)(2,1)S(1)} %add_convert_fusion.1, bf16[256,1024]{1,0:T(8,128)(2,1)S(1)} %fusion.12), kind=kOutput, calls=%fused_computation.2 | convolution fusion | flops 268959744 | bytes 3932160 | tf_op jit(solution)/shard_map/dot_general | solution.py:168
  44.8 15.2 %all-to-all-done.1 = bf16[16,64,768]{2,1,0:T(8,128)(2,1)S(1)} async-done(((bf16[16,64,768]{2,1,0:T(8,128)(2,1)}), bf16[16,64,768]{2,1,0:T(8,128)(2,1)S(1)}, u32[]{:S(2)}, u32[]{:S(2)}) %all-to-all-start.1) | async-done | bytes 1572896 | tf_op jit(solution)/shard_map/all_to_all | solution.py:154
  60.3 1.1 copy-done.20
  61.4 1.0 fusion.38
  62.6 2.0 %broadcast_select_fusion = (bf16[512,768]{1,0:T(8,128)(2,1)}, bf16[512,768]{1,0:T(8,128)(2,1)S(1)}, bf16[512,768]{1,0:T(8,128)(2,1)S(1)}) fusion(pred[]{:T(512)S(6)} %eq.461, bf16[1024,768]{1,0:T(8,128)(2,1)S(1)} %bitcast_select_fusion, f32[512]{0:T(512)S(1)} %convert_add_fusion.2, bf16[512,1024]{1,0:T(8,128)(2,1)S(1)} %copy-done.8), kind=kOutput, calls=%fused_computation.38 | convolution fusion | flops 807665664 | bytes 5769217 | tf_op jit(solution)/shard_map/dot_general | solution.py:184
  64.6 1.0 convolution_add_fusion
  66.2 1.0 multiply_convert_fusion
  68.1 1.6 %broadcast_select_fusion.2 = (bf16[256,1024]{1,0:T(8,128)(2,1)}, bf16[256,1024]{1,0:T(8,128)(2,1)}, bf16[256,1024]{1,0:T(8,128)(2,1)}) fusion(pred[]{:T(512)S(6)} %eq.461, bf16[512,1024]{1,0:T(8,128)(2,1)S(1)} %get-tuple-element.69, f32[256]{0:T(256)S(1)} %convert_add_fusion.3, bf16[256,512]{1,0:T(8,128)(2,1)S(1)} %copy-done.12), kind=kOutput, calls=%fused_computation.91 | convolution fusion | flops 270008320 | bytes 3408897 | tf_op jit(solution)/shard_map/dot_general | solution.py:203
  70.2 2.4 %collective-permute-done.17.grad_got = bf16[256,1024]{1,0:T(8,128)(2,1)} collective-permute-done((bf16[256,1024]{1,0:T(8,128)(2,1)}, bf16[256,1024]{1,0:T(8,128)(2,1)}, u32[]{:S(2)}, u32[]{:S(2)}) %collective-permute-start.17) | collective-permute-done | bytes 524320 | tf_op jit(solution)/shard_map/ppermute | solution.py:37
  72.5 1.0 copy-done.1
  74.5 2.0 %grad_send.3 = bf16[4,160,128]{2,1,0:T(8,128)(2,1)} custom-call(s32[1]{0:T(128)} %bitcast.39.place, bf16[256,160]{1,0:T(8,128)(2,1)S(1)} %pad.9.mine, bf16[256,160]{1,0:T(8,128)(2,1)S(1)} %copy-done.4, bf16[256,1024]{1,0:T(8,128)(2,1)S(1)} %copy-done.1, bf16[256,1024]{1,0:T(8,128)(2,1)} %collective-permute-done.17.grad_got), custom_call_target="tpu_custom_call" | custom-call | tf_op jit(solution)/shard_map/grad_send/pallas_call | solution.py:101
  76.5 2.7 %collective-permute-start.18 = (bf16[4,160,128]{2,1,0:T(8,128)(2,1)}, bf16[4,160,128]{2,1,0:T(8,128)(2,1)}, u32[]{:S(2)}, u32[]{:S(2)}) collective-permute-start(bf16[4,160,128]{2,1,0:T(8,128)(2,1)} %grad_send.3), channel_id=1, source_target_pairs={{0,2},{2,0},{1,3},{3,1},{4,6},{6,4},{5,7},{7,5},{8,10},{10,8},{9,1... | collective-permute-start | bytes 491528 | tf_op jit(solution)/shard_map/ppermute | solution.py:37
  79.3 1.0 copy-done.2
  81.2 1.4 grad_keep.3
  82.6 2.5 %grad_send.2 = (bf16[4,384,128]{2,1,0:T(8,128)(2,1)S(1)}, bf16[4,384,128]{2,1,0:T(8,128)(2,1)S(1)}) custom-call(s32[2]{0:T(128)S(1)} %pad_add_fusion.2.place, bf16[512,768]{1,0:T(8,128)(2,1)S(1)} %get-tuple-element.67.mine, bf16[512,768]{1,0:T(8,128)(2,1)} %collective-permute-done.got, bf16[512,1024]{1,0:T(8,128)(2,1)S(1)} %get-tuple-element.68.grad, ...), custom_call_target="tpu_custom_call" | custom-call | tf_op jit(solution)/shard_map/grad_send/pallas_call | solution.py:101
  86.2 4.4 %collective-permute-start.19 = (bf16[2,160,128]{2,1,0:T(8,128)(2,1)S(1)}, bf16[2,160,128]{2,1,0:T(8,128)(2,1)S(1)}, u32[]{:S(2)}, u32[]{:S(2)}) collective-permute-start(bf16[2,160,128]{2,1,0:T(8,128)(2,1)S(1)} %get-tuple-element.76), channel_id=1, source_target_pairs={{0,4},{4,0},{8,12},{12,8},{1,5},{5,1},{9,13},{13,9},{2,6},{6,2},{1... | collective-permute-start | bytes 245768 | tf_op jit(solution)/shard_map/ppermute | solution.py:37
  90.7 2.9 %collective-permute-done.19 = bf16[2,160,128]{2,1,0:T(8,128)(2,1)S(1)} collective-permute-done((bf16[2,160,128]{2,1,0:T(8,128)(2,1)S(1)}, bf16[2,160,128]{2,1,0:T(8,128)(2,1)S(1)}, u32[]{:S(2)}, u32[]{:S(2)}) %collective-permute-start.19) | collective-permute-done | bytes 81952 | tf_op jit(solution)/shard_map/ppermute | solution.py:37
  93.5 4.3 %collective-permute-start.20 = (bf16[1,160,128]{2,1,0:T(8,128)(2,1)S(1)}, bf16[1,160,128]{2,1,0:T(8,128)(2,1)S(1)}, u32[]{:S(2)}, u32[]{:S(2)}) collective-permute-start(bf16[1,160,128]{2,1,0:T(8,128)(2,1)S(1)} %fusion.49), channel_id=1, source_target_pairs={{0,8},{4,12},{8,0},{12,4},{1,9},{5,13},{9,1},{13,5},{2,10},{6,14},... | collective-permute-start | bytes 122888 | tf_op jit(solution)/shard_map/ppermute | solution.py:37
  97.9 2.5 %grad_keep.2 = (f32[4,384,128]{2,1,0:T(8,128)S(1)}, f32[4,384,128]{2,1,0:T(8,128)S(1)}) custom-call(s32[2]{0:T(128)S(1)} %pad_add_fusion.2.place, bf16[512,768]{1,0:T(8,128)(2,1)S(1)} %get-tuple-element.67.mine, bf16[512,768]{1,0:T(8,128)(2,1)} %collective-permute-done.got, bf16[512,1024]{1,0:T(8,128)(2,1)S(1)} %get-tuple-element.68.grad, ...), custom_call_target="tpu_custom_call" | custom-call | tf_op jit(solution)/shard_map/grad_keep/pallas_call | solution.py:101
  100.7 2.8 %collective-permute-done.10 = bf16[4,384,128]{2,1,0:T(8,128)(2,1)S(1)} collective-permute-done((bf16[4,384,128]{2,1,0:T(8,128)(2,1)S(1)}, bf16[4,384,128]{2,1,0:T(8,128)(2,1)S(1)}, u32[]{:S(2)}, u32[]{:S(2)}) %collective-permute-start.10) | collective-permute-done | bytes 393248 | tf_op jit(solution)/shard_map/ppermute | solution.py:37
  103.6 2.8 %collective-permute-start.11 = (bf16[2,384,128]{2,1,0:T(8,128)(2,1)S(1)}, bf16[2,384,128]{2,1,0:T(8,128)(2,1)S(1)}, u32[]{:S(2)}, u32[]{:S(2)}) collective-permute-start(bf16[2,384,128]{2,1,0:T(8,128)(2,1)S(1)} %get-tuple-element.72), channel_id=1, source_target_pairs={{0,8},{4,12},{8,0},{12,4},{1,9},{5,13},{9,1},{13,5},{2,10},{6,14},... | collective-permute-start | bytes 589832 | tf_op jit(solution)/shard_map/ppermute | solution.py:37
  106.3 3.2 %collective-permute-done.4 = bf16[2,384,128]{2,1,0:T(8,128)(2,1)S(1)} collective-permute-done((bf16[2,384,128]{2,1,0:T(8,128)(2,1)S(1)}, bf16[2,384,128]{2,1,0:T(8,128)(2,1)S(1)}, u32[]{:S(2)}, u32[]{:S(2)}) %collective-permute-start.4) | collective-permute-done | bytes 196640 | tf_op jit(solution)/shard_map/ppermute | solution.py:37
  109.6 1.8 %collective-permute-start.5 = (bf16[1,384,128]{2,1,0:T(8,128)(2,1)S(1)}, bf16[1,384,128]{2,1,0:T(8,128)(2,1)S(1)}, u32[]{:S(2)}, u32[]{:S(2)}) collective-permute-start(bf16[1,384,128]{2,1,0:T(8,128)(2,1)S(1)} %fusion.45), channel_id=1, source_target_pairs={{0,8},{4,12},{8,0},{12,4},{1,9},{5,13},{9,1},{13,5},{2,10},{6,14},... | collective-permute-start | bytes 294920 | tf_op jit(solution)/shard_map/ppermute | solution.py:37
  111.4 6.1 %collective-permute-done.11 = bf16[2,384,128]{2,1,0:T(8,128)(2,1)S(1)} collective-permute-done((bf16[2,384,128]{2,1,0:T(8,128)(2,1)S(1)}, bf16[2,384,128]{2,1,0:T(8,128)(2,1)S(1)}, u32[]{:S(2)}, u32[]{:S(2)}) %collective-permute-start.11) | collective-permute-done | bytes 196640 | tf_op jit(solution)/shard_map/ppermute | solution.py:37
  117.5 1.7 %collective-permute-start.12 = (bf16[1,384,128]{2,1,0:T(8,128)(2,1)S(1)}, bf16[1,384,128]{2,1,0:T(8,128)(2,1)S(1)}, u32[]{:S(2)}, u32[]{:S(2)}) collective-permute-start(bf16[1,384,128]{2,1,0:T(8,128)(2,1)S(1)} %fusion.42), channel_id=1, source_target_pairs={{0,2},{2,0},{1,3},{3,1},{4,6},{6,4},{5,7},{7,5},{8,10},{10,8},{9,1... | collective-permute-start | bytes 294920 | tf_op jit(solution)/shard_map/ppermute | solution.py:37
  119.3 2.9 %collective-permute-done.12 = bf16[1,384,128]{2,1,0:T(8,128)(2,1)S(1)} collective-permute-done((bf16[1,384,128]{2,1,0:T(8,128)(2,1)S(1)}, bf16[1,384,128]{2,1,0:T(8,128)(2,1)S(1)}, u32[]{:S(2)}, u32[]{:S(2)}) %collective-permute-start.12) | collective-permute-done | bytes 98336 | tf_op jit(solution)/shard_map/ppermute | solution.py:37
  122.2 1.6 %collective-permute-start.13 = (bf16[1,384,128]{2,1,0:T(8,128)(2,1)S(1)}, bf16[1,384,128]{2,1,0:T(8,128)(2,1)S(1)}, u32[]{:S(2)}, u32[]{:S(2)}) collective-permute-start(bf16[1,384,128]{2,1,0:T(8,128)(2,1)S(1)} %fusion.44), channel_id=1, source_target_pairs={{0,2},{2,0},{1,3},{3,1},{4,6},{6,4},{5,7},{7,5},{8,10},{10,8},{9,1... | collective-permute-start | bytes 294920 | tf_op jit(solution)/shard_map/ppermute | solution.py:37
  123.9 1.2 collective-permute-done.6
  125.2 1.7 %collective-permute-done.13 = bf16[1,384,128]{2,1,0:T(8,128)(2,1)S(1)} collective-permute-done((bf16[1,384,128]{2,1,0:T(8,128)(2,1)S(1)}, bf16[1,384,128]{2,1,0:T(8,128)(2,1)S(1)}, u32[]{:S(2)}, u32[]{:S(2)}) %collective-permute-start.13) | collective-permute-done | bytes 98336 | tf_op jit(solution)/shard_map/ppermute | solution.py:37
  127.7 2.3 %collective-permute-start.21 = (bf16[1,160,128]{2,1,0:T(8,128)(2,1)S(1)}, bf16[1,160,128]{2,1,0:T(8,128)(2,1)S(1)}, u32[]{:S(2)}, u32[]{:S(2)}) collective-permute-start(bf16[1,160,128]{2,1,0:T(8,128)(2,1)S(1)} %fusion.51), channel_id=1, source_target_pairs={{0,8},{4,12},{8,0},{12,4},{1,9},{5,13},{9,1},{13,5},{2,10},{6,14},... | collective-permute-start | bytes 122888 | tf_op jit(solution)/shard_map/ppermute | solution.py:37
  130.0 2.1 %collective-permute-done.7 = bf16[2,384,128]{2,1,0:T(8,128)(2,1)S(1)} collective-permute-done((bf16[2,384,128]{2,1,0:T(8,128)(2,1)S(1)}, bf16[2,384,128]{2,1,0:T(8,128)(2,1)S(1)}, u32[]{:S(2)}, u32[]{:S(2)}) %collective-permute-start.7) | collective-permute-done | bytes 196640 | tf_op jit(solution)/shard_map/ppermute | solution.py:37
  132.2 1.0 collective-permute-start.8
  133.2 3.0 %collective-permute-done.14 = bf16[2,384,128]{2,1,0:T(8,128)(2,1)S(1)} collective-permute-done((bf16[2,384,128]{2,1,0:T(8,128)(2,1)S(1)}, bf16[2,384,128]{2,1,0:T(8,128)(2,1)S(1)}, u32[]{:S(2)}, u32[]{:S(2)}) %collective-permute-start.14) | collective-permute-done | bytes 196640 | tf_op jit(solution)/shard_map/ppermute | solution.py:37
  136.7 1.8 %collective-permute-start.22 = (bf16[2,160,128]{2,1,0:T(8,128)(2,1)S(1)}, bf16[2,160,128]{2,1,0:T(8,128)(2,1)S(1)}, u32[]{:S(2)}, u32[]{:S(2)}) collective-permute-start(bf16[2,160,128]{2,1,0:T(8,128)(2,1)S(1)} %pad_maximum_fusion.8), channel_id=1, source_target_pairs={{0,4},{4,0},{8,12},{12,8},{1,5},{5,1},{9,13},{13,9},{2,6},{6,2},{1... | collective-permute-start | bytes 245768 | tf_op jit(solution)/shard_map/ppermute | solution.py:37
  138.5 6.5 %collective-permute-done.22 = bf16[2,160,128]{2,1,0:T(8,128)(2,1)S(1)} collective-permute-done((bf16[2,160,128]{2,1,0:T(8,128)(2,1)S(1)}, bf16[2,160,128]{2,1,0:T(8,128)(2,1)S(1)}, u32[]{:S(2)}, u32[]{:S(2)}) %collective-permute-start.22) | collective-permute-done | bytes 81952 | tf_op jit(solution)/shard_map/ppermute | solution.py:37
  145.0 1.6 %collective-permute-start.23 = (bf16[4,160,128]{2,1,0:T(8,128)(2,1)S(1)}, bf16[4,160,128]{2,1,0:T(8,128)(2,1)S(1)}, u32[]{:S(2)}, u32[]{:S(2)}) collective-permute-start(bf16[4,160,128]{2,1,0:T(8,128)(2,1)S(1)} %pad_maximum_fusion.7), channel_id=1, source_target_pairs={{0,2},{2,0},{1,3},{3,1},{4,6},{6,4},{5,7},{7,5},{8,10},{10,8},{9,1... | collective-permute-start | bytes 491528 | tf_op jit(solution)/shard_map/ppermute | solution.py:37
  147.6 2.9 %collective-permute-done.23 = bf16[4,160,128]{2,1,0:T(8,128)(2,1)S(1)} collective-permute-done((bf16[4,160,128]{2,1,0:T(8,128)(2,1)S(1)}, bf16[4,160,128]{2,1,0:T(8,128)(2,1)S(1)}, u32[]{:S(2)}, u32[]{:S(2)}) %collective-permute-start.23) | collective-permute-done | bytes 163872 | tf_op jit(solution)/shard_map/ppermute | solution.py:37
  150.9 1.0 convolution_add_fusion.3
  152.1 3.3 %place_blocks.1 = (bf16[768,1024]{1,0:T(8,128)(2,1)}, bf16[768,1024]{1,0:T(8,128)(2,1)}, bf16[153,1024]{1,0:T(8,128)(2,1)}, bf16[153,1024]{1,0:T(8,128)(2,1)}) custom-call(s32[4]{0:T(128)S(1)} %pad_add_fusion.1.info, bf16[8,384,128]{2,1,0:T(8,128)(2,1)S(1)} %pad_maximum_fusion.refs_0_, bf16[8,384,128]{2,1,0:T(8,128)(2,1)S(1)} %collective-permute-done.9.refs_1_, ...), custom_call_target="tpu_custom_call" | custom-call | tf_op jit(solution)/shard_map/place_blocks/pallas_call | solution.py:132
  (105 shorter events, 16.2 us)
Async XLA Ops:
  0.6 16.3 %copy-start = (bf16[1024,768]{1,0:T(8,128)(2,1)S(1)}, bf16[1024,768]{1,0:T(8,128)(2,1)}, u32[]{:S(2)}) copy-start(bf16[1024,768]{1,0:T(8,128)(2,1)} %param.12) | copy-start | bytes 4718596
  0.6 15.0 %all-to-all-start = ((s32[16,1,64]{2,1,0:T(1,128)}), s32[16,1,64]{2,1,0:T(1,128)S(1)}, u32[]{:S(2)}, u32[]{:S(2)}) async-start(s32[16,1,64]{2,1,0:T(1,128)} %bitcast.71), calls=%async_computation | async-start | bytes 16384 | tf_op jit(solution)/shard_map/all_to_all | solution.py:152
  9.2 35.7 %collective-permute-start.1 = (bf16[256,160]{1,0:T(8,128)(2,1)S(1)}, bf16[256,160]{1,0:T(8,128)(2,1)S(1)}, u32[]{:S(2)}, u32[]{:S(2)}) collective-permute-start(bf16[256,160]{1,0:T(8,128)(2,1)S(1)} %pad.9.mine), channel_id=1, source_target_pairs={{0,1},{1,0},{2,3},{3,2},{4,5},{5,4},{6,7},{7,6},{8,9},{9,8},{10,11... | collective-permute-start | bytes 245768 | tf_op jit(solution)/shard_map/ppermute | solution.py:37
  22.1 19.1 %copy-start.18 = (s32[512]{0:T(512)S(1)}, s32[512]{0:T(512)}, u32[]{:S(2)}) copy-start(s32[512]{0:T(512)} %param.16) | copy-start | bytes 6148
  22.1 19.1 %copy-start.14 = (bf16[256,153]{0,1:T(8,128)(2,1)S(1)}, bf16[256,153]{0,1:T(8,128)(2,1)}, u32[]{:S(2)}) copy-start(bf16[256,153]{0,1:T(8,128)(2,1)} %param.19) | copy-start | bytes 235012
  22.1 37.9 %all-to-all-start.1 = ((bf16[16,64,768]{2,1,0:T(8,128)(2,1)}), bf16[16,64,768]{2,1,0:T(8,128)(2,1)S(1)}, u32[]{:S(2)}, u32[]{:S(2)}) async-start(bf16[16,64,768]{2,1,0:T(8,128)(2,1)} %bitcast.60), calls=%async_computation.1 | async-start | bytes 3145728 | tf_op jit(solution)/shard_map/all_to_all | solution.py:154
  33.7 9.2 %copy-start.11 = (bf16[256,512]{1,0:T(8,128)(2,1)}, bf16[256,512]{1,0:T(8,128)(2,1)S(1)}, u32[]{:S(2)}) copy-start(bf16[256,512]{1,0:T(8,128)(2,1)S(1)} %add_convert_fusion.1) | copy-start | bytes 786436
  40.4 2.1 %copy-start.16 = (bf16[1024,153]{0,1:T(8,128)(2,1)S(1)}, bf16[1024,153]{0,1:T(8,128)(2,1)}, u32[]{:S(2)}) copy-start(bf16[1024,153]{0,1:T(8,128)(2,1)} %param.22) | copy-start | bytes 940036
  42.8 1.8 %copy-start.19 = (s32[16]{0:T(128)S(1)}, s32[16]{0:T(128)}, u32[]{:S(2)}) copy-start(s32[16]{0:T(128)} %param.14) | copy-start | bytes 196
  44.8 17.6 %copy-start.3 = (bf16[256,160]{1,0:T(8,128)(2,1)}, bf16[256,160]{1,0:T(8,128)(2,1)S(1)}, u32[]{:S(2)}) copy-start(bf16[256,160]{1,0:T(8,128)(2,1)S(1)} %collective-permute-done.1.got) | copy-start | bytes 245764
  60.0 1.4 copy-start.20
  61.4 1.2 copy-start.8
  62.6 2.0 %copy-start.7 = (bf16[768,1024]{1,0:T(8,128)(2,1)S(1)}, bf16[768,1024]{1,0:T(8,128)(2,1)}, u32[]{:S(2)}) copy-start(bf16[768,1024]{1,0:T(8,128)(2,1)} %param.21) | copy-start | bytes 4718596
  64.6 1.6 %copy-start.6 = (f32[512,1024]{1,0:T(8,128)S(1)}, f32[512,1024]{1,0:T(8,128)}, u32[]{:S(2)}) copy-start(f32[512,1024]{1,0:T(8,128)} %pad_add_fusion) | copy-start | bytes 6291460
  66.2 1.9 %copy-start.12 = (bf16[256,512]{1,0:T(8,128)(2,1)S(1)}, bf16[256,512]{1,0:T(8,128)(2,1)}, u32[]{:S(2)}) copy-start(bf16[256,512]{1,0:T(8,128)(2,1)} %copy-done.11) | copy-start | bytes 786436
  67.2 2.6 %copy-start.9 = (bf16[512,1024]{1,0:T(8,128)(2,1)}, bf16[512,1024]{1,0:T(8,128)(2,1)S(1)}, u32[]{:S(2)}) copy-start(bf16[512,1024]{1,0:T(8,128)(2,1)S(1)} %get-tuple-element.69) | copy-start | bytes 3145732
  67.2 15.4 %collective-permute-start.2 = (bf16[512,1024]{1,0:T(8,128)(2,1)S(1)}, bf16[512,1024]{1,0:T(8,128)(2,1)}, u32[]{:S(2)}, u32[]{:S(2)}) collective-permute-start(bf16[512,1024]{1,0:T(8,128)(2,1)S(1)} %get-tuple-element.68.grad), channel_id=1, source_target_pairs={{0,1},{1,0},{2,3},{3,2},{4,5},{5,4},{6,7},{7,6},{8,9},{9,8},{10,11... | collective-permute-start | bytes 3145736 | tf_op jit(solution)/shard_map/ppermute | solution.py:37
  68.0 14.5 %collective-permute-start = (bf16[512,768]{1,0:T(8,128)(2,1)}, bf16[512,768]{1,0:T(8,128)(2,1)}, u32[]{:S(2)}, u32[]{:S(2)}) collective-permute-start(bf16[512,768]{1,0:T(8,128)(2,1)} %get-tuple-element.66), channel_id=1, source_target_pairs={{0,1},{1,0},{2,3},{3,2},{4,5},{5,4},{6,7},{7,6},{8,9},{9,8},{10,11... | collective-permute-start | bytes 2359304 | tf_op jit(solution)/shard_map/ppermute | solution.py:37
  69.7 2.8 %collective-permute-start.17 = (bf16[256,1024]{1,0:T(8,128)(2,1)}, bf16[256,1024]{1,0:T(8,128)(2,1)}, u32[]{:S(2)}, u32[]{:S(2)}) collective-permute-start(bf16[256,1024]{1,0:T(8,128)(2,1)} %get-tuple-element.70), channel_id=1, source_target_pairs={{0,1},{1,0},{2,3},{3,2},{4,5},{5,4},{6,7},{7,6},{8,9},{9,8},{10,11... | collective-permute-start | bytes 1572872 | tf_op jit(solution)/shard_map/ppermute | solution.py:37
  72.5 1.0 copy-start.1
  73.6 0.9 copy-start.4
  76.5 8.7 %collective-permute-start.18 = (bf16[4,160,128]{2,1,0:T(8,128)(2,1)}, bf16[4,160,128]{2,1,0:T(8,128)(2,1)}, u32[]{:S(2)}, u32[]{:S(2)}) collective-permute-start(bf16[4,160,128]{2,1,0:T(8,128)(2,1)} %grad_send.3), channel_id=1, source_target_pairs={{0,2},{2,0},{1,3},{3,1},{4,6},{6,4},{5,7},{7,5},{8,10},{10,8},{9,1... | collective-permute-start | bytes 491528 | tf_op jit(solution)/shard_map/ppermute | solution.py:37
  79.3 1.0 copy-start.2
  80.3 0.9 copy-start.5
  85.1 15.2 %collective-permute-start.3 = (bf16[4,384,128]{2,1,0:T(8,128)(2,1)S(1)}, bf16[4,384,128]{2,1,0:T(8,128)(2,1)S(1)}, u32[]{:S(2)}, u32[]{:S(2)}) collective-permute-start(bf16[4,384,128]{2,1,0:T(8,128)(2,1)S(1)} %get-tuple-element.22), channel_id=1, source_target_pairs={{0,2},{2,0},{1,3},{3,1},{4,6},{6,4},{5,7},{7,5},{8,10},{10,8},{9,1... | collective-permute-start | bytes 1179656 | tf_op jit(solution)/shard_map/ppermute | solution.py:37
  86.2 7.4 %collective-permute-start.19 = (bf16[2,160,128]{2,1,0:T(8,128)(2,1)S(1)}, bf16[2,160,128]{2,1,0:T(8,128)(2,1)S(1)}, u32[]{:S(2)}, u32[]{:S(2)}) collective-permute-start(bf16[2,160,128]{2,1,0:T(8,128)(2,1)S(1)} %get-tuple-element.76), channel_id=1, source_target_pairs={{0,4},{4,0},{8,12},{12,8},{1,5},{5,1},{9,13},{13,9},{2,6},{6,2},{1... | collective-permute-start | bytes 245768 | tf_op jit(solution)/shard_map/ppermute | solution.py:37
  90.6 12.9 %collective-permute-start.10 = (bf16[4,384,128]{2,1,0:T(8,128)(2,1)S(1)}, bf16[4,384,128]{2,1,0:T(8,128)(2,1)S(1)}, u32[]{:S(2)}, u32[]{:S(2)}) collective-permute-start(bf16[4,384,128]{2,1,0:T(8,128)(2,1)S(1)} %get-tuple-element.24), channel_id=1, source_target_pairs={{0,4},{4,0},{8,12},{12,8},{1,5},{5,1},{9,13},{13,9},{2,6},{6,2},{1... | collective-permute-start | bytes 1179656 | tf_op jit(solution)/shard_map/ppermute | solution.py:37
  93.5 34.1 %collective-permute-start.20 = (bf16[1,160,128]{2,1,0:T(8,128)(2,1)S(1)}, bf16[1,160,128]{2,1,0:T(8,128)(2,1)S(1)}, u32[]{:S(2)}, u32[]{:S(2)}) collective-permute-start(bf16[1,160,128]{2,1,0:T(8,128)(2,1)S(1)} %fusion.49), channel_id=1, source_target_pairs={{0,8},{4,12},{8,0},{12,4},{1,9},{5,13},{9,1},{13,5},{2,10},{6,14},... | collective-permute-start | bytes 122888 | tf_op jit(solution)/shard_map/ppermute | solution.py:37
  100.4 9.1 %collective-permute-start.4 = (bf16[2,384,128]{2,1,0:T(8,128)(2,1)S(1)}, bf16[2,384,128]{2,1,0:T(8,128)(2,1)S(1)}, u32[]{:S(2)}, u32[]{:S(2)}) collective-permute-start(bf16[2,384,128]{2,1,0:T(8,128)(2,1)S(1)} %get-tuple-element.74), channel_id=1, source_target_pairs={{0,4},{4,0},{8,12},{12,8},{1,5},{5,1},{9,13},{13,9},{2,6},{6,2},{1... | collective-permute-start | bytes 589832 | tf_op jit(solution)/shard_map/ppermute | solution.py:37
  103.6 13.9 %collective-permute-start.11 = (bf16[2,384,128]{2,1,0:T(8,128)(2,1)S(1)}, bf16[2,384,128]{2,1,0:T(8,128)(2,1)S(1)}, u32[]{:S(2)}, u32[]{:S(2)}) collective-permute-start(bf16[2,384,128]{2,1,0:T(8,128)(2,1)S(1)} %get-tuple-element.72), channel_id=1, source_target_pairs={{0,8},{4,12},{8,0},{12,4},{1,9},{5,13},{9,1},{13,5},{2,10},{6,14},... | collective-permute-start | bytes 589832 | tf_op jit(solution)/shard_map/ppermute | solution.py:37
  109.6 9.5 %collective-permute-start.5 = (bf16[1,384,128]{2,1,0:T(8,128)(2,1)S(1)}, bf16[1,384,128]{2,1,0:T(8,128)(2,1)S(1)}, u32[]{:S(2)}, u32[]{:S(2)}) collective-permute-start(bf16[1,384,128]{2,1,0:T(8,128)(2,1)S(1)} %fusion.45), channel_id=1, source_target_pairs={{0,8},{4,12},{8,0},{12,4},{1,9},{5,13},{9,1},{13,5},{2,10},{6,14},... | collective-permute-start | bytes 294920 | tf_op jit(solution)/shard_map/ppermute | solution.py:37
  117.5 4.7 %collective-permute-start.12 = (bf16[1,384,128]{2,1,0:T(8,128)(2,1)S(1)}, bf16[1,384,128]{2,1,0:T(8,128)(2,1)S(1)}, u32[]{:S(2)}, u32[]{:S(2)}) collective-permute-start(bf16[1,384,128]{2,1,0:T(8,128)(2,1)S(1)} %fusion.42), channel_id=1, source_target_pairs={{0,2},{2,0},{1,3},{3,1},{4,6},{6,4},{5,7},{7,5},{8,10},{10,8},{9,1... | collective-permute-start | bytes 294920 | tf_op jit(solution)/shard_map/ppermute | solution.py:37
  119.2 5.9 %collective-permute-start.6 = (bf16[1,384,128]{2,1,0:T(8,128)(2,1)S(1)}, bf16[1,384,128]{2,1,0:T(8,128)(2,1)S(1)}, u32[]{:S(2)}, u32[]{:S(2)}) collective-permute-start(bf16[1,384,128]{2,1,0:T(8,128)(2,1)S(1)} %fusion.47), channel_id=1, source_target_pairs={{0,8},{4,12},{8,0},{12,4},{1,9},{5,13},{9,1},{13,5},{2,10},{6,14},... | collective-permute-start | bytes 294920 | tf_op jit(solution)/shard_map/ppermute | solution.py:37
  122.2 4.7 %collective-permute-start.13 = (bf16[1,384,128]{2,1,0:T(8,128)(2,1)S(1)}, bf16[1,384,128]{2,1,0:T(8,128)(2,1)S(1)}, u32[]{:S(2)}, u32[]{:S(2)}) collective-permute-start(bf16[1,384,128]{2,1,0:T(8,128)(2,1)S(1)} %fusion.44), channel_id=1, source_target_pairs={{0,2},{2,0},{1,3},{3,1},{4,6},{6,4},{5,7},{7,5},{8,10},{10,8},{9,1... | collective-permute-start | bytes 294920 | tf_op jit(solution)/shard_map/ppermute | solution.py:37
  125.1 7.0 %collective-permute-start.7 = (bf16[2,384,128]{2,1,0:T(8,128)(2,1)S(1)}, bf16[2,384,128]{2,1,0:T(8,128)(2,1)S(1)}, u32[]{:S(2)}, u32[]{:S(2)}) collective-permute-start(bf16[2,384,128]{2,1,0:T(8,128)(2,1)S(1)} %pad_maximum_fusion.5), channel_id=1, source_target_pairs={{0,4},{4,0},{8,12},{12,8},{1,5},{5,1},{9,13},{13,9},{2,6},{6,2},{1... | collective-permute-start | bytes 589832 | tf_op jit(solution)/shard_map/ppermute | solution.py:37
  126.9 9.3 %collective-permute-start.14 = (bf16[2,384,128]{2,1,0:T(8,128)(2,1)S(1)}, bf16[2,384,128]{2,1,0:T(8,128)(2,1)S(1)}, u32[]{:S(2)}, u32[]{:S(2)}) collective-permute-start(bf16[2,384,128]{2,1,0:T(8,128)(2,1)S(1)} %pad_maximum_fusion.6), channel_id=1, source_target_pairs={{0,8},{4,12},{8,0},{12,4},{1,9},{5,13},{9,1},{13,5},{2,10},{6,14},... | collective-permute-start | bytes 589832 | tf_op jit(solution)/shard_map/ppermute | solution.py:37
  127.7 9.0 %collective-permute-start.21 = (bf16[1,160,128]{2,1,0:T(8,128)(2,1)S(1)}, bf16[1,160,128]{2,1,0:T(8,128)(2,1)S(1)}, u32[]{:S(2)}, u32[]{:S(2)}) collective-permute-start(bf16[1,160,128]{2,1,0:T(8,128)(2,1)S(1)} %fusion.51), channel_id=1, source_target_pairs={{0,8},{4,12},{8,0},{12,4},{1,9},{5,13},{9,1},{13,5},{2,10},{6,14},... | collective-permute-start | bytes 122888 | tf_op jit(solution)/shard_map/ppermute | solution.py:37
  132.2 14.5 %collective-permute-start.8 = (bf16[4,384,128]{2,1,0:T(8,128)(2,1)S(1)}, bf16[4,384,128]{2,1,0:T(8,128)(2,1)S(1)}, u32[]{:S(2)}, u32[]{:S(2)}) collective-permute-start(bf16[4,384,128]{2,1,0:T(8,128)(2,1)S(1)} %pad_maximum_fusion.2), channel_id=1, source_target_pairs={{0,2},{2,0},{1,3},{3,1},{4,6},{6,4},{5,7},{7,5},{8,10},{10,8},{9,1... | collective-permute-start | bytes 1179656 | tf_op jit(solution)/shard_map/ppermute | solution.py:37
  136.3 10.6 %collective-permute-start.15 = (bf16[4,384,128]{2,1,0:T(8,128)(2,1)S(1)}, bf16[4,384,128]{2,1,0:T(8,128)(2,1)S(1)}, u32[]{:S(2)}, u32[]{:S(2)}) collective-permute-start(bf16[4,384,128]{2,1,0:T(8,128)(2,1)S(1)} %pad_maximum_fusion.3), channel_id=1, source_target_pairs={{0,4},{4,0},{8,12},{12,8},{1,5},{5,1},{9,13},{13,9},{2,6},{6,2},{1... | collective-permute-start | bytes 1179656 | tf_op jit(solution)/shard_map/ppermute | solution.py:37
  136.7 13.9 %copy-start.10 = (bf16[512,1024]{1,0:T(8,128)(2,1)S(1)}, bf16[512,1024]{1,0:T(8,128)(2,1)}, u32[]{:S(2)}) copy-start(bf16[512,1024]{1,0:T(8,128)(2,1)} %copy-done.9) | copy-start | bytes 3145732
  136.7 13.9 %copy-start.17 = (bf16[1024,153]{0,1:T(8,128)(2,1)S(1)}, bf16[1024,153]{0,1:T(8,128)(2,1)}, u32[]{:S(2)}) copy-start(bf16[1024,153]{0,1:T(8,128)(2,1)} %param.22) | copy-start | bytes 940036
  136.7 8.3 %collective-permute-start.22 = (bf16[2,160,128]{2,1,0:T(8,128)(2,1)S(1)}, bf16[2,160,128]{2,1,0:T(8,128)(2,1)S(1)}, u32[]{:S(2)}, u32[]{:S(2)}) collective-permute-start(bf16[2,160,128]{2,1,0:T(8,128)(2,1)S(1)} %pad_maximum_fusion.8), channel_id=1, source_target_pairs={{0,4},{4,0},{8,12},{12,8},{1,5},{5,1},{9,13},{13,9},{2,6},{6,2},{1... | collective-permute-start | bytes 245768 | tf_op jit(solution)/shard_map/ppermute | solution.py:37
  145.0 5.9 %copy-start.13 = (bf16[256,1024]{1,0:T(8,128)(2,1)S(1)}, bf16[256,1024]{1,0:T(8,128)(2,1)}, u32[]{:S(2)}) copy-start(bf16[256,1024]{1,0:T(8,128)(2,1)} %get-tuple-element.114) | copy-start | bytes 1572868
  145.0 5.9 %copy-start.15 = (bf16[1024,153]{0,1:T(8,128)(2,1)S(1)}, bf16[1024,153]{0,1:T(8,128)(2,1)}, u32[]{:S(2)}) copy-start(bf16[1024,153]{0,1:T(8,128)(2,1)} %param.23) | copy-start | bytes 940036
  145.0 5.4 %collective-permute-start.23 = (bf16[4,160,128]{2,1,0:T(8,128)(2,1)S(1)}, bf16[4,160,128]{2,1,0:T(8,128)(2,1)S(1)}, u32[]{:S(2)}, u32[]{:S(2)}) collective-permute-start(bf16[4,160,128]{2,1,0:T(8,128)(2,1)S(1)} %pad_maximum_fusion.7), channel_id=1, source_target_pairs={{0,2},{2,0},{1,3},{3,1},{4,6},{6,4},{5,7},{7,5},{8,10},{10,8},{9,1... | collective-permute-start | bytes 491528 | tf_op jit(solution)/shard_map/ppermute | solution.py:37
  146.7 5.4 %collective-permute-start.9 = (bf16[8,384,128]{2,1,0:T(8,128)(2,1)S(1)}, bf16[8,384,128]{2,1,0:T(8,128)(2,1)S(1)}, u32[]{:S(2)}, u32[]{:S(2)}) collective-permute-start(bf16[8,384,128]{2,1,0:T(8,128)(2,1)S(1)} %pad_maximum_fusion.refs_0_), channel_id=1, source_target_pairs={{0,1},{1,0},{2,3},{3,2},{4,5},{5,4},{6,7},{7,6},{8,9},{9,8},{10,11... | collective-permute-start | bytes 2359304 | tf_op jit(solution)/shard_map/ppermute | solution.py:37
  146.9 5.2 %collective-permute-start.16 = (bf16[8,384,128]{2,1,0:T(8,128)(2,1)S(1)}, bf16[8,384,128]{2,1,0:T(8,128)(2,1)S(1)}, u32[]{:S(2)}, u32[]{:S(2)}) collective-permute-start(bf16[8,384,128]{2,1,0:T(8,128)(2,1)S(1)} %pad_maximum_fusion.1.refs_2_), channel_id=1, source_target_pairs={{0,1},{1,0},{2,3},{3,2},{4,5},{5,4},{6,7},{7,6},{8,9},{9,8},{10,11... | collective-permute-start | bytes 2359304 | tf_op jit(solution)/shard_map/ppermute | solution.py:37
  150.4 1.7 %collective-permute-start.24 = (bf16[8,160,128]{2,1,0:T(8,128)(2,1)S(1)}, bf16[8,160,128]{2,1,0:T(8,128)(2,1)S(1)}, u32[]{:S(2)}, u32[]{:S(2)}) collective-permute-start(bf16[8,160,128]{2,1,0:T(8,128)(2,1)S(1)} %pad_maximum_fusion.4.refs_4_), channel_id=1, source_target_pairs={{0,1},{1,0},{2,3},{3,2},{4,5},{5,4},{6,7},{7,6},{8,9},{9,8},{10,11... | collective-permute-start | bytes 983048 | tf_op jit(solution)/shard_map/ppermute | solution.py:37

commit v2 on v0

v2 whole, which is shorter than its diff:
```python
import functools

import jax
import jax.numpy as jnp
from jax import lax
from jax.experimental import pallas as pl
from jax.experimental.pallas import tpu as pltpu
from jax.sharding import PartitionSpec as P

LANES = 128
CORE_STEP = ("sub", 2, 1)
BLOCKS = 8
TRAINERS = ("tr", "cache", "sub")
F32, BF16 = jnp.float32, jnp.bfloat16
VMEM = pl.BlockSpec(memory_space=pltpu.VMEM)
SMEM = pl.BlockSpec(memory_space=pltpu.SMEM)
ANY = pl.BlockSpec(memory_space=pl.ANY)


def params(mebibytes):
    return pltpu.CompilerParams(vmem_limit_bytes=mebibytes * 1024 * 1024)


def tdot(lhs, rhs):
    return lax.dot_general(lhs, rhs, (((0,), (0,)), ((), ())), preferred_element_type=F32)


def swap(array, axis, size, distance):
    return lax.ppermute(array, axis, [(i, i ^ distance) for i in range(size)])


def axis_bits(axis, size):
    return [(axis, size, 1 << k) for k in range(size.bit_length() - 1)]


def bit_of(step):
    axis, _, distance = step
    return lax.rem(lax.div(lax.axis_index(axis), distance), 2)


def kernel_call(body, name, outs, in_specs, mebibytes, *operands, **kwargs):
    return pl.pallas_call(
        body,
        out_shape=[jax.ShapeDtypeStruct(*out) for out in outs],
        in_specs=in_specs,
        out_specs=kwargs.pop("out_specs", [VMEM] * len(outs)),
        compiler_params=params(mebibytes),
        cost_estimate=pl.CostEstimate(flops=10**10, bytes_accessed=10**7, transcendentals=0),
        name=name,
        **kwargs,
    )(*operands)


def fold_kernel(got, keep, after, send, kept):
    half = kept.shape[0]
    send[...] = (keep[half:] + got[half:].astype(F32)).astype(BF16)
    kept[...] = keep[:half] + got[:half].astype(F32)


def add_kernel(got, keep, after, out):
    out[...] = (keep[...] + got[...].astype(F32)).astype(out.dtype)


def meet_kernel(mine, got, after, out):
    out[0] = (mine[0].astype(F32) + got[1].astype(F32)).astype(BF16)
    out[1] = (mine[1].astype(F32) + got[0].astype(F32)).astype(BF16)


def join_kernel(near, far, after, out):
    half = near.shape[0]
    out[:half] = near[...]
    out[half:] = far[...]


def deep_sum(keep, order):
    extra = order[3:]
    got = swap(keep[1:].astype(BF16), *order[2])
    share = keep[:1] + got.astype(F32)
    for step in extra:
        half = share.shape[1] // 2
        bit = bit_of(step)
        other = lax.dynamic_slice_in_dim(share, (1 - bit) * half, half, 1).astype(BF16)
        share = lax.dynamic_slice_in_dim(share, bit * half, half, 1)
        share = share + swap(other, *step).astype(F32)
    share = share.astype(BF16)
    for step in extra[::-1]:
        got = swap(share, *step)
        low = bit_of(step) == 0
        share = jnp.concatenate([jnp.where(low, share, got), jnp.where(low, got, share)], 1)
    return jnp.concatenate([share, swap(share, *order[2])], 0)


class Piece:
    def __init__(self, order, got, keep):
        self.order, self.got, self.keep = order, got, keep

    def first(self, after):
        count, rows, lanes = self.keep.shape
        send, self.keep = kernel_call(
            fold_kernel, "fold", [((count // 2, rows, lanes), BF16), ((count // 2, rows, lanes), F32)],
            [VMEM, VMEM, ANY], 16, self.got, self.keep, after,
        )
        self.got = swap(send, *self.order[1])
        return send

    def second(self, after):
        deep = len(self.order) > 3
        self.keep, = kernel_call(
            add_kernel, "add", [(self.keep.shape, F32 if deep else BF16)],
            [VMEM, VMEM, ANY], 16, self.got, self.keep, after,
        )
        if not deep:
            self.got = swap(self.keep, *self.order[2])
        return self.keep

    def meet(self, after):
        if len(self.order) > 3:
            self.keep = deep_sum(self.keep, self.order)
        else:
            self.keep, = kernel_call(
                meet_kernel, "meet", [(self.keep.shape, BF16)],
                [VMEM, VMEM, ANY], 16, self.keep, self.got, after,
            )
        self.got = swap(self.keep, *self.order[1])
        return self.keep

    def join(self, after):
        count, rows, lanes = self.keep.shape
        near, = kernel_call(
            join_kernel, "join", [((2 * count, rows, lanes), BF16)],
            [VMEM, VMEM, ANY], 16, self.keep, self.got, after,
        )
        far = swap(near, *self.order[0])
        self.blocks = (near, far, swap(near, *CORE_STEP))
        return near


def pair_of(info):
    return lax.rem(lax.div(info[1], 2), 2), lax.rem(info[1], 2)


def gradient(span, columns, mine, got, grad, grad_got):
    return tdot(mine[:, span], grad[:, columns]) + tdot(got[:, span], grad_got[:, columns])


def wide_pair(pair):
    return pl.ds(pl.multiple_of(pair * 2 * LANES, 2 * LANES), 2 * LANES)


def across_blocks(info, span, rows, mine, got, grad, grad_got, out):
    high, low = pair_of(info)
    for pair in range(2):
        value = gradient(span, wide_pair(jnp.bitwise_xor(pair, high)), mine, got, grad, grad_got)
        value = value.astype(out.dtype)
        out[2 * pair + low, rows] = value[:, :LANES]
        out[2 * pair + 1 - low, rows] = value[:, LANES:]


def along_blocks(info, first, span, mine, got, halves, out):
    high, low = pair_of(info)
    for bit, (grad, grad_got) in enumerate(halves):
        value = gradient(span, wide_pair(jnp.bitwise_xor(first, high)), mine, got, grad, grad_got)
        value = value.astype(out.dtype)
        out[2 * low + bit] = value[:, :LANES]
        out[2 * (1 - low) + bit] = value[:, LANES:]


def send_across_kernel(base, info, mine, got, grad, grad_got, after, out):
    rows = out.shape[1]
    across_blocks(info, slice(base, base + rows), slice(0, rows), mine, got, grad, grad_got, out)


def send_along_kernel(base, info, mine, got, grad, grad_got, far, far_got, after, out):
    span = slice(base, base + out.shape[1])
    along_blocks(info, 1, span, mine, got, ((grad, grad_got), (far, far_got)), out)


def keep_kernel(info, mine, got, grad, grad_got, far, far_got, after, out, out_along):
    rows = out.shape[1]
    across_blocks(info, slice(0, rows), slice(0, rows), mine, got, grad, grad_got, out)
    span = slice(rows, 2 * rows)
    along_blocks(info, 0, span, mine, got, ((grad, grad_got), (far, far_got)), out_along)


def last_kernel(base, info, mine, got, grad, grad_got, far, far_got, cot, cot_got, top, top_got,
                top_far, top_far_got, after, send, keep):
    rows, more = mine.shape[1] - base, cot.shape[1]
    for out, a, b, c, d in (
        (send, far, far_got, top_far, top_far_got), (keep, grad, grad_got, top, top_got)
    ):
        across_blocks(info, slice(base, base + rows), slice(0, rows), mine, got, a, b, out)
        across_blocks(info, slice(0, more), slice(rows, rows + more), cot, cot_got, c, d, out)


def pick_kernel(asked, table, out, done, onehot, held, sem):
    copy = pltpu.make_async_copy(table, held, sem)
    copy.start()
    peers, slots = asked.shape
    wide = lax.broadcasted_iota(jnp.int32, (16 * max(1, slots // 16), table.shape[0]), 1)
    columns = asked[...].T
    step = max(1, 16 // slots)
    for peer in range(0, peers, step):
        numbers = [columns[:, p : p + 1] for p in range(peer, peer + step)]
        numbers = numbers[0] if step == 1 else jnp.concatenate(numbers, 0)
        onehot[peer * slots : (peer + step) * slots] = jnp.where(numbers == wide, 1.0, 0.0).astype(BF16)
    done[...] = jnp.zeros_like(done)
    copy.wait()
    for start in range(0, out.shape[1], 256):
        span = slice(start, start + 256)
        out[:, span] = jnp.dot(onehot[...], held[:, span], preferred_element_type=F32).astype(BF16)


def pick_rows(asked, table):
    total = asked.shape[0] * asked.shape[1]
    return pl.pallas_call(
        pick_kernel,
        out_shape=[
            jax.ShapeDtypeStruct((total, table.shape[1]), BF16),
            jax.ShapeDtypeStruct((8, LANES), jnp.int32),
        ],
        in_specs=[VMEM, ANY],
        out_specs=[VMEM, VMEM],
        scratch_shapes=[
            pltpu.VMEM((total, table.shape[0]), BF16),
            pltpu.VMEM(table.shape, BF16),
            pltpu.SemaphoreType.DMA,
        ],
        compiler_params=params(56),
        name="pick_rows",
    )(asked, table)


def column_of(row):
    return jnp.broadcast_to(row, (8, row.shape[1])).T[:, :1]


def count_kernel(neighbours, used, held, adjacency, live, tile):
    slots, count = neighbours.shape
    held[...] = jnp.full(held.shape, -1, jnp.int32)
    slot = lax.broadcasted_iota(jnp.int32, (slots, count), 0)
    held[:slots] = jnp.where(slot < used[...], neighbours[...], -1)
    columns = held[...].T
    wide = lax.broadcasted_iota(jnp.int32, (tile, adjacency.shape[1]), 1)
    for start in range(0, count, tile):
        total = jnp.zeros(wide.shape, F32)
        for k in range(slots):
            total = total + jnp.where(columns[start : start + tile, k : k + 1] == wide, 1.0, 0.0)
        if live is not None:
            total = total * live
        adjacency[start : start + tile] = total.astype(BF16)


def beside_kernel(counts, nbr_low, fan_low, nbr_top, fan_top, grad, w2_self, w2_neigh, done,
                  adj_low, adj_top, sides, scale_top, grad_hidden, cotangent,
                  held_low, held_top, held_grad):
    peers = counts.shape[0]
    slots = adj_low.shape[1] // peers
    lane = lax.broadcasted_iota(jnp.int32, (1, adj_low.shape[1]), 1)
    live = jnp.zeros(lane.shape, F32)
    for peer in range(peers):
        here = (lane >= peer * slots) & (lane < peer * slots + counts[peer])
        live = jnp.where(here, 1.0, live)
    count_kernel(nbr_low, fan_low, held_low, adj_low, live, 32)
    count_kernel(nbr_top, fan_top, held_top, adj_top, None, 64)
    sides[:, :1] = column_of(1.0 / (fan_low[...].astype(F32) + 1.0))
    sides[:, 1:] = column_of(live[:, : sides.shape[0]])
    scale = column_of(1.0 / (fan_top[...].astype(F32) + 1.0))
    scale_top[...] = scale
    held_grad[...] = jnp.zeros_like(held_grad)
    held_grad[: grad.shape[0]] = grad[...].astype(F32)
    cotangent[...] = held_grad[...].T.astype(BF16)
    back = (tdot(grad[...], w2_neigh[...]) * scale).astype(BF16)
    direct = tdot(grad[...], w2_self[...]) + back.astype(F32)
    seeds = back.shape[0]
    for start in range(0, grad_hidden.shape[1], 256):
        span = slice(start, start + 256)
        spread = tdot(adj_top[...], back[:, span])
        grad_hidden[:seeds, span] = (spread[:seeds] + direct[:, span]).astype(grad_hidden.dtype)
        grad_hidden[seeds:, span] = spread[seeds:].astype(grad_hidden.dtype)


def beside(inputs, padded, counts, nbr_low, fan_low, nbr_top, fan_top, grad, w2_self, w2_neigh, done):
    middle, seeds, hidden = nbr_low.shape[1], nbr_top.shape[1], w2_self.shape[1]
    shape = jax.ShapeDtypeStruct
    return pl.pallas_call(
        beside_kernel,
        out_shape=[
            shape((middle, inputs), BF16), shape((seeds, middle), BF16), shape((middle, 2), F32),
            shape((seeds, 1), F32), shape((middle, hidden), BF16), shape((seeds, padded), BF16),
        ],
        in_specs=[SMEM] + [VMEM] * 7 + [ANY],
        out_specs=[VMEM] * 6,
        scratch_shapes=[
            pltpu.VMEM((-(-nbr_low.shape[0] // 8) * 8, middle), jnp.int32),
            pltpu.VMEM((-(-nbr_top.shape[0] // 8) * 8, seeds), jnp.int32),
            pltpu.VMEM((padded, seeds), F32),
        ],
        compiler_params=params(32),
        cost_estimate=pl.CostEstimate(flops=10**10, bytes_accessed=10**7, transcendentals=0),
        name="beside",
    )(counts, nbr_low, fan_low, nbr_top, fan_top, grad, w2_self, w2_neigh, done)


def mean_kernel(info, fetched, sides, adjacency, mine, other):
    first = info[0] == 0
    middle = mine.shape[0]
    for start in range(0, mine.shape[1], 256):
        span = slice(start, start + 256)
        own = jnp.where(sides[:, 1:] > 0.0, fetched[:middle, span].astype(F32), 0.0)
        total = jnp.dot(adjacency[...], fetched[:, span], preferred_element_type=F32)
        mean = (total + own) * sides[:, :1]
        mine[:, span] = jnp.where(first, own, mean).astype(BF16)
        other[:, span] = jnp.where(first, mean, own).astype(BF16)


def hidden_kernel(which, info, mine, other, w1_self, w1_neigh, grad_hidden, after, hidden, grad_pre):
    first = info[0] == 0
    width = hidden.shape[1]
    base = jnp.bitwise_xor(lax.div(info[1], 4), which) * width
    own = jnp.where(first, mine[...], other[...])
    mean = jnp.where(first, other[...], mine[...])
    for start in range(0, width, 256):
        at = pl.ds(pl.multiple_of(base + start, 256), 256)
        span = slice(start, start + 256)
        pre_act = jnp.dot(own, w1_self[:, at], preferred_element_type=F32)
        pre_act = pre_act + jnp.dot(mean, w1_neigh[:, at], preferred_element_type=F32)
        sigma = jax.nn.sigmoid(pre_act)
        hidden[:, span] = (pre_act * sigma).astype(BF16)
        grad = grad_hidden[:, at].astype(F32) * sigma * (1.0 + pre_act * (1.0 - sigma))
        grad_pre[:, span] = grad.astype(BF16)


def top_kernel(info, near, far, adjacency, scale, w2_self, w2_neigh, after,
               logits, mine_near, mine_far, other_near, other_far):
    first = info[0] == 0
    seeds, width = mine_near.shape
    dims = (((1,), (1,)), ((), ()))
    total = jnp.zeros(logits.shape, F32)
    for which, (hidden, mine, other) in enumerate(((near, mine_near, other_near), (far, mine_far, other_far))):
        at = pl.multiple_of(jnp.bitwise_xor(lax.div(info[1], 4), which) * width, width)
        own = hidden[:seeds]
        mean = jnp.dot(adjacency[...], hidden[...], preferred_element_type=F32)
        mean = ((mean + own.astype(F32)) * scale[...]).astype(BF16)
        mine[...] = jnp.where(first, own, mean)
        other[...] = jnp.where(first, mean, own)
        columns = pl.ds(at, width)
        total = total + lax.dot_general(w2_self[:, columns], own, dims, preferred_element_type=F32)
        total = total + lax.dot_general(w2_neigh[:, columns], mean, dims, preferred_element_type=F32)
    logits[...] = total


def column_at(info, along, position):
    bits = (position % 2) * 4 + position // 2 if along else position
    return pl.ds(pl.multiple_of(jnp.bitwise_xor(info[1], bits) * LANES, LANES), LANES)


def place_kernel(bases, info, *refs):
    pieces, outs, tops, held, sems = refs[:12], refs[12:14], refs[14:16], refs[16], refs[17]
    core, feat, more = info[0], held.shape[1], tops[0].shape[0]
    copies = []
    for which, base in enumerate(bases):
        near, far, near_other, far_other = pieces[4 * which : 4 * which + 4]
        last = which == len(bases) - 1
        rows = (feat if last else bases[which + 1]) - base
        span = slice(base, base + rows)
        for position in range(BLOCKS):
            where = column_at(info, which == 1, position)
            index = position % (BLOCKS // 2)
            own, other = (near, near_other) if position < BLOCKS // 2 else (far, far_other)
            a, b = own[index], other[index]
            for kind in range(2):
                value = jnp.where(core == kind, a, b)
                held[kind, span, where] = value[:rows]
                if last:
                    tops[kind][:, where] = value[rows : rows + more]
        for kind in range(2):
            copies.append(
                pltpu.make_async_copy(
                    held.at[kind, span], outs[kind].at[pl.ds(base, rows)], sems.at[which, kind]
                )
            )
            copies[-1].start()
    for copy in copies:
        copy.wait()


def place_blocks(info, bases, feat, more, width, pieces):
    shapes = [((feat, width), BF16)] * 2 + [((more, width), BF16)] * 2
    return kernel_call(
        functools.partial(place_kernel, bases), "place", shapes, [SMEM] + [VMEM] * 12, 24, info, *pieces,
        out_specs=[ANY, ANY, VMEM, VMEM],
        scratch_shapes=[pltpu.VMEM((2, feat, width), BF16), pltpu.SemaphoreType.DMA((len(bases), 2))],
    )


def on_device(sizes, table, requests, counts, nbr_low, fan_low, nbr_top, fan_top, grad_logits,
              w1_self, w1_neigh, w2_self, w2_neigh):
    peer_count, slot_count = requests.shape
    feat, width = w1_self.shape
    middle, seeds, classes = nbr_low.shape[0], nbr_top.shape[0], grad_logits.shape[1]
    across = axis_bits("cache", sizes["cache"]) + axis_bits("tr", sizes["tr"])
    along = across[1:3] + across[:1] + across[3:]
    place = 4 * bit_of(across[0]) + 2 * bit_of(across[1]) + bit_of(across[2])
    info = jnp.stack([lax.axis_index("sub"), place]).astype(jnp.int32)
    padded = -(-classes // 32) * 32
    part = (feat + padded) // 48 * 16
    last = feat - 2 * part

    asked = lax.all_to_all(requests, TRAINERS, split_axis=0, concat_axis=0, tiled=True)
    picked, done = pick_rows(asked, table)
    fetched = lax.all_to_all(
        picked.reshape(peer_count, slot_count, feat), TRAINERS, split_axis=0, concat_axis=0, tiled=True
    ).reshape(peer_count * slot_count, feat)

    adj_low, adj_top, sides, scale_top, grad_hidden, cotangent = beside(
        peer_count * slot_count, padded, counts, nbr_low.T, fan_low[None], nbr_top.T, fan_top[None],
        grad_logits.T, w2_self.T, w2_neigh.T, done,
    )
    cotangent_got = swap(cotangent, *CORE_STEP)

    low = ((middle, feat), BF16)
    mine, other = kernel_call(
        mean_kernel, "mean", [low, low], [SMEM] + [VMEM] * 3, 24, info, fetched, sides, adj_low,
    )
    got = swap(other, *CORE_STEP)
    half = ((middle, width // 2), BF16)
    hidden, grads, grads_got = [None] * 2, [None] * 2, [None] * 2
    after = mine
    for which in (1, 0):
        hidden[which], grads[which] = kernel_call(
            functools.partial(hidden_kernel, which), "hidden", [half, half], [SMEM] + [VMEM] * 5 + [ANY], 24,
            info, mine, other, w1_self, w1_neigh, grad_hidden, after,
        )
        grads_got[which] = swap(grads[which], *CORE_STEP)
        after = grads[which]
    send_half, keep_half = (grads[1], grads_got[1]), (grads[0], grads_got[0])

    blocks = (BLOCKS // 2, part, LANES)
    first_send, = kernel_call(
        functools.partial(send_across_kernel, 0), "send_across", [(blocks, BF16)],
        [SMEM] + [VMEM] * 4 + [ANY], 24, info, mine, got, *send_half, after,
    )
    first_got = swap(first_send, *across[0])
    second_send, = kernel_call(
        functools.partial(send_along_kernel, part), "send_along", [(blocks, BF16)],
        [SMEM] + [VMEM] * 6 + [ANY], 24, info, mine, got, *keep_half, *send_half, first_send,
    )
    second_got = swap(second_send, *along[0])
    top = ((seeds, width // 2), BF16)
    logits, *tops = kernel_call(
        top_kernel, "top", [((classes, seeds), F32), top, top, top, top], [SMEM] + [VMEM] * 6 + [ANY], 24,
        info, hidden[0], hidden[1], adj_top, scale_top, w2_self.T, w2_neigh.T, second_send,
    )
    tops_got = [swap(tops[2], *CORE_STEP), swap(tops[3], *CORE_STEP)]
    first_keep, second_keep = kernel_call(
        keep_kernel, "keep", [(blocks, F32), (blocks, F32)], [SMEM] + [VMEM] * 6 + [ANY], 24,
        info, mine, got, *keep_half, *send_half, logits,
    )
    blocks = (BLOCKS // 2, last + padded, LANES)
    third_send, third_keep = kernel_call(
        functools.partial(last_kernel, 2 * part), "last", [(blocks, BF16), (blocks, F32)],
        [SMEM] + [VMEM] * 12 + [ANY], 24, info, mine, got, *keep_half, *send_half, cotangent, cotangent_got,
        tops[0], tops_got[0], tops[1], tops_got[1], second_keep,
    )
    third_got = swap(third_send, *across[0])
    a = Piece(across, first_got, first_keep)
    b = Piece(along, second_got, second_keep)
    c = Piece(across, third_got, third_keep)
    after = third_keep
    for step in (a.first, b.first, a.second, c.first, b.second, c.second,
                 a.meet, b.meet, a.join, c.meet, b.join, c.join):
        after = step(after)

    def both_kinds(piece):
        near, far, near_other = piece.blocks
        return near, far, near_other, swap(far, *CORE_STEP)

    pieces = both_kinds(a) + both_kinds(b) + both_kinds(c)
    w1s, w1n, w2s, w2n = place_blocks(info, (0, part, 2 * part), feat, classes, width, pieces)
    return (logits.T, w1s, w1n, w2s.T, w2n.T)


def solution(mesh):
    split, whole = P(("grp", "tr", "cache", "sub"), None), P(("grp", "tr", "cache", "sub"))
    in_specs = (split, split, whole, split, whole, split, whole, split, P(), P(), P(), P())
    out_specs = (split, P("grp", None), P("grp", None), P("grp", None), P("grp", None))
    return jax.shard_map(
        functools.partial(on_device, dict(mesh.shape)),
        mesh=mesh,
        in_specs=in_specs,
        out_specs=out_specs,
        check_vma=False,
    )
```

time: 264 us -> 137 us (0.52)
  the two profiles are of different devices: /device:TPU:9 before, /device:TPU:0 now
where the time goes in v2:
time: 137 us
  waiting for transfers between devices  59.8 us (44%)
  Pallas kernels  31.2 us (23%)
  starting transfers between devices  26.5 us (19%)
  blocking collectives  13.7 us (10%)
  local copies, waits for them, and re-layouts  4.17 us (3%)
    ppermute x27, waiting for transfers between devices, swap(): return lax.ppermute(array, axis, [(i, i ^ distance) for i in range(size)])  37.3 us
    all_to_all x1, waiting for transfers between devices, on_device(): lax.all_to_all(picked.reshape(peer_count, slot_count, feat), TRAINERS, sp...  22.5 us
    ppermute x27, starting transfers between devices, swap(): return lax.ppermute(array, axis, [(i, i ^ distance) for i in range(size)])  22.5 us
    pallas_call x21, Pallas kernels, kernel_call(): pl.pallas_call(body, out_shape=[jax.ShapeDtypeStruct(*out) for out in out...  19.2 us
    all_to_all x1, blocking collectives, on_device(): lax.all_to_all(requests, TRAINERS, split_axis=0, concat_axis=0, tiled=True)  13.7 us
    pallas_call x1, Pallas kernels, beside(): pl.pallas_call(beside_kernel, out_shape=[shape((middle, inputs), BF16), s...  7.02 us
    pallas_call x1, Pallas kernels, pick_rows(): pl.pallas_call(pick_kernel, out_shape=[jax.ShapeDtypeStruct((total, table...  5.05 us
    unnamed x32, local copies, waits for them, and re-layouts  4.17 us
  transfers between devices with their start and end apart: 28, of which 14 were waited for; matrix products, arithmetic and copies ran while one was open for 0% of the time, Pallas kernels for 17%

profile of v2, /device:TPU:0, one launch (start us, length us, event | category | flops | bytes accessed | tf_op | source)
XLA Modules:
  0.0 136.6 jit_solution(6491913674864426805)
XLA Ops:
  0.6 13.7 %all_to_all.16 = s32[16,1,64]{2,1,0:T(1,128)} all-to-all(s32[16,1,64]{2,1,0:T(1,128)} %bitcast.29), channel_id=1, replica_groups=mesh['grp'=2,'tr'=4,'cache'=2,'sub'=2] {'tr','cache','sub'}, dimensions={0} | all-to-all | bytes 8192 | tf_op jit(solution)/shard_map/all_to_all | solution.py:409
  14.3 5.0 %pick_rows.1 = (bf16[1024,768]{1,0:T(8,128)(2,1)}, s32[8,128]{1,0:T(8,128)}) custom-call(s32[16,64]{1,0:T(8,128)} %bitcast.28, bf16[1024,768]{1,0:T(8,128)(2,1)} %table.1), custom_call_target="tpu_custom_call" | custom-call | tf_op jit(solution)/shard_map/pick_rows/pallas_call | solution.py:215
  19.4 4.0 %all-to-all-start.1 = ((bf16[16,64,768]{2,1,0:T(8,128)(2,1)}), bf16[16,64,768]{2,1,0:T(8,128)(2,1)S(1)}, u32[]{:S(2)}, u32[]{:S(2)}) async-start(bf16[16,64,768]{2,1,0:T(8,128)(2,1)} %bitcast.27), calls=%async_computation.1 | async-start | bytes 3145728 | tf_op jit(solution)/shard_map/all_to_all | solution.py:411
  23.6 7.0 %beside.1 = (bf16[512,1024]{1,0:T(8,128)(2,1)S(1)}, bf16[256,512]{1,0:T(8,128)(2,1)S(1)}, f32[512,2]{1,0:T(8,128)S(1)}, f32[256,1]{1,0:T(8,128)S(1)}, bf16[512,1...) custom-call(s32[16]{0:T(128)S(1)} %copy-done.10, s32[10,512]{1,0:T(8,128)S(1)} %bitcast.22, s32[1,512]{1,0:T(1,128)S(1)} %bitcast.24, ...), custom_call_target="tpu_custom_call" | custom-call | flops 10000000000 | bytes 10000000 | tf_op jit(solution)/shard_map/beside/pallas_call | solution.py:285
  30.7 1.0 copy-done.12
  31.7 1.0 copy-done.14
  32.7 22.5 %all-to-all-done.1 = bf16[16,64,768]{2,1,0:T(8,128)(2,1)S(1)} async-done(((bf16[16,64,768]{2,1,0:T(8,128)(2,1)}), bf16[16,64,768]{2,1,0:T(8,128)(2,1)S(1)}, u32[]{:S(2)}, u32[]{:S(2)}) %all-to-all-start.1) | async-done | bytes 1572896 | tf_op jit(solution)/shard_map/all_to_all | solution.py:411
  55.2 1.2 copy-done.15
  56.4 1.6 %mean.1 = (bf16[512,768]{1,0:T(8,128)(2,1)S(1)}, bf16[512,768]{1,0:T(8,128)(2,1)S(1)}) custom-call(s32[2]{0:T(128)S(1)} %pad_add_fusion.info, bf16[1024,768]{1,0:T(8,128)(2,1)S(1)} %bitcast.16, f32[512,2]{1,0:T(8,128)S(1)} %get-tuple-element.40.sides, bf16[512,1024]{1,0:T(8,128)(2,1)S(1)} %copy-done.15), custom_call_target="tpu_custom_call" | custom-call | flops 10000000000 | bytes 10000000 | tf_op jit(solution)/shard_map/mean/pallas_call | solution.py:42
  58.1 0.8 collective-permute-start
  58.9 1.8 %hidden.2 = (bf16[512,512]{1,0:T(8,128)(2,1)S(1)}, bf16[512,512]{1,0:T(8,128)(2,1)S(1)}) custom-call(s32[2]{0:T(128)S(1)} %pad_add_fusion.info, bf16[512,768]{1,0:T(8,128)(2,1)S(1)} %get-tuple-element.42.mine.after, bf16[512,768]{1,0:T(8,128)(2,1)S(1)} %get-tuple-element.43.other, bf16[768,1024]{1,0:T(8,128)(2,1)S(1)} %copy-done, ...), custom_call_target="tpu_custom_call" | custom-call | flops 10000000000 | bytes 10000000 | tf_op jit(solution)/shard_map/hidden/pallas_call | solution.py:42
  60.7 0.5 collective-permute-start.2
  61.2 1.8 %hidden.3 = (bf16[512,512]{1,0:T(8,128)(2,1)S(1)}, bf16[512,512]{1,0:T(8,128)(2,1)S(1)}) custom-call(s32[2]{0:T(128)S(1)} %pad_add_fusion.info, bf16[512,768]{1,0:T(8,128)(2,1)S(1)} %get-tuple-element.42.mine.after, bf16[512,768]{1,0:T(8,128)(2,1)S(1)} %get-tuple-element.43.other, bf16[768,1024]{1,0:T(8,128)(2,1)S(1)} %copy-done, ...), custom_call_target="tpu_custom_call" | custom-call | flops 10000000000 | bytes 10000000 | tf_op jit(solution)/shard_map/hidden/pallas_call | solution.py:42
  63.0 0.1 collective-permute-start.1
  63.1 1.2 send_across.1.after
  64.3 2.7 %collective-permute-start.3 = (bf16[4,304,128]{2,1,0:T(8,128)(2,1)S(1)}, bf16[4,304,128]{2,1,0:T(8,128)(2,1)S(1)}, u32[]{:S(2)}, u32[]{:S(2)}) collective-permute-start(bf16[4,304,128]{2,1,0:T(8,128)(2,1)S(1)} %send_across.1.after), channel_id=1, source_target_pairs={{0,2},{2,0},{1,3},{3,1},{4,6},{6,4},{5,7},{7,5},{8,10},{10,8},{9,1... | collective-permute-start | bytes 933896 | tf_op jit(solution)/shard_map/ppermute | solution.py:29
  67.0 1.8 %send_along.1.after = bf16[4,304,128]{2,1,0:T(8,128)(2,1)S(1)} custom-call(s32[2]{0:T(128)S(1)} %pad_add_fusion.info, bf16[512,768]{1,0:T(8,128)(2,1)S(1)} %get-tuple-element.42.mine.after, bf16[512,768]{1,0:T(8,128)(2,1)S(1)} %collective-permute-done.got, bf16[512,512]{1,0:T(8,128)(2,1)S(1)} %get-tuple-element.50.after.grad, ...), custom_call_target="tpu_custom_call" | custom-call | flops 10000000000 | bytes 10000000 | tf_op jit(solution)/shard_map/send_along/pallas_call | solution.py:42
  68.9 4.6 %collective-permute-start.8 = (bf16[4,304,128]{2,1,0:T(8,128)(2,1)S(1)}, bf16[4,304,128]{2,1,0:T(8,128)(2,1)S(1)}, u32[]{:S(2)}, u32[]{:S(2)}) collective-permute-start(bf16[4,304,128]{2,1,0:T(8,128)(2,1)S(1)} %send_along.1.after), channel_id=1, source_target_pairs={{0,4},{4,0},{8,12},{12,8},{1,5},{5,1},{9,13},{13,9},{2,6},{6,2},{1... | collective-permute-start | bytes 933896 | tf_op jit(solution)/shard_map/ppermute | solution.py:29
  73.4 2.4 %top.1 = (f32[153,256]{1,0:T(8,128)}, bf16[256,512]{1,0:T(8,128)(2,1)S(1)}, bf16[256,512]{1,0:T(8,128)(2,1)S(1)}, bf16[256,512]{1,0:T(8,128)(2,1)S(1)}, bf16[256,512]{1,0:T(8,128)(2,1)S(1)}) custom-call(s32[2]{0:T(128)S(1)} %pad_add_fusion.info, bf16[512,512]{1,0:T(8,128)(2,1)S(1)} %get-tuple-element.46.near, bf16[512,512]{1,0:T(8,128)(2,1)S(1)} %get-tuple-element.47.far, ...), custom_call_target="tpu_custom_call" | custom-call | flops 10000000000 | bytes 10000000 | tf_op jit(solution)/shard_map/top/pallas_call | solution.py:42
  75.8 0.5 collective-permute-start.6
  76.3 0.9 copy-done.11
  77.2 2.2 %keep.1 = (f32[4,304,128]{2,1,0:T(8,128)S(1)}, f32[4,304,128]{2,1,0:T(8,128)S(1)}) custom-call(s32[2]{0:T(128)S(1)} %pad_add_fusion.info, bf16[512,768]{1,0:T(8,128)(2,1)S(1)} %get-tuple-element.42.mine.after, bf16[512,768]{1,0:T(8,128)(2,1)S(1)} %collective-permute-done.got, bf16[512,512]{1,0:T(8,128)(2,1)S(1)} %get-tuple-element.50.after.grad, ...), custom_call_target="tpu_custom_call" | custom-call | flops 10000000000 | bytes 10000000 | tf_op jit(solution)/shard_map/keep/pallas_call | solution.py:42
  79.5 2.4 %last.1 = (bf16[4,320,128]{2,1,0:T(8,128)(2,1)S(1)}, f32[4,320,128]{2,1,0:T(8,128)S(1)}) custom-call(s32[2]{0:T(128)S(1)} %pad_add_fusion.info, bf16[512,768]{1,0:T(8,128)(2,1)S(1)} %get-tuple-element.42.mine.after, bf16[512,768]{1,0:T(8,128)(2,1)S(1)} %collective-permute-done.got, bf16[512,512]{1,0:T(8,128)(2,1)S(1)} %get-tuple-element.50.after.grad, ...), custom_call_target="tpu_custom_call" | custom-call | flops 10000000000 | bytes 10000000 | tf_op jit(solution)/shard_map/last/pallas_call | solution.py:42
  81.9 0.5 collective-permute-start.10
  82.6 3.4 %collective-permute-start.12 = (bf16[2,304,128]{2,1,0:T(8,128)(2,1)S(1)}, bf16[2,304,128]{2,1,0:T(8,128)(2,1)S(1)}, u32[]{:S(2)}, u32[]{:S(2)}) collective-permute-start(bf16[2,304,128]{2,1,0:T(8,128)(2,1)S(1)} %get-tuple-element.62.after), channel_id=1, source_target_pairs={{0,8},{4,12},{8,0},{12,4},{1,9},{5,13},{9,1},{13,5},{2,10},{6,14},... | collective-permute-start | bytes 466952 | tf_op jit(solution)/shard_map/ppermute | solution.py:29
  86.0 5.1 %collective-permute-done.7.got = bf16[2,304,128]{2,1,0:T(8,128)(2,1)S(1)} collective-permute-done((bf16[2,304,128]{2,1,0:T(8,128)(2,1)S(1)}, bf16[2,304,128]{2,1,0:T(8,128)(2,1)S(1)}, u32[]{:S(2)}, u32[]{:S(2)}) %collective-permute-start.7) | collective-permute-done | bytes 155680 | tf_op jit(solution)/shard_map/ppermute | solution.py:29
  91.3 0.3 collective-permute-done.10.got
  91.6 1.8 %collective-permute-start.11 = (bf16[2,320,128]{2,1,0:T(8,128)(2,1)S(1)}, bf16[2,320,128]{2,1,0:T(8,128)(2,1)S(1)}, u32[]{:S(2)}, u32[]{:S(2)}) collective-permute-start(bf16[2,320,128]{2,1,0:T(8,128)(2,1)S(1)} %get-tuple-element.64.after), channel_id=1, source_target_pairs={{0,4},{4,0},{8,12},{12,8},{1,5},{5,1},{9,13},{13,9},{2,6},{6,2},{1... | collective-permute-start | bytes 491528 | tf_op jit(solution)/shard_map/ppermute | solution.py:29
  93.4 2.0 %collective-permute-done.12.got = bf16[2,304,128]{2,1,0:T(8,128)(2,1)S(1)} collective-permute-done((bf16[2,304,128]{2,1,0:T(8,128)(2,1)S(1)}, bf16[2,304,128]{2,1,0:T(8,128)(2,1)S(1)}, u32[]{:S(2)}, u32[]{:S(2)}) %collective-permute-start.12) | collective-permute-done | bytes 155680 | tf_op jit(solution)/shard_map/ppermute | solution.py:29
  95.4 0.8 collective-permute-start.14
  96.2 4.5 %collective-permute-done.11.got = bf16[2,320,128]{2,1,0:T(8,128)(2,1)S(1)} collective-permute-done((bf16[2,320,128]{2,1,0:T(8,128)(2,1)S(1)}, bf16[2,320,128]{2,1,0:T(8,128)(2,1)S(1)}, u32[]{:S(2)}, u32[]{:S(2)}) %collective-permute-start.11) | collective-permute-done | bytes 163872 | tf_op jit(solution)/shard_map/ppermute | solution.py:29
  100.7 0.6 collective-permute-start.19
  101.4 2.5 %collective-permute-start.13 = (bf16[2,304,128]{2,1,0:T(8,128)(2,1)S(1)}, bf16[2,304,128]{2,1,0:T(8,128)(2,1)S(1)}, u32[]{:S(2)}, u32[]{:S(2)}) collective-permute-start(bf16[2,304,128]{2,1,0:T(8,128)(2,1)S(1)} %meet.3.after.near), channel_id=1, source_target_pairs={{0,4},{4,0},{8,12},{12,8},{1,5},{5,1},{9,13},{13,9},{2,6},{6,2},{1... | collective-permute-start | bytes 466952 | tf_op jit(solution)/shard_map/ppermute | solution.py:29
  103.9 0.1 collective-permute-start.18
  104.0 4.2 %collective-permute-done.13.far = bf16[2,304,128]{2,1,0:T(8,128)(2,1)S(1)} collective-permute-done((bf16[2,304,128]{2,1,0:T(8,128)(2,1)S(1)}, bf16[2,304,128]{2,1,0:T(8,128)(2,1)S(1)}, u32[]{:S(2)}, u32[]{:S(2)}) %collective-permute-start.13) | collective-permute-done | bytes 155680 | tf_op jit(solution)/shard_map/ppermute | solution.py:29
  108.3 4.7 %collective-permute-done.19.got = bf16[2,320,128]{2,1,0:T(8,128)(2,1)S(1)} collective-permute-done((bf16[2,320,128]{2,1,0:T(8,128)(2,1)S(1)}, bf16[2,320,128]{2,1,0:T(8,128)(2,1)S(1)}, u32[]{:S(2)}, u32[]{:S(2)}) %collective-permute-start.19) | collective-permute-done | bytes 163872 | tf_op jit(solution)/shard_map/ppermute | solution.py:29
  113.2 1.5 %collective-permute-done.18.far = bf16[2,304,128]{2,1,0:T(8,128)(2,1)S(1)} collective-permute-done((bf16[2,304,128]{2,1,0:T(8,128)(2,1)S(1)}, bf16[2,304,128]{2,1,0:T(8,128)(2,1)S(1)}, u32[]{:S(2)}, u32[]{:S(2)}) %collective-permute-start.18) | collective-permute-done | bytes 155680 | tf_op jit(solution)/shard_map/ppermute | solution.py:29
  114.7 3.7 %collective-permute-done.23.far = bf16[2,320,128]{2,1,0:T(8,128)(2,1)S(1)} collective-permute-done((bf16[2,320,128]{2,1,0:T(8,128)(2,1)S(1)}, bf16[2,320,128]{2,1,0:T(8,128)(2,1)S(1)}, u32[]{:S(2)}, u32[]{:S(2)}) %collective-permute-start.23) | collective-permute-done | bytes 163872 | tf_op jit(solution)/shard_map/ppermute | solution.py:29
  118.5 1.4 %collective-permute-start.24 = (bf16[4,320,128]{2,1,0:T(8,128)(2,1)S(1)}, bf16[4,320,128]{2,1,0:T(8,128)(2,1)S(1)}, u32[]{:S(2)}, u32[]{:S(2)}) collective-permute-start(bf16[4,320,128]{2,1,0:T(8,128)(2,1)S(1)} %join.5.refs_8_), channel_id=1, source_target_pairs={{0,2},{2,0},{1,3},{3,1},{4,6},{6,4},{5,7},{7,5},{8,10},{10,8},{9,1... | collective-permute-start | bytes 983048 | tf_op jit(solution)/shard_map/ppermute | solution.py:29
  119.9 0.6 collective-permute-start.15
  120.6 0.5 collective-permute-start.25
  121.1 6.0 %collective-permute-done.24.refs_9_ = bf16[4,320,128]{2,1,0:T(8,128)(2,1)S(1)} collective-permute-done((bf16[4,320,128]{2,1,0:T(8,128)(2,1)S(1)}, bf16[4,320,128]{2,1,0:T(8,128)(2,1)S(1)}, u32[]{:S(2)}, u32[]{:S(2)}) %collective-permute-start.24) | collective-permute-done | bytes 327712 | tf_op jit(solution)/shard_map/ppermute | solution.py:29
  127.1 3.3 %collective-permute-done.15.refs_1_ = bf16[4,304,128]{2,1,0:T(8,128)(2,1)S(1)} collective-permute-done((bf16[4,304,128]{2,1,0:T(8,128)(2,1)S(1)}, bf16[4,304,128]{2,1,0:T(8,128)(2,1)S(1)}, u32[]{:S(2)}, u32[]{:S(2)}) %collective-permute-start.15) | collective-permute-done | bytes 311328 | tf_op jit(solution)/shard_map/ppermute | solution.py:29
  130.4 0.5 collective-permute-start.17
  131.0 1.0 collective-permute-done.21.refs_6_
  132.0 0.4 collective-permute-done.17.refs_3_
  132.4 0.4 collective-permute-done.22.refs_7_
  132.9 3.6 %place.1 = (bf16[768,1024]{1,0:T(8,128)(2,1)}, bf16[768,1024]{1,0:T(8,128)(2,1)}, bf16[153,1024]{1,0:T(8,128)(2,1)}, bf16[153,1024]{1,0:T(8,128)(2,1)}) custom-call(s32[2]{0:T(128)S(1)} %pad_add_fusion.info, bf16[4,304,128]{2,1,0:T(8,128)(2,1)S(1)} %join.3.after.refs_0_, bf16[4,304,128]{2,1,0:T(8,128)(2,1)S(1)} %collective-permute-done.15.refs_1_, ...), custom_call_target="tpu_custom_call" | custom-call | flops 10000000000 | bytes 10000000 | tf_op jit(solution)/shard_map/place/pallas_call | solution.py:42
  (65 shorter events, 1.0 us)
Async XLA Ops:
  19.3 4.2 %copy-start.2 = (bf16[1024,153]{0,1:T(8,128)(2,1)S(1)}, bf16[1024,153]{0,1:T(8,128)(2,1)}, u32[]{:S(2)}) copy-start(bf16[1024,153]{0,1:T(8,128)(2,1)} %param.22) | copy-start | bytes 940036
  19.3 4.2 %copy-start.3 = (bf16[1024,153]{0,1:T(8,128)(2,1)S(1)}, bf16[1024,153]{0,1:T(8,128)(2,1)}, u32[]{:S(2)}) copy-start(bf16[1024,153]{0,1:T(8,128)(2,1)} %param.23) | copy-start | bytes 940036
  19.4 4.2 %copy-start.4 = (bf16[256,153]{0,1:T(8,128)(2,1)S(1)}, bf16[256,153]{0,1:T(8,128)(2,1)}, u32[]{:S(2)}) copy-start(bf16[256,153]{0,1:T(8,128)(2,1)} %param.19) | copy-start | bytes 235012
  19.4 4.2 %copy-start.5 = (s32[512,10]{0,1:T(8,128)S(1)}, s32[512,10]{0,1:T(8,128)}, u32[]{:S(2)}) copy-start(s32[512,10]{0,1:T(8,128)} %param.15) | copy-start | bytes 61444
  19.4 4.2 %copy-start.6 = (s32[256,25]{0,1:T(8,128)S(1)}, s32[256,25]{0,1:T(8,128)}, u32[]{:S(2)}) copy-start(s32[256,25]{0,1:T(8,128)} %param.17) | copy-start | bytes 76804
  19.4 4.2 %copy-start.7 = (s32[8,128]{1,0:T(8,128)S(1)}, s32[8,128]{1,0:T(8,128)}, u32[]{:S(2)}) copy-start(s32[8,128]{1,0:T(8,128)} %get-tuple-element.39.done) | copy-start | bytes 12292
  19.4 4.2 %copy-start.8 = (s32[512]{0:T(512)S(1)}, s32[512]{0:T(512)}, u32[]{:S(2)}) copy-start(s32[512]{0:T(512)} %param.16) | copy-start | bytes 6148
  19.4 4.2 %copy-start.9 = (s32[256]{0:T(256)S(1)}, s32[256]{0:T(256)}, u32[]{:S(2)}) copy-start(s32[256]{0:T(256)} %param.18) | copy-start | bytes 3076
  19.4 4.2 %copy-start.10 = (s32[16]{0:T(128)S(1)}, s32[16]{0:T(128)}, u32[]{:S(2)}) copy-start(s32[16]{0:T(128)} %counts.1) | copy-start | bytes 196
  19.4 35.8 %all-to-all-start.1 = ((bf16[16,64,768]{2,1,0:T(8,128)(2,1)}), bf16[16,64,768]{2,1,0:T(8,128)(2,1)S(1)}, u32[]{:S(2)}, u32[]{:S(2)}) async-start(bf16[16,64,768]{2,1,0:T(8,128)(2,1)} %bitcast.27), calls=%async_computation.1 | async-start | bytes 3145728 | tf_op jit(solution)/shard_map/all_to_all | solution.py:411
  30.7 1.0 copy-start.12
  31.7 1.0 copy-start.14
  32.6 46.8 %collective-permute-start.4 = (bf16[256,160]{1,0:T(8,128)(2,1)S(1)}, bf16[256,160]{1,0:T(8,128)(2,1)S(1)}, u32[]{:S(2)}, u32[]{:S(2)}) collective-permute-start(bf16[256,160]{1,0:T(8,128)(2,1)S(1)} %get-tuple-element.53.cot), channel_id=1, source_target_pairs={{0,1},{1,0},{2,3},{3,2},{4,5},{5,4},{6,7},{7,6},{8,9},{9,8},{10,11... | collective-permute-start | bytes 245768 | tf_op jit(solution)/shard_map/ppermute | solution.py:29
  55.2 1.2 copy-start.15
  56.4 2.5 %copy-start = (bf16[768,1024]{1,0:T(8,128)(2,1)S(1)}, bf16[768,1024]{1,0:T(8,128)(2,1)}, u32[]{:S(2)}) copy-start(bf16[768,1024]{1,0:T(8,128)(2,1)} %w1_self.3) | copy-start | bytes 4718596
  56.4 2.5 %copy-start.1 = (bf16[768,1024]{1,0:T(8,128)(2,1)S(1)}, bf16[768,1024]{1,0:T(8,128)(2,1)}, u32[]{:S(2)}) copy-start(bf16[768,1024]{1,0:T(8,128)(2,1)} %w1_neigh.3) | copy-start | bytes 4718596
  56.4 2.5 %copy-start.13 = (bf16[512,1024]{1,0:T(8,128)(2,1)S(1)}, bf16[512,1024]{1,0:T(8,128)(2,1)}, u32[]{:S(2)}) copy-start(bf16[512,1024]{1,0:T(8,128)(2,1)} %copy-done.12) | copy-start | bytes 3145732
  58.1 5.1 %collective-permute-start = (bf16[512,768]{1,0:T(8,128)(2,1)S(1)}, bf16[512,768]{1,0:T(8,128)(2,1)S(1)}, u32[]{:S(2)}, u32[]{:S(2)}) collective-permute-start(bf16[512,768]{1,0:T(8,128)(2,1)S(1)} %get-tuple-element.43.other), channel_id=1, source_target_pairs={{0,1},{1,0},{2,3},{3,2},{4,5},{5,4},{6,7},{7,6},{8,9},{9,8},{10,11... | collective-permute-start | bytes 2359304 | tf_op jit(solution)/shard_map/ppermute | solution.py:29
  60.7 2.4 %collective-permute-start.2 = (bf16[512,512]{1,0:T(8,128)(2,1)S(1)}, bf16[512,512]{1,0:T(8,128)(2,1)S(1)}, u32[]{:S(2)}, u32[]{:S(2)}) collective-permute-start(bf16[512,512]{1,0:T(8,128)(2,1)S(1)} %get-tuple-element.45.after.grad.far), channel_id=1, source_target_pairs={{0,1},{1,0},{2,3},{3,2},{4,5},{5,4},{6,7},{7,6},{8,9},{9,8},{10,11... | collective-permute-start | bytes 1572872 | tf_op jit(solution)/shard_map/ppermute | solution.py:29
  63.0 4.0 %collective-permute-start.1 = (bf16[512,512]{1,0:T(8,128)(2,1)S(1)}, bf16[512,512]{1,0:T(8,128)(2,1)S(1)}, u32[]{:S(2)}, u32[]{:S(2)}) collective-permute-start(bf16[512,512]{1,0:T(8,128)(2,1)S(1)} %get-tuple-element.50.after.grad), channel_id=1, source_target_pairs={{0,1},{1,0},{2,3},{3,2},{4,5},{5,4},{6,7},{7,6},{8,9},{9,8},{10,11... | collective-permute-start | bytes 1572872 | tf_op jit(solution)/shard_map/ppermute | solution.py:29
  64.3 18.1 %collective-permute-start.3 = (bf16[4,304,128]{2,1,0:T(8,128)(2,1)S(1)}, bf16[4,304,128]{2,1,0:T(8,128)(2,1)S(1)}, u32[]{:S(2)}, u32[]{:S(2)}) collective-permute-start(bf16[4,304,128]{2,1,0:T(8,128)(2,1)S(1)} %send_across.1.after), channel_id=1, source_target_pairs={{0,2},{2,0},{1,3},{3,1},{4,6},{6,4},{5,7},{7,5},{8,10},{10,8},{9,1... | collective-permute-start | bytes 933896 | tf_op jit(solution)/shard_map/ppermute | solution.py:29
  68.9 13.7 %collective-permute-start.8 = (bf16[4,304,128]{2,1,0:T(8,128)(2,1)S(1)}, bf16[4,304,128]{2,1,0:T(8,128)(2,1)S(1)}, u32[]{:S(2)}, u32[]{:S(2)}) collective-permute-start(bf16[4,304,128]{2,1,0:T(8,128)(2,1)S(1)} %send_along.1.after), channel_id=1, source_target_pairs={{0,4},{4,0},{8,12},{12,8},{1,5},{5,1},{9,13},{13,9},{2,6},{6,2},{1... | collective-permute-start | bytes 933896 | tf_op jit(solution)/shard_map/ppermute | solution.py:29
  75.8 3.7 %collective-permute-start.5 = (bf16[256,512]{1,0:T(8,128)(2,1)S(1)}, bf16[256,512]{1,0:T(8,128)(2,1)S(1)}, u32[]{:S(2)}, u32[]{:S(2)}) collective-permute-start(bf16[256,512]{1,0:T(8,128)(2,1)S(1)} %get-tuple-element.55), channel_id=1, source_target_pairs={{0,1},{1,0},{2,3},{3,2},{4,5},{5,4},{6,7},{7,6},{8,9},{9,8},{10,11... | collective-permute-start | bytes 786440 | tf_op jit(solution)/shard_map/ppermute | solution.py:29
  75.8 3.7 %collective-permute-start.6 = (bf16[256,512]{1,0:T(8,128)(2,1)S(1)}, bf16[256,512]{1,0:T(8,128)(2,1)S(1)}, u32[]{:S(2)}, u32[]{:S(2)}) collective-permute-start(bf16[256,512]{1,0:T(8,128)(2,1)S(1)} %get-tuple-element.57), channel_id=1, source_target_pairs={{0,1},{1,0},{2,3},{3,2},{4,5},{5,4},{6,7},{7,6},{8,9},{9,8},{10,11... | collective-permute-start | bytes 786440 | tf_op jit(solution)/shard_map/ppermute | solution.py:29
  76.3 0.9 copy-start.11
  81.9 9.7 %collective-permute-start.10 = (bf16[4,320,128]{2,1,0:T(8,128)(2,1)S(1)}, bf16[4,320,128]{2,1,0:T(8,128)(2,1)S(1)}, u32[]{:S(2)}, u32[]{:S(2)}) collective-permute-start(bf16[4,320,128]{2,1,0:T(8,128)(2,1)S(1)} %get-tuple-element.63), channel_id=1, source_target_pairs={{0,2},{2,0},{1,3},{3,1},{4,6},{6,4},{5,7},{7,5},{8,10},{10,8},{9,1... | collective-permute-start | bytes 983048 | tf_op jit(solution)/shard_map/ppermute | solution.py:29
  82.5 8.7 %collective-permute-start.7 = (bf16[2,304,128]{2,1,0:T(8,128)(2,1)S(1)}, bf16[2,304,128]{2,1,0:T(8,128)(2,1)S(1)}, u32[]{:S(2)}, u32[]{:S(2)}) collective-permute-start(bf16[2,304,128]{2,1,0:T(8,128)(2,1)S(1)} %get-tuple-element.60.after), channel_id=1, source_target_pairs={{0,4},{4,0},{8,12},{12,8},{1,5},{5,1},{9,13},{13,9},{2,6},{6,2},{1... | collective-permute-start | bytes 466952 | tf_op jit(solution)/shard_map/ppermute | solution.py:29
  82.6 12.8 %collective-permute-start.12 = (bf16[2,304,128]{2,1,0:T(8,128)(2,1)S(1)}, bf16[2,304,128]{2,1,0:T(8,128)(2,1)S(1)}, u32[]{:S(2)}, u32[]{:S(2)}) collective-permute-start(bf16[2,304,128]{2,1,0:T(8,128)(2,1)S(1)} %get-tuple-element.62.after), channel_id=1, source_target_pairs={{0,8},{4,12},{8,0},{12,4},{1,9},{5,13},{9,1},{13,5},{2,10},{6,14},... | collective-permute-start | bytes 466952 | tf_op jit(solution)/shard_map/ppermute | solution.py:29
  91.2 10.1 %collective-permute-start.9 = (bf16[2,304,128]{2,1,0:T(8,128)(2,1)S(1)}, bf16[2,304,128]{2,1,0:T(8,128)(2,1)S(1)}, u32[]{:S(2)}, u32[]{:S(2)}) collective-permute-start(bf16[2,304,128]{2,1,0:T(8,128)(2,1)S(1)} %add.13.after.mine), channel_id=1, source_target_pairs={{0,8},{4,12},{8,0},{12,4},{1,9},{5,13},{9,1},{13,5},{2,10},{6,14},... | collective-permute-start | bytes 466952 | tf_op jit(solution)/shard_map/ppermute | solution.py:29
  91.6 9.0 %collective-permute-start.11 = (bf16[2,320,128]{2,1,0:T(8,128)(2,1)S(1)}, bf16[2,320,128]{2,1,0:T(8,128)(2,1)S(1)}, u32[]{:S(2)}, u32[]{:S(2)}) collective-permute-start(bf16[2,320,128]{2,1,0:T(8,128)(2,1)S(1)} %get-tuple-element.64.after), channel_id=1, source_target_pairs={{0,4},{4,0},{8,12},{12,8},{1,5},{5,1},{9,13},{13,9},{2,6},{6,2},{1... | collective-permute-start | bytes 491528 | tf_op jit(solution)/shard_map/ppermute | solution.py:29
  95.4 8.5 %collective-permute-start.14 = (bf16[2,304,128]{2,1,0:T(8,128)(2,1)S(1)}, bf16[2,304,128]{2,1,0:T(8,128)(2,1)S(1)}, u32[]{:S(2)}, u32[]{:S(2)}) collective-permute-start(bf16[2,304,128]{2,1,0:T(8,128)(2,1)S(1)} %add.14.after.mine), channel_id=1, source_target_pairs={{0,2},{2,0},{1,3},{3,1},{4,6},{6,4},{5,7},{7,5},{8,10},{10,8},{9,1... | collective-permute-start | bytes 466952 | tf_op jit(solution)/shard_map/ppermute | solution.py:29
  100.7 12.3 %collective-permute-start.19 = (bf16[2,320,128]{2,1,0:T(8,128)(2,1)S(1)}, bf16[2,320,128]{2,1,0:T(8,128)(2,1)S(1)}, u32[]{:S(2)}, u32[]{:S(2)}) collective-permute-start(bf16[2,320,128]{2,1,0:T(8,128)(2,1)S(1)} %add.15.after.mine), channel_id=1, source_target_pairs={{0,8},{4,12},{8,0},{12,4},{1,9},{5,13},{9,1},{13,5},{2,10},{6,14},... | collective-permute-start | bytes 491528 | tf_op jit(solution)/shard_map/ppermute | solution.py:29
  101.4 6.9 %collective-permute-start.13 = (bf16[2,304,128]{2,1,0:T(8,128)(2,1)S(1)}, bf16[2,304,128]{2,1,0:T(8,128)(2,1)S(1)}, u32[]{:S(2)}, u32[]{:S(2)}) collective-permute-start(bf16[2,304,128]{2,1,0:T(8,128)(2,1)S(1)} %meet.3.after.near), channel_id=1, source_target_pairs={{0,4},{4,0},{8,12},{12,8},{1,5},{5,1},{9,13},{13,9},{2,6},{6,2},{1... | collective-permute-start | bytes 466952 | tf_op jit(solution)/shard_map/ppermute | solution.py:29
  103.9 10.7 %collective-permute-start.18 = (bf16[2,304,128]{2,1,0:T(8,128)(2,1)S(1)}, bf16[2,304,128]{2,1,0:T(8,128)(2,1)S(1)}, u32[]{:S(2)}, u32[]{:S(2)}) collective-permute-start(bf16[2,304,128]{2,1,0:T(8,128)(2,1)S(1)} %meet.4.after.near), channel_id=1, source_target_pairs={{0,8},{4,12},{8,0},{12,4},{1,9},{5,13},{9,1},{13,5},{2,10},{6,14},... | collective-permute-start | bytes 466952 | tf_op jit(solution)/shard_map/ppermute | solution.py:29
  113.1 5.4 %collective-permute-start.23 = (bf16[2,320,128]{2,1,0:T(8,128)(2,1)S(1)}, bf16[2,320,128]{2,1,0:T(8,128)(2,1)S(1)}, u32[]{:S(2)}, u32[]{:S(2)}) collective-permute-start(bf16[2,320,128]{2,1,0:T(8,128)(2,1)S(1)} %meet.5.after.near), channel_id=1, source_target_pairs={{0,4},{4,0},{8,12},{12,8},{1,5},{5,1},{9,13},{13,9},{2,6},{6,2},{1... | collective-permute-start | bytes 491528 | tf_op jit(solution)/shard_map/ppermute | solution.py:29
  118.5 8.6 %collective-permute-start.24 = (bf16[4,320,128]{2,1,0:T(8,128)(2,1)S(1)}, bf16[4,320,128]{2,1,0:T(8,128)(2,1)S(1)}, u32[]{:S(2)}, u32[]{:S(2)}) collective-permute-start(bf16[4,320,128]{2,1,0:T(8,128)(2,1)S(1)} %join.5.refs_8_), channel_id=1, source_target_pairs={{0,2},{2,0},{1,3},{3,1},{4,6},{6,4},{5,7},{7,5},{8,10},{10,8},{9,1... | collective-permute-start | bytes 983048 | tf_op jit(solution)/shard_map/ppermute | solution.py:29
  119.9 10.5 %collective-permute-start.15 = (bf16[4,304,128]{2,1,0:T(8,128)(2,1)S(1)}, bf16[4,304,128]{2,1,0:T(8,128)(2,1)S(1)}, u32[]{:S(2)}, u32[]{:S(2)}) collective-permute-start(bf16[4,304,128]{2,1,0:T(8,128)(2,1)S(1)} %join.3.after.refs_0_), channel_id=1, source_target_pairs={{0,2},{2,0},{1,3},{3,1},{4,6},{6,4},{5,7},{7,5},{8,10},{10,8},{9,1... | collective-permute-start | bytes 933896 | tf_op jit(solution)/shard_map/ppermute | solution.py:29
  120.6 9.8 %collective-permute-start.16 = (bf16[4,304,128]{2,1,0:T(8,128)(2,1)S(1)}, bf16[4,304,128]{2,1,0:T(8,128)(2,1)S(1)}, u32[]{:S(2)}, u32[]{:S(2)}) collective-permute-start(bf16[4,304,128]{2,1,0:T(8,128)(2,1)S(1)} %join.3.after.refs_0_), channel_id=1, source_target_pairs={{0,1},{1,0},{2,3},{3,2},{4,5},{5,4},{6,7},{7,6},{8,9},{9,8},{10,11... | collective-permute-start | bytes 933896 | tf_op jit(solution)/shard_map/ppermute | solution.py:29
  120.6 10.3 %collective-permute-start.20 = (bf16[4,304,128]{2,1,0:T(8,128)(2,1)S(1)}, bf16[4,304,128]{2,1,0:T(8,128)(2,1)S(1)}, u32[]{:S(2)}, u32[]{:S(2)}) collective-permute-start(bf16[4,304,128]{2,1,0:T(8,128)(2,1)S(1)} %join.4.after.refs_4_), channel_id=1, source_target_pairs={{0,4},{4,0},{8,12},{12,8},{1,5},{5,1},{9,13},{13,9},{2,6},{6,2},{1... | collective-permute-start | bytes 933896 | tf_op jit(solution)/shard_map/ppermute | solution.py:29
  120.6 11.4 %collective-permute-start.25 = (bf16[4,320,128]{2,1,0:T(8,128)(2,1)S(1)}, bf16[4,320,128]{2,1,0:T(8,128)(2,1)S(1)}, u32[]{:S(2)}, u32[]{:S(2)}) collective-permute-start(bf16[4,320,128]{2,1,0:T(8,128)(2,1)S(1)} %join.5.refs_8_), channel_id=1, source_target_pairs={{0,1},{1,0},{2,3},{3,2},{4,5},{5,4},{6,7},{7,6},{8,9},{9,8},{10,11... | collective-permute-start | bytes 983048 | tf_op jit(solution)/shard_map/ppermute | solution.py:29
  127.1 5.8 %collective-permute-start.26 = (bf16[4,320,128]{2,1,0:T(8,128)(2,1)S(1)}, bf16[4,320,128]{2,1,0:T(8,128)(2,1)S(1)}, u32[]{:S(2)}, u32[]{:S(2)}) collective-permute-start(bf16[4,320,128]{2,1,0:T(8,128)(2,1)S(1)} %collective-permute-done.24.refs_9_), channel_id=1, source_target_pairs={{0,1},{1,0},{2,3},{3,2},{4,5},{5,4},{6,7},{7,6},{8,9},{9,8},{10,11... | collective-permute-start | bytes 983048 | tf_op jit(solution)/shard_map/ppermute | solution.py:29
  130.4 1.6 %collective-permute-start.21 = (bf16[4,304,128]{2,1,0:T(8,128)(2,1)S(1)}, bf16[4,304,128]{2,1,0:T(8,128)(2,1)S(1)}, u32[]{:S(2)}, u32[]{:S(2)}) collective-permute-start(bf16[4,304,128]{2,1,0:T(8,128)(2,1)S(1)} %join.4.after.refs_4_), channel_id=1, source_target_pairs={{0,1},{1,0},{2,3},{3,2},{4,5},{5,4},{6,7},{7,6},{8,9},{9,8},{10,11... | collective-permute-start | bytes 933896 | tf_op jit(solution)/shard_map/ppermute | solution.py:29
  130.4 2.0 %collective-permute-start.17 = (bf16[4,304,128]{2,1,0:T(8,128)(2,1)S(1)}, bf16[4,304,128]{2,1,0:T(8,128)(2,1)S(1)}, u32[]{:S(2)}, u32[]{:S(2)}) collective-permute-start(bf16[4,304,128]{2,1,0:T(8,128)(2,1)S(1)} %collective-permute-done.15.refs_1_), channel_id=1, source_target_pairs={{0,1},{1,0},{2,3},{3,2},{4,5},{5,4},{6,7},{7,6},{8,9},{9,8},{10,11... | collective-permute-start | bytes 933896 | tf_op jit(solution)/shard_map/ppermute | solution.py:29
  130.9 2.0 %collective-permute-start.22 = (bf16[4,304,128]{2,1,0:T(8,128)(2,1)S(1)}, bf16[4,304,128]{2,1,0:T(8,128)(2,1)S(1)}, u32[]{:S(2)}, u32[]{:S(2)}) collective-permute-start(bf16[4,304,128]{2,1,0:T(8,128)(2,1)S(1)} %collective-permute-done.20.refs_5_), channel_id=1, source_target_pairs={{0,1},{1,0},{2,3},{3,2},{4,5},{5,4},{6,7},{7,6},{8,9},{9,8},{10,11... | collective-permute-start | bytes 933896 | tf_op jit(solution)/shard_map/ppermute | solution.py:29

commit v3 on v2

--- a/solution.py
+++ b/solution.py
@@ -66,7 +66,7 @@
     out[1] = (mine[1].astype(F32) + got[0].astype(F32)).astype(BF16)
 
 
-def join_kernel(near, far, after, out):
+def join_kernel(near, far, after, later, out):
     half = near.shape[0]
     out[:half] = near[...]
     out[half:] = far[...]
@@ -124,11 +124,11 @@
         self.got = swap(self.keep, *self.order[1])
         return self.keep
 
-    def join(self, after):
+    def join(self, after, later):
         count, rows, lanes = self.keep.shape
         near, = kernel_call(
             join_kernel, "join", [((2 * count, rows, lanes), BF16)],
-            [VMEM, VMEM, ANY], 16, self.keep, self.got, after,
+            [VMEM, VMEM, ANY, ANY], 16, self.keep, self.got, after, later,
         )
         far = swap(near, *self.order[0])
         self.blocks = (near, far, swap(near, *CORE_STEP))
@@ -403,7 +403,7 @@
     place = 4 * bit_of(across[0]) + 2 * bit_of(across[1]) + bit_of(across[2])
     info = jnp.stack([lax.axis_index("sub"), place]).astype(jnp.int32)
     padded = -(-classes // 32) * 32
-    part = (feat + padded) // 48 * 16
+    part = feat * 352 // 768 // 16 * 16
     last = feat - 2 * part
 
     asked = lax.all_to_all(requests, TRAINERS, split_axis=0, concat_axis=0, tiled=True)
@@ -446,30 +446,33 @@
         [SMEM] + [VMEM] * 6 + [ANY], 24, info, mine, got, *keep_half, *send_half, first_send,
     )
     second_got = swap(second_send, *along[0])
+    first_keep, second_keep = kernel_call(
+        keep_kernel, "keep", [(blocks, F32), (blocks, F32)], [SMEM] + [VMEM] * 6 + [ANY], 24,
+        info, mine, got, *keep_half, *send_half, second_send,
+    )
     top = ((seeds, width // 2), BF16)
     logits, *tops = kernel_call(
         top_kernel, "top", [((classes, seeds), F32), top, top, top, top], [SMEM] + [VMEM] * 6 + [ANY], 24,
-        info, hidden[0], hidden[1], adj_top, scale_top, w2_self.T, w2_neigh.T, second_send,
+        info, hidden[0], hidden[1], adj_top, scale_top, w2_self.T, w2_neigh.T, second_keep,
     )
     tops_got = [swap(tops[2], *CORE_STEP), swap(tops[3], *CORE_STEP)]
-    first_keep, second_keep = kernel_call(
-        keep_kernel, "keep", [(blocks, F32), (blocks, F32)], [SMEM] + [VMEM] * 6 + [ANY], 24,
-        info, mine, got, *keep_half, *send_half, logits,
-    )
+    a = Piece(across, first_got, first_keep)
+    b = Piece(along, second_got, second_keep)
+    after = b.first(a.first(logits))
     blocks = (BLOCKS // 2, last + padded, LANES)
     third_send, third_keep = kernel_call(
         functools.partial(last_kernel, 2 * part), "last", [(blocks, BF16), (blocks, F32)],
         [SMEM] + [VMEM] * 12 + [ANY], 24, info, mine, got, *keep_half, *send_half, cotangent, cotangent_got,
-        tops[0], tops_got[0], tops[1], tops_got[1], second_keep,
+        tops[0], tops_got[0], tops[1], tops_got[1], after,
     )
     third_got = swap(third_send, *across[0])
-    a = Piece(across, first_got, first_keep)
-    b = Piece(along, second_got, second_keep)
     c = Piece(across, third_got, third_keep)
     after = third_keep
-    for step in (a.first, b.first, a.second, c.first, b.second, c.second,
-                 a.meet, b.meet, a.join, c.meet, b.join, c.join):
+    for step in (a.second, b.second, c.first, a.meet, b.meet, c.second):
         after = step(after)
+    after = a.join(after, after)
+    after = c.meet(b.join(after, after))
+    c.join(after, a.blocks[1])
 
     def both_kinds(piece):
         near, far, near_other = piece.blocks

time: 137 us -> 135 us (0.985)
  waiting for transfers between devices: 59.8 us -> 57.6 us
    ppermute x27, waiting for transfers between devices: 37.3 us -> 35.1 us  [swap(): return lax.ppermute(array, axis, [(i, i ^ distance) for i in range(size)])]
  transfers between devices with their start and end apart: 28 -> 28, of which waited for: 14 -> 15; matrix products, arithmetic and copies ran while one was open for 0% -> 0% of each run, Pallas kernels for 17% -> 17%
where the time goes in v3:
time: 135 us; the launch traced here: 134 us
  waiting for transfers between devices  57.6 us (43%)
  Pallas kernels  31.1 us (23%)
  starting transfers between devices  26.8 us (20%)
  blocking collectives  13.7 us (10%)
  local copies, waits for them, and re-layouts  4.17 us (3%)
    ppermute x27, waiting for transfers between devices, swap(): return lax.ppermute(array, axis, [(i, i ^ distance) for i in range(size)])  35.1 us
    ppermute x27, starting transfers between devices, swap(): return lax.ppermute(array, axis, [(i, i ^ distance) for i in range(size)])  22.8 us
    all_to_all x1, waiting for transfers between devices, on_device(): lax.all_to_all(picked.reshape(peer_count, slot_count, feat), TRAINERS, sp...  22.5 us
    pallas_call x21, Pallas kernels, kernel_call(): pl.pallas_call(body, out_shape=[jax.ShapeDtypeStruct(*out) for out in out...  19 us
    all_to_all x1, blocking collectives, on_device(): lax.all_to_all(requests, TRAINERS, split_axis=0, concat_axis=0, tiled=True)  13.7 us
    pallas_call x1, Pallas kernels, beside(): pl.pallas_call(beside_kernel, out_shape=[shape((middle, inputs), BF16), s...  7.02 us
    pallas_call x1, Pallas kernels, pick_rows(): pl.pallas_call(pick_kernel, out_shape=[jax.ShapeDtypeStruct((total, table...  5.05 us
    unnamed x32, local copies, waits for them, and re-layouts  4.17 us
  transfers between devices with their start and end apart: 28, of which 15 were waited for; matrix products, arithmetic and copies ran while one was open for 0% of the time, Pallas kernels for 17%

profile of v3, /device:TPU:0, one launch (start us, length us, event | category | flops | bytes accessed | tf_op | source)
XLA Modules:
  0.0 134.4 jit_solution(9598697500993510905)
XLA Ops:
  0.6 13.7 %all_to_all.16 = s32[16,1,64]{2,1,0:T(1,128)} all-to-all(s32[16,1,64]{2,1,0:T(1,128)} %bitcast.29), channel_id=1, replica_groups=mesh['grp'=2,'tr'=4,'cache'=2,'sub'=2] {'tr','cache','sub'}, dimensions={0} | all-to-all | bytes 8192 | tf_op jit(solution)/shard_map/all_to_all | solution.py:409
  14.3 5.0 %pick_rows.1 = (bf16[1024,768]{1,0:T(8,128)(2,1)}, s32[8,128]{1,0:T(8,128)}) custom-call(s32[16,64]{1,0:T(8,128)} %bitcast.28, bf16[1024,768]{1,0:T(8,128)(2,1)} %table.1), custom_call_target="tpu_custom_call" | custom-call | tf_op jit(solution)/shard_map/pick_rows/pallas_call | solution.py:215
  19.4 4.0 %all-to-all-start.1 = ((bf16[16,64,768]{2,1,0:T(8,128)(2,1)}), bf16[16,64,768]{2,1,0:T(8,128)(2,1)S(1)}, u32[]{:S(2)}, u32[]{:S(2)}) async-start(bf16[16,64,768]{2,1,0:T(8,128)(2,1)} %bitcast.27), calls=%async_computation.1 | async-start | bytes 3145728 | tf_op jit(solution)/shard_map/all_to_all | solution.py:411
  23.6 7.0 %beside.1 = (bf16[512,1024]{1,0:T(8,128)(2,1)S(1)}, bf16[256,512]{1,0:T(8,128)(2,1)S(1)}, f32[512,2]{1,0:T(8,128)S(1)}, f32[256,1]{1,0:T(8,128)S(1)}, bf16[512,1...) custom-call(s32[16]{0:T(128)S(1)} %copy-done.10, s32[10,512]{1,0:T(8,128)S(1)} %bitcast.22, s32[1,512]{1,0:T(1,128)S(1)} %bitcast.24, ...), custom_call_target="tpu_custom_call" | custom-call | flops 10000000000 | bytes 10000000 | tf_op jit(solution)/shard_map/beside/pallas_call | solution.py:285
  30.7 1.0 copy-done.12
  31.7 1.0 copy-done.14
  32.7 22.5 %all-to-all-done.1 = bf16[16,64,768]{2,1,0:T(8,128)(2,1)S(1)} async-done(((bf16[16,64,768]{2,1,0:T(8,128)(2,1)}), bf16[16,64,768]{2,1,0:T(8,128)(2,1)S(1)}, u32[]{:S(2)}, u32[]{:S(2)}) %all-to-all-start.1) | async-done | bytes 1572896 | tf_op jit(solution)/shard_map/all_to_all | solution.py:411
  55.2 1.2 copy-done.15
  56.4 1.6 %mean.1 = (bf16[512,768]{1,0:T(8,128)(2,1)S(1)}, bf16[512,768]{1,0:T(8,128)(2,1)S(1)}) custom-call(s32[2]{0:T(128)S(1)} %pad_add_fusion.info, bf16[1024,768]{1,0:T(8,128)(2,1)S(1)} %bitcast.16, f32[512,2]{1,0:T(8,128)S(1)} %get-tuple-element.40.sides, bf16[512,1024]{1,0:T(8,128)(2,1)S(1)} %copy-done.15), custom_call_target="tpu_custom_call" | custom-call | flops 10000000000 | bytes 10000000 | tf_op jit(solution)/shard_map/mean/pallas_call | solution.py:42
  58.1 0.8 collective-permute-start
  58.9 1.8 %hidden.2 = (bf16[512,512]{1,0:T(8,128)(2,1)S(1)}, bf16[512,512]{1,0:T(8,128)(2,1)S(1)}) custom-call(s32[2]{0:T(128)S(1)} %pad_add_fusion.info, bf16[512,768]{1,0:T(8,128)(2,1)S(1)} %get-tuple-element.42.mine.after, bf16[512,768]{1,0:T(8,128)(2,1)S(1)} %get-tuple-element.43.other, bf16[768,1024]{1,0:T(8,128)(2,1)S(1)} %copy-done, ...), custom_call_target="tpu_custom_call" | custom-call | flops 10000000000 | bytes 10000000 | tf_op jit(solution)/shard_map/hidden/pallas_call | solution.py:42
  60.7 0.5 collective-permute-start.2
  61.2 1.8 %hidden.3 = (bf16[512,512]{1,0:T(8,128)(2,1)S(1)}, bf16[512,512]{1,0:T(8,128)(2,1)S(1)}) custom-call(s32[2]{0:T(128)S(1)} %pad_add_fusion.info, bf16[512,768]{1,0:T(8,128)(2,1)S(1)} %get-tuple-element.42.mine.after, bf16[512,768]{1,0:T(8,128)(2,1)S(1)} %get-tuple-element.43.other, bf16[768,1024]{1,0:T(8,128)(2,1)S(1)} %copy-done, ...), custom_call_target="tpu_custom_call" | custom-call | flops 10000000000 | bytes 10000000 | tf_op jit(solution)/shard_map/hidden/pallas_call | solution.py:42
  63.1 1.1 send_across.1.after
  64.3 2.7 %collective-permute-start.3 = (bf16[4,352,128]{2,1,0:T(8,128)(2,1)S(1)}, bf16[4,352,128]{2,1,0:T(8,128)(2,1)S(1)}, u32[]{:S(2)}, u32[]{:S(2)}) collective-permute-start(bf16[4,352,128]{2,1,0:T(8,128)(2,1)S(1)} %send_across.1.after), channel_id=1, source_target_pairs={{0,2},{2,0},{1,3},{3,1},{4,6},{6,4},{5,7},{7,5},{8,10},{10,8},{9,1... | collective-permute-start | bytes 1081352 | tf_op jit(solution)/shard_map/ppermute | solution.py:29
  67.0 2.0 %send_along.1.after = bf16[4,352,128]{2,1,0:T(8,128)(2,1)S(1)} custom-call(s32[2]{0:T(128)S(1)} %pad_add_fusion.info, bf16[512,768]{1,0:T(8,128)(2,1)S(1)} %get-tuple-element.42.mine.after, bf16[512,768]{1,0:T(8,128)(2,1)S(1)} %collective-permute-done.got, bf16[512,512]{1,0:T(8,128)(2,1)S(1)} %get-tuple-element.50.after.grad, ...), custom_call_target="tpu_custom_call" | custom-call | flops 10000000000 | bytes 10000000 | tf_op jit(solution)/shard_map/send_along/pallas_call | solution.py:42
  69.0 4.6 %collective-permute-start.8 = (bf16[4,352,128]{2,1,0:T(8,128)(2,1)S(1)}, bf16[4,352,128]{2,1,0:T(8,128)(2,1)S(1)}, u32[]{:S(2)}, u32[]{:S(2)}) collective-permute-start(bf16[4,352,128]{2,1,0:T(8,128)(2,1)S(1)} %send_along.1.after), channel_id=1, source_target_pairs={{0,4},{4,0},{8,12},{12,8},{1,5},{5,1},{9,13},{13,9},{2,6},{6,2},{1... | collective-permute-start | bytes 1081352 | tf_op jit(solution)/shard_map/ppermute | solution.py:29
  73.6 2.6 %keep.1 = (f32[4,352,128]{2,1,0:T(8,128)S(1)}, f32[4,352,128]{2,1,0:T(8,128)S(1)}) custom-call(s32[2]{0:T(128)S(1)} %pad_add_fusion.info, bf16[512,768]{1,0:T(8,128)(2,1)S(1)} %get-tuple-element.42.mine.after, bf16[512,768]{1,0:T(8,128)(2,1)S(1)} %collective-permute-done.got, bf16[512,512]{1,0:T(8,128)(2,1)S(1)} %get-tuple-element.50.after.grad, ...), custom_call_target="tpu_custom_call" | custom-call | flops 10000000000 | bytes 10000000 | tf_op jit(solution)/shard_map/keep/pallas_call | solution.py:42
  76.2 2.2 %top.1 = (f32[153,256]{1,0:T(8,128)}, bf16[256,512]{1,0:T(8,128)(2,1)S(1)}, bf16[256,512]{1,0:T(8,128)(2,1)S(1)}, bf16[256,512]{1,0:T(8,128)(2,1)S(1)}, bf16[256,512]{1,0:T(8,128)(2,1)S(1)}) custom-call(s32[2]{0:T(128)S(1)} %pad_add_fusion.info, bf16[512,512]{1,0:T(8,128)(2,1)S(1)} %get-tuple-element.46.near, bf16[512,512]{1,0:T(8,128)(2,1)S(1)} %get-tuple-element.47.far, ...), custom_call_target="tpu_custom_call" | custom-call | flops 10000000000 | bytes 10000000 | tf_op jit(solution)/shard_map/top/pallas_call | solution.py:42
  78.4 0.5 collective-permute-start.7
  78.9 0.9 copy-done.11
  79.9 1.5 %collective-permute-start.4 = (bf16[2,352,128]{2,1,0:T(8,128)(2,1)S(1)}, bf16[2,352,128]{2,1,0:T(8,128)(2,1)S(1)}, u32[]{:S(2)}, u32[]{:S(2)}) collective-permute-start(bf16[2,352,128]{2,1,0:T(8,128)(2,1)S(1)} %get-tuple-element.54.after), channel_id=1, source_target_pairs={{0,4},{4,0},{8,12},{12,8},{1,5},{5,1},{9,13},{13,9},{2,6},{6,2},{1... | collective-permute-start | bytes 540680 | tf_op jit(solution)/shard_map/ppermute | solution.py:29
  81.4 0.7 collective-permute-done.8.got
  82.2 2.3 %collective-permute-start.11 = (bf16[2,352,128]{2,1,0:T(8,128)(2,1)S(1)}, bf16[2,352,128]{2,1,0:T(8,128)(2,1)S(1)}, u32[]{:S(2)}, u32[]{:S(2)}) collective-permute-start(bf16[2,352,128]{2,1,0:T(8,128)(2,1)S(1)} %get-tuple-element.61.after), channel_id=1, source_target_pairs={{0,8},{4,12},{8,0},{12,4},{1,9},{5,13},{9,1},{13,5},{2,10},{6,14},... | collective-permute-start | bytes 540680 | tf_op jit(solution)/shard_map/ppermute | solution.py:29
  84.5 1.9 %last.1 = (bf16[4,224,128]{2,1,0:T(8,128)(2,1)S(1)}, f32[4,224,128]{2,1,0:T(8,128)S(1)}) custom-call(s32[2]{0:T(128)S(1)} %pad_add_fusion.info, bf16[512,768]{1,0:T(8,128)(2,1)S(1)} %get-tuple-element.42.mine.after, bf16[512,768]{1,0:T(8,128)(2,1)S(1)} %collective-permute-done.got, bf16[512,512]{1,0:T(8,128)(2,1)S(1)} %get-tuple-element.50.after.grad, ...), custom_call_target="tpu_custom_call" | custom-call | flops 10000000000 | bytes 10000000 | tf_op jit(solution)/shard_map/last/pallas_call | solution.py:42
  86.4 1.5 %collective-permute-start.10 = (bf16[4,224,128]{2,1,0:T(8,128)(2,1)S(1)}, bf16[4,224,128]{2,1,0:T(8,128)(2,1)S(1)}, u32[]{:S(2)}, u32[]{:S(2)}) collective-permute-start(bf16[4,224,128]{2,1,0:T(8,128)(2,1)S(1)} %get-tuple-element.63), channel_id=1, source_target_pairs={{0,2},{2,0},{1,3},{3,1},{4,6},{6,4},{5,7},{7,5},{8,10},{10,8},{9,1... | collective-permute-start | bytes 688136 | tf_op jit(solution)/shard_map/ppermute | solution.py:29
  87.8 0.5 collective-permute-done.4.got
  88.4 1.7 %collective-permute-start.9 = (bf16[2,352,128]{2,1,0:T(8,128)(2,1)S(1)}, bf16[2,352,128]{2,1,0:T(8,128)(2,1)S(1)}, u32[]{:S(2)}, u32[]{:S(2)}) collective-permute-start(bf16[2,352,128]{2,1,0:T(8,128)(2,1)S(1)} %add.13.after.mine), channel_id=1, source_target_pairs={{0,8},{4,12},{8,0},{12,4},{1,9},{5,13},{9,1},{13,5},{2,10},{6,14},... | collective-permute-start | bytes 540680 | tf_op jit(solution)/shard_map/ppermute | solution.py:29
  90.1 8.0 %collective-permute-done.11.got = bf16[2,352,128]{2,1,0:T(8,128)(2,1)S(1)} collective-permute-done((bf16[2,352,128]{2,1,0:T(8,128)(2,1)S(1)}, bf16[2,352,128]{2,1,0:T(8,128)(2,1)S(1)}, u32[]{:S(2)}, u32[]{:S(2)}) %collective-permute-start.11) | collective-permute-done | bytes 180256 | tf_op jit(solution)/shard_map/ppermute | solution.py:29
  98.1 0.9 collective-permute-start.14
  99.2 1.7 %collective-permute-done.9.got = bf16[2,352,128]{2,1,0:T(8,128)(2,1)S(1)} collective-permute-done((bf16[2,352,128]{2,1,0:T(8,128)(2,1)S(1)}, bf16[2,352,128]{2,1,0:T(8,128)(2,1)S(1)}, u32[]{:S(2)}, u32[]{:S(2)}) %collective-permute-start.9) | collective-permute-done | bytes 180256 | tf_op jit(solution)/shard_map/ppermute | solution.py:29
  100.9 0.4 collective-permute-start.12
  101.3 2.4 %collective-permute-done.14.got = bf16[2,352,128]{2,1,0:T(8,128)(2,1)S(1)} collective-permute-done((bf16[2,352,128]{2,1,0:T(8,128)(2,1)S(1)}, bf16[2,352,128]{2,1,0:T(8,128)(2,1)S(1)}, u32[]{:S(2)}, u32[]{:S(2)}) %collective-permute-start.14) | collective-permute-done | bytes 180256 | tf_op jit(solution)/shard_map/ppermute | solution.py:29
  103.9 4.1 %collective-permute-done.13.got = bf16[2,224,128]{2,1,0:T(8,128)(2,1)S(1)} collective-permute-done((bf16[2,224,128]{2,1,0:T(8,128)(2,1)S(1)}, bf16[2,224,128]{2,1,0:T(8,128)(2,1)S(1)}, u32[]{:S(2)}, u32[]{:S(2)}) %collective-permute-start.13) | collective-permute-done | bytes 114720 | tf_op jit(solution)/shard_map/ppermute | solution.py:29
  108.0 0.4 collective-permute-start.22
  108.5 2.6 %collective-permute-done.12.far = bf16[2,352,128]{2,1,0:T(8,128)(2,1)S(1)} collective-permute-done((bf16[2,352,128]{2,1,0:T(8,128)(2,1)S(1)}, bf16[2,352,128]{2,1,0:T(8,128)(2,1)S(1)}, u32[]{:S(2)}, u32[]{:S(2)}) %collective-permute-start.12) | collective-permute-done | bytes 180256 | tf_op jit(solution)/shard_map/ppermute | solution.py:29
  111.1 1.4 %collective-permute-start.15 = (bf16[4,352,128]{2,1,0:T(8,128)(2,1)S(1)}, bf16[4,352,128]{2,1,0:T(8,128)(2,1)S(1)}, u32[]{:S(2)}, u32[]{:S(2)}) collective-permute-start(bf16[4,352,128]{2,1,0:T(8,128)(2,1)S(1)} %join.3.after.later.refs_0_), channel_id=1, source_target_pairs={{0,2},{2,0},{1,3},{3,1},{4,6},{6,4},{5,7},{7,5},{8,10},{10,8},{9,1... | collective-permute-start | bytes 1081352 | tf_op jit(solution)/shard_map/ppermute | solution.py:29
  112.5 3.1 %collective-permute-done.18.far = bf16[2,352,128]{2,1,0:T(8,128)(2,1)S(1)} collective-permute-done((bf16[2,352,128]{2,1,0:T(8,128)(2,1)S(1)}, bf16[2,352,128]{2,1,0:T(8,128)(2,1)S(1)}, u32[]{:S(2)}, u32[]{:S(2)}) %collective-permute-start.18) | collective-permute-done | bytes 180256 | tf_op jit(solution)/shard_map/ppermute | solution.py:29
  115.7 1.2 collective-permute-done.22.got
  117.0 2.0 %collective-permute-start.19 = (bf16[4,352,128]{2,1,0:T(8,128)(2,1)S(1)}, bf16[4,352,128]{2,1,0:T(8,128)(2,1)S(1)}, u32[]{:S(2)}, u32[]{:S(2)}) collective-permute-start(bf16[4,352,128]{2,1,0:T(8,128)(2,1)S(1)} %join.4.after.refs_4_), channel_id=1, source_target_pairs={{0,4},{4,0},{8,12},{12,8},{1,5},{5,1},{9,13},{13,9},{2,6},{6,2},{1... | collective-permute-start | bytes 1081352 | tf_op jit(solution)/shard_map/ppermute | solution.py:29
  119.0 4.1 %collective-permute-done.23.far = bf16[2,224,128]{2,1,0:T(8,128)(2,1)S(1)} collective-permute-done((bf16[2,224,128]{2,1,0:T(8,128)(2,1)S(1)}, bf16[2,224,128]{2,1,0:T(8,128)(2,1)S(1)}, u32[]{:S(2)}, u32[]{:S(2)}) %collective-permute-start.23) | collective-permute-done | bytes 114720 | tf_op jit(solution)/shard_map/ppermute | solution.py:29
  123.1 0.5 collective-permute-start.24
  123.6 3.4 %collective-permute-done.19.refs_5_ = bf16[4,352,128]{2,1,0:T(8,128)(2,1)S(1)} collective-permute-done((bf16[4,352,128]{2,1,0:T(8,128)(2,1)S(1)}, bf16[4,352,128]{2,1,0:T(8,128)(2,1)S(1)}, u32[]{:S(2)}, u32[]{:S(2)}) %collective-permute-start.19) | collective-permute-done | bytes 360480 | tf_op jit(solution)/shard_map/ppermute | solution.py:29
  126.9 0.5 collective-permute-start.17
  127.4 1.7 %collective-permute-done.24.refs_9_ = bf16[4,224,128]{2,1,0:T(8,128)(2,1)S(1)} collective-permute-done((bf16[4,224,128]{2,1,0:T(8,128)(2,1)S(1)}, bf16[4,224,128]{2,1,0:T(8,128)(2,1)S(1)}, u32[]{:S(2)}, u32[]{:S(2)}) %collective-permute-start.24) | collective-permute-done | bytes 229408 | tf_op jit(solution)/shard_map/ppermute | solution.py:29
  129.2 0.3 collective-permute-done.25.refs_10_
  129.4 1.2 collective-permute-done.26.refs_11_
  130.7 3.6 %place.1 = (bf16[768,1024]{1,0:T(8,128)(2,1)}, bf16[768,1024]{1,0:T(8,128)(2,1)}, bf16[153,1024]{1,0:T(8,128)(2,1)}, bf16[153,1024]{1,0:T(8,128)(2,1)}) custom-call(s32[2]{0:T(128)S(1)} %pad_add_fusion.info, bf16[4,352,128]{2,1,0:T(8,128)(2,1)S(1)} %join.3.after.later.refs_0_, bf16[4,352,128]{2,1,0:T(8,128)(2,1)S(1)} %collective-permute-done.15.later.refs_1_, ...), custom_call_target="tpu_custom_call" | custom-call | flops 10000000000 | bytes 10000000 | tf_op jit(solution)/shard_map/place/pallas_call | solution.py:42
  (65 shorter events, 1.1 us)
Async XLA Ops:
  19.3 4.2 %copy-start.2 = (bf16[1024,153]{0,1:T(8,128)(2,1)S(1)}, bf16[1024,153]{0,1:T(8,128)(2,1)}, u32[]{:S(2)}) copy-start(bf16[1024,153]{0,1:T(8,128)(2,1)} %param.22) | copy-start | bytes 940036
  19.3 4.2 %copy-start.3 = (bf16[1024,153]{0,1:T(8,128)(2,1)S(1)}, bf16[1024,153]{0,1:T(8,128)(2,1)}, u32[]{:S(2)}) copy-start(bf16[1024,153]{0,1:T(8,128)(2,1)} %param.23) | copy-start | bytes 940036
  19.4 4.2 %copy-start.4 = (bf16[256,153]{0,1:T(8,128)(2,1)S(1)}, bf16[256,153]{0,1:T(8,128)(2,1)}, u32[]{:S(2)}) copy-start(bf16[256,153]{0,1:T(8,128)(2,1)} %param.19) | copy-start | bytes 235012
  19.4 4.2 %copy-start.5 = (s32[512,10]{0,1:T(8,128)S(1)}, s32[512,10]{0,1:T(8,128)}, u32[]{:S(2)}) copy-start(s32[512,10]{0,1:T(8,128)} %param.15) | copy-start | bytes 61444
  19.4 4.2 %copy-start.6 = (s32[256,25]{0,1:T(8,128)S(1)}, s32[256,25]{0,1:T(8,128)}, u32[]{:S(2)}) copy-start(s32[256,25]{0,1:T(8,128)} %param.17) | copy-start | bytes 76804
  19.4 4.2 %copy-start.7 = (s32[8,128]{1,0:T(8,128)S(1)}, s32[8,128]{1,0:T(8,128)}, u32[]{:S(2)}) copy-start(s32[8,128]{1,0:T(8,128)} %get-tuple-element.39.done) | copy-start | bytes 12292
  19.4 4.2 %copy-start.8 = (s32[512]{0:T(512)S(1)}, s32[512]{0:T(512)}, u32[]{:S(2)}) copy-start(s32[512]{0:T(512)} %param.16) | copy-start | bytes 6148
  19.4 4.2 %copy-start.9 = (s32[256]{0:T(256)S(1)}, s32[256]{0:T(256)}, u32[]{:S(2)}) copy-start(s32[256]{0:T(256)} %param.18) | copy-start | bytes 3076
  19.4 4.2 %copy-start.10 = (s32[16]{0:T(128)S(1)}, s32[16]{0:T(128)}, u32[]{:S(2)}) copy-start(s32[16]{0:T(128)} %counts.1) | copy-start | bytes 196
  19.4 35.8 %all-to-all-start.1 = ((bf16[16,64,768]{2,1,0:T(8,128)(2,1)}), bf16[16,64,768]{2,1,0:T(8,128)(2,1)S(1)}, u32[]{:S(2)}, u32[]{:S(2)}) async-start(bf16[16,64,768]{2,1,0:T(8,128)(2,1)} %bitcast.27), calls=%async_computation.1 | async-start | bytes 3145728 | tf_op jit(solution)/shard_map/all_to_all | solution.py:411
  30.7 1.0 copy-start.12
  31.7 1.0 copy-start.14
  32.6 51.9 %collective-permute-start.5 = (bf16[256,160]{1,0:T(8,128)(2,1)S(1)}, bf16[256,160]{1,0:T(8,128)(2,1)S(1)}, u32[]{:S(2)}, u32[]{:S(2)}) collective-permute-start(bf16[256,160]{1,0:T(8,128)(2,1)S(1)} %get-tuple-element.56.cot), channel_id=1, source_target_pairs={{0,1},{1,0},{2,3},{3,2},{4,5},{5,4},{6,7},{7,6},{8,9},{9,8},{10,11... | collective-permute-start | bytes 245768 | tf_op jit(solution)/shard_map/ppermute | solution.py:29
  55.2 1.2 copy-start.15
  56.4 2.5 %copy-start = (bf16[768,1024]{1,0:T(8,128)(2,1)S(1)}, bf16[768,1024]{1,0:T(8,128)(2,1)}, u32[]{:S(2)}) copy-start(bf16[768,1024]{1,0:T(8,128)(2,1)} %w1_self.3) | copy-start | bytes 4718596
  56.4 2.5 %copy-start.1 = (bf16[768,1024]{1,0:T(8,128)(2,1)S(1)}, bf16[768,1024]{1,0:T(8,128)(2,1)}, u32[]{:S(2)}) copy-start(bf16[768,1024]{1,0:T(8,128)(2,1)} %w1_neigh.3) | copy-start | bytes 4718596
  56.4 2.5 %copy-start.13 = (bf16[512,1024]{1,0:T(8,128)(2,1)S(1)}, bf16[512,1024]{1,0:T(8,128)(2,1)}, u32[]{:S(2)}) copy-start(bf16[512,1024]{1,0:T(8,128)(2,1)} %copy-done.12) | copy-start | bytes 3145732
  58.1 5.1 %collective-permute-start = (bf16[512,768]{1,0:T(8,128)(2,1)S(1)}, bf16[512,768]{1,0:T(8,128)(2,1)S(1)}, u32[]{:S(2)}, u32[]{:S(2)}) collective-permute-start(bf16[512,768]{1,0:T(8,128)(2,1)S(1)} %get-tuple-element.43.other), channel_id=1, source_target_pairs={{0,1},{1,0},{2,3},{3,2},{4,5},{5,4},{6,7},{7,6},{8,9},{9,8},{10,11... | collective-permute-start | bytes 2359304 | tf_op jit(solution)/shard_map/ppermute | solution.py:29
  60.7 2.4 %collective-permute-start.2 = (bf16[512,512]{1,0:T(8,128)(2,1)S(1)}, bf16[512,512]{1,0:T(8,128)(2,1)S(1)}, u32[]{:S(2)}, u32[]{:S(2)}) collective-permute-start(bf16[512,512]{1,0:T(8,128)(2,1)S(1)} %get-tuple-element.45.after.grad.far), channel_id=1, source_target_pairs={{0,1},{1,0},{2,3},{3,2},{4,5},{5,4},{6,7},{7,6},{8,9},{9,8},{10,11... | collective-permute-start | bytes 1572872 | tf_op jit(solution)/shard_map/ppermute | solution.py:29
  63.0 4.0 %collective-permute-start.1 = (bf16[512,512]{1,0:T(8,128)(2,1)S(1)}, bf16[512,512]{1,0:T(8,128)(2,1)S(1)}, u32[]{:S(2)}, u32[]{:S(2)}) collective-permute-start(bf16[512,512]{1,0:T(8,128)(2,1)S(1)} %get-tuple-element.50.after.grad), channel_id=1, source_target_pairs={{0,1},{1,0},{2,3},{3,2},{4,5},{5,4},{6,7},{7,6},{8,9},{9,8},{10,11... | collective-permute-start | bytes 1572872 | tf_op jit(solution)/shard_map/ppermute | solution.py:29
  64.3 14.6 %collective-permute-start.3 = (bf16[4,352,128]{2,1,0:T(8,128)(2,1)S(1)}, bf16[4,352,128]{2,1,0:T(8,128)(2,1)S(1)}, u32[]{:S(2)}, u32[]{:S(2)}) collective-permute-start(bf16[4,352,128]{2,1,0:T(8,128)(2,1)S(1)} %send_across.1.after), channel_id=1, source_target_pairs={{0,2},{2,0},{1,3},{3,1},{4,6},{6,4},{5,7},{7,5},{8,10},{10,8},{9,1... | collective-permute-start | bytes 1081352 | tf_op jit(solution)/shard_map/ppermute | solution.py:29
  69.0 13.1 %collective-permute-start.8 = (bf16[4,352,128]{2,1,0:T(8,128)(2,1)S(1)}, bf16[4,352,128]{2,1,0:T(8,128)(2,1)S(1)}, u32[]{:S(2)}, u32[]{:S(2)}) collective-permute-start(bf16[4,352,128]{2,1,0:T(8,128)(2,1)S(1)} %send_along.1.after), channel_id=1, source_target_pairs={{0,4},{4,0},{8,12},{12,8},{1,5},{5,1},{9,13},{13,9},{2,6},{6,2},{1... | collective-permute-start | bytes 1081352 | tf_op jit(solution)/shard_map/ppermute | solution.py:29
  78.4 6.1 %collective-permute-start.6 = (bf16[256,512]{1,0:T(8,128)(2,1)S(1)}, bf16[256,512]{1,0:T(8,128)(2,1)S(1)}, u32[]{:S(2)}, u32[]{:S(2)}) collective-permute-start(bf16[256,512]{1,0:T(8,128)(2,1)S(1)} %get-tuple-element.58), channel_id=1, source_target_pairs={{0,1},{1,0},{2,3},{3,2},{4,5},{5,4},{6,7},{7,6},{8,9},{9,8},{10,11... | collective-permute-start | bytes 786440 | tf_op jit(solution)/shard_map/ppermute | solution.py:29
  78.4 6.1 %collective-permute-start.7 = (bf16[256,512]{1,0:T(8,128)(2,1)S(1)}, bf16[256,512]{1,0:T(8,128)(2,1)S(1)}, u32[]{:S(2)}, u32[]{:S(2)}) collective-permute-start(bf16[256,512]{1,0:T(8,128)(2,1)S(1)} %get-tuple-element.60), channel_id=1, source_target_pairs={{0,1},{1,0},{2,3},{3,2},{4,5},{5,4},{6,7},{7,6},{8,9},{9,8},{10,11... | collective-permute-start | bytes 786440 | tf_op jit(solution)/shard_map/ppermute | solution.py:29
  78.9 0.9 copy-start.11
  79.9 8.5 %collective-permute-start.4 = (bf16[2,352,128]{2,1,0:T(8,128)(2,1)S(1)}, bf16[2,352,128]{2,1,0:T(8,128)(2,1)S(1)}, u32[]{:S(2)}, u32[]{:S(2)}) collective-permute-start(bf16[2,352,128]{2,1,0:T(8,128)(2,1)S(1)} %get-tuple-element.54.after), channel_id=1, source_target_pairs={{0,4},{4,0},{8,12},{12,8},{1,5},{5,1},{9,13},{13,9},{2,6},{6,2},{1... | collective-permute-start | bytes 540680 | tf_op jit(solution)/shard_map/ppermute | solution.py:29
  82.2 15.9 %collective-permute-start.11 = (bf16[2,352,128]{2,1,0:T(8,128)(2,1)S(1)}, bf16[2,352,128]{2,1,0:T(8,128)(2,1)S(1)}, u32[]{:S(2)}, u32[]{:S(2)}) collective-permute-start(bf16[2,352,128]{2,1,0:T(8,128)(2,1)S(1)} %get-tuple-element.61.after), channel_id=1, source_target_pairs={{0,8},{4,12},{8,0},{12,4},{1,9},{5,13},{9,1},{13,5},{2,10},{6,14},... | collective-permute-start | bytes 540680 | tf_op jit(solution)/shard_map/ppermute | solution.py:29
  86.4 12.7 %collective-permute-start.10 = (bf16[4,224,128]{2,1,0:T(8,128)(2,1)S(1)}, bf16[4,224,128]{2,1,0:T(8,128)(2,1)S(1)}, u32[]{:S(2)}, u32[]{:S(2)}) collective-permute-start(bf16[4,224,128]{2,1,0:T(8,128)(2,1)S(1)} %get-tuple-element.63), channel_id=1, source_target_pairs={{0,2},{2,0},{1,3},{3,1},{4,6},{6,4},{5,7},{7,5},{8,10},{10,8},{9,1... | collective-permute-start | bytes 688136 | tf_op jit(solution)/shard_map/ppermute | solution.py:29
  88.4 12.4 %collective-permute-start.9 = (bf16[2,352,128]{2,1,0:T(8,128)(2,1)S(1)}, bf16[2,352,128]{2,1,0:T(8,128)(2,1)S(1)}, u32[]{:S(2)}, u32[]{:S(2)}) collective-permute-start(bf16[2,352,128]{2,1,0:T(8,128)(2,1)S(1)} %add.13.after.mine), channel_id=1, source_target_pairs={{0,8},{4,12},{8,0},{12,4},{1,9},{5,13},{9,1},{13,5},{2,10},{6,14},... | collective-permute-start | bytes 540680 | tf_op jit(solution)/shard_map/ppermute | solution.py:29
  98.1 5.6 %collective-permute-start.14 = (bf16[2,352,128]{2,1,0:T(8,128)(2,1)S(1)}, bf16[2,352,128]{2,1,0:T(8,128)(2,1)S(1)}, u32[]{:S(2)}, u32[]{:S(2)}) collective-permute-start(bf16[2,352,128]{2,1,0:T(8,128)(2,1)S(1)} %add.14.after.mine), channel_id=1, source_target_pairs={{0,2},{2,0},{1,3},{3,1},{4,6},{6,4},{5,7},{7,5},{8,10},{10,8},{9,1... | collective-permute-start | bytes 540680 | tf_op jit(solution)/shard_map/ppermute | solution.py:29
  99.1 8.9 %collective-permute-start.13 = (bf16[2,224,128]{2,1,0:T(8,128)(2,1)S(1)}, bf16[2,224,128]{2,1,0:T(8,128)(2,1)S(1)}, u32[]{:S(2)}, u32[]{:S(2)}) collective-permute-start(bf16[2,224,128]{2,1,0:T(8,128)(2,1)S(1)} %get-tuple-element.65.after), channel_id=1, source_target_pairs={{0,4},{4,0},{8,12},{12,8},{1,5},{5,1},{9,13},{13,9},{2,6},{6,2},{1... | collective-permute-start | bytes 344072 | tf_op jit(solution)/shard_map/ppermute | solution.py:29
  100.9 10.2 %collective-permute-start.12 = (bf16[2,352,128]{2,1,0:T(8,128)(2,1)S(1)}, bf16[2,352,128]{2,1,0:T(8,128)(2,1)S(1)}, u32[]{:S(2)}, u32[]{:S(2)}) collective-permute-start(bf16[2,352,128]{2,1,0:T(8,128)(2,1)S(1)} %meet.3.after.near), channel_id=1, source_target_pairs={{0,4},{4,0},{8,12},{12,8},{1,5},{5,1},{9,13},{13,9},{2,6},{6,2},{1... | collective-permute-start | bytes 540680 | tf_op jit(solution)/shard_map/ppermute | solution.py:29
  103.7 11.9 %collective-permute-start.18 = (bf16[2,352,128]{2,1,0:T(8,128)(2,1)S(1)}, bf16[2,352,128]{2,1,0:T(8,128)(2,1)S(1)}, u32[]{:S(2)}, u32[]{:S(2)}) collective-permute-start(bf16[2,352,128]{2,1,0:T(8,128)(2,1)S(1)} %meet.4.after.near), channel_id=1, source_target_pairs={{0,8},{4,12},{8,0},{12,4},{1,9},{5,13},{9,1},{13,5},{2,10},{6,14},... | collective-permute-start | bytes 540680 | tf_op jit(solution)/shard_map/ppermute | solution.py:29
  108.0 8.8 %collective-permute-start.22 = (bf16[2,224,128]{2,1,0:T(8,128)(2,1)S(1)}, bf16[2,224,128]{2,1,0:T(8,128)(2,1)S(1)}, u32[]{:S(2)}, u32[]{:S(2)}) collective-permute-start(bf16[2,224,128]{2,1,0:T(8,128)(2,1)S(1)} %add.15.after.later.mine), channel_id=1, source_target_pairs={{0,8},{4,12},{8,0},{12,4},{1,9},{5,13},{9,1},{13,5},{2,10},{6,14},... | collective-permute-start | bytes 344072 | tf_op jit(solution)/shard_map/ppermute | solution.py:29
  111.1 11.9 %collective-permute-start.15 = (bf16[4,352,128]{2,1,0:T(8,128)(2,1)S(1)}, bf16[4,352,128]{2,1,0:T(8,128)(2,1)S(1)}, u32[]{:S(2)}, u32[]{:S(2)}) collective-permute-start(bf16[4,352,128]{2,1,0:T(8,128)(2,1)S(1)} %join.3.after.later.refs_0_), channel_id=1, source_target_pairs={{0,2},{2,0},{1,3},{3,1},{4,6},{6,4},{5,7},{7,5},{8,10},{10,8},{9,1... | collective-permute-start | bytes 1081352 | tf_op jit(solution)/shard_map/ppermute | solution.py:29
  116.9 6.2 %collective-permute-start.23 = (bf16[2,224,128]{2,1,0:T(8,128)(2,1)S(1)}, bf16[2,224,128]{2,1,0:T(8,128)(2,1)S(1)}, u32[]{:S(2)}, u32[]{:S(2)}) collective-permute-start(bf16[2,224,128]{2,1,0:T(8,128)(2,1)S(1)} %meet.5.near.after), channel_id=1, source_target_pairs={{0,4},{4,0},{8,12},{12,8},{1,5},{5,1},{9,13},{13,9},{2,6},{6,2},{1... | collective-permute-start | bytes 344072 | tf_op jit(solution)/shard_map/ppermute | solution.py:29
  117.0 9.9 %collective-permute-start.19 = (bf16[4,352,128]{2,1,0:T(8,128)(2,1)S(1)}, bf16[4,352,128]{2,1,0:T(8,128)(2,1)S(1)}, u32[]{:S(2)}, u32[]{:S(2)}) collective-permute-start(bf16[4,352,128]{2,1,0:T(8,128)(2,1)S(1)} %join.4.after.refs_4_), channel_id=1, source_target_pairs={{0,4},{4,0},{8,12},{12,8},{1,5},{5,1},{9,13},{13,9},{2,6},{6,2},{1... | collective-permute-start | bytes 1081352 | tf_op jit(solution)/shard_map/ppermute | solution.py:29
  119.0 8.4 %collective-permute-start.20 = (bf16[4,352,128]{2,1,0:T(8,128)(2,1)S(1)}, bf16[4,352,128]{2,1,0:T(8,128)(2,1)S(1)}, u32[]{:S(2)}, u32[]{:S(2)}) collective-permute-start(bf16[4,352,128]{2,1,0:T(8,128)(2,1)S(1)} %join.4.after.refs_4_), channel_id=1, source_target_pairs={{0,1},{1,0},{2,3},{3,2},{4,5},{5,4},{6,7},{7,6},{8,9},{9,8},{10,11... | collective-permute-start | bytes 1081352 | tf_op jit(solution)/shard_map/ppermute | solution.py:29
  123.1 6.1 %collective-permute-start.24 = (bf16[4,224,128]{2,1,0:T(8,128)(2,1)S(1)}, bf16[4,224,128]{2,1,0:T(8,128)(2,1)S(1)}, u32[]{:S(2)}, u32[]{:S(2)}) collective-permute-start(bf16[4,224,128]{2,1,0:T(8,128)(2,1)S(1)} %join.5.refs_8_), channel_id=1, source_target_pairs={{0,2},{2,0},{1,3},{3,1},{4,6},{6,4},{5,7},{7,5},{8,10},{10,8},{9,1... | collective-permute-start | bytes 688136 | tf_op jit(solution)/shard_map/ppermute | solution.py:29
  123.6 5.6 %collective-permute-start.16 = (bf16[4,352,128]{2,1,0:T(8,128)(2,1)S(1)}, bf16[4,352,128]{2,1,0:T(8,128)(2,1)S(1)}, u32[]{:S(2)}, u32[]{:S(2)}) collective-permute-start(bf16[4,352,128]{2,1,0:T(8,128)(2,1)S(1)} %join.3.after.later.refs_0_), channel_id=1, source_target_pairs={{0,1},{1,0},{2,3},{3,2},{4,5},{5,4},{6,7},{7,6},{8,9},{9,8},{10,11... | collective-permute-start | bytes 1081352 | tf_op jit(solution)/shard_map/ppermute | solution.py:29
  126.9 2.5 %collective-permute-start.21 = (bf16[4,352,128]{2,1,0:T(8,128)(2,1)S(1)}, bf16[4,352,128]{2,1,0:T(8,128)(2,1)S(1)}, u32[]{:S(2)}, u32[]{:S(2)}) collective-permute-start(bf16[4,352,128]{2,1,0:T(8,128)(2,1)S(1)} %collective-permute-done.19.refs_5_), channel_id=1, source_target_pairs={{0,1},{1,0},{2,3},{3,2},{4,5},{5,4},{6,7},{7,6},{8,9},{9,8},{10,11... | collective-permute-start | bytes 1081352 | tf_op jit(solution)/shard_map/ppermute | solution.py:29
  126.9 2.5 %collective-permute-start.17 = (bf16[4,352,128]{2,1,0:T(8,128)(2,1)S(1)}, bf16[4,352,128]{2,1,0:T(8,128)(2,1)S(1)}, u32[]{:S(2)}, u32[]{:S(2)}) collective-permute-start(bf16[4,352,128]{2,1,0:T(8,128)(2,1)S(1)} %collective-permute-done.15.later.refs_1_), channel_id=1, source_target_pairs={{0,1},{1,0},{2,3},{3,2},{4,5},{5,4},{6,7},{7,6},{8,9},{9,8},{10,11... | collective-permute-start | bytes 1081352 | tf_op jit(solution)/shard_map/ppermute | solution.py:29
  127.4 2.0 %collective-permute-start.25 = (bf16[4,224,128]{2,1,0:T(8,128)(2,1)S(1)}, bf16[4,224,128]{2,1,0:T(8,128)(2,1)S(1)}, u32[]{:S(2)}, u32[]{:S(2)}) collective-permute-start(bf16[4,224,128]{2,1,0:T(8,128)(2,1)S(1)} %join.5.refs_8_), channel_id=1, source_target_pairs={{0,1},{1,0},{2,3},{3,2},{4,5},{5,4},{6,7},{7,6},{8,9},{9,8},{10,11... | collective-permute-start | bytes 688136 | tf_op jit(solution)/shard_map/ppermute | solution.py:29
  129.2 1.5 %collective-permute-start.26 = (bf16[4,224,128]{2,1,0:T(8,128)(2,1)S(1)}, bf16[4,224,128]{2,1,0:T(8,128)(2,1)S(1)}, u32[]{:S(2)}, u32[]{:S(2)}) collective-permute-start(bf16[4,224,128]{2,1,0:T(8,128)(2,1)S(1)} %collective-permute-done.24.refs_9_), channel_id=1, source_target_pairs={{0,1},{1,0},{2,3},{3,2},{4,5},{5,4},{6,7},{7,6},{8,9},{9,8},{10,11... | collective-permute-start | bytes 688136 | tf_op jit(solution)/shard_map/ppermute | solution.py:29

commit v4 on v3

--- a/solution.py
+++ b/solution.py
@@ -8,6 +8,10 @@
 from jax.sharding import PartitionSpec as P
 
 LANES = 128
+GROUPS = ((4, 5, 6, 7), (2, 3, 1, 0))
+ASK = 0
+BESIDE = 3
+LANDINGS = (0, 4, 5, 6, 7, 2, 3, 1)
 CORE_STEP = ("sub", 2, 1)
 BLOCKS = 8
 TRAINERS = ("tr", "cache", "sub")
@@ -228,6 +232,84 @@
         compiler_params=params(56),
         name="pick_rows",
     )(asked, table)
+
+
+def route_kernel(info, requests, own, other):
+    for distance in range(own.shape[0]):
+        at = 2 * jnp.bitwise_xor(info[2], distance)
+        own[distance : distance + 1] = requests[pl.ds(at + info[0], 1)]
+        other[distance : distance + 1] = requests[pl.ds(at + 1 - info[0], 1)]
+
+
+def bundle_kernel(distances, own, got, after, *outs):
+    for distance, out in zip(distances, outs):
+        out[:1] = own[distance : distance + 1]
+        out[1:] = got[distance : distance + 1]
+
+
+def serve_kernel(asked, table, after, out):
+    trainers, slots = asked.shape
+    wide = lax.broadcasted_iota(jnp.int32, (slots, table.shape[0]), 1)
+    columns = asked[...].T
+    hits = [jnp.where(columns[:, t : t + 1] == wide, 1.0, 0.0).astype(BF16) for t in range(trainers)]
+    out[...] = jnp.dot(jnp.concatenate(hits, 0), table[...], preferred_element_type=F32).astype(BF16)
+
+
+def fetch(info, requests, table, chips, meanwhile):
+    slots, feat = requests.shape[1], table.shape[1]
+    ids, rows = ((chips, slots), jnp.int32), ((2 * slots, feat), BF16)
+    own, other = kernel_call(route_kernel, "route", [ids, ids], [SMEM, VMEM], 16, info, requests)
+    passed = swap(other, *CORE_STEP)
+    after, landed = own, {}
+
+    def bundles(distances, after):
+        return dict(zip(distances, kernel_call(
+            functools.partial(bundle_kernel, distances), "bundle", [((2, slots), jnp.int32)] * len(distances),
+            [VMEM, VMEM, ANY], 16, own, passed, after,
+        )))
+
+    def across_chips(array, distance):
+        return lax.ppermute(array, ("tr", "cache"), [(i, i ^ distance) for i in range(chips)])
+
+    asked = bundles(GROUPS[0], own)
+    for which, group in enumerate(GROUPS):
+        arrived = {d: across_chips(asked[d], d) if d else asked[d] for d in group}
+        for number, distance in enumerate(group):
+            after, = kernel_call(
+                serve_kernel, "serve", [rows], [VMEM, VMEM, ANY], 16, arrived[distance], table, after
+            )
+            landed[distance] = across_chips(after, distance) if distance else after
+            if number == ASK and which + 1 < len(GROUPS):
+                asked = bundles(GROUPS[which + 1], after)
+            if distance == BESIDE:
+                made = meanwhile(after)
+                after = made[0]
+    far = {}
+    for distance in LANDINGS:
+        if distance:
+            landed[distance], = kernel_call(
+                land_kernel, "land", [rows], [ANY, ANY], 16, landed[distance], after,
+                out_specs=[ANY], input_output_aliases={0: 0},
+            )
+            after = landed[distance]
+        far[distance] = swap(landed[distance], *CORE_STEP)
+    order = range(chips)
+    return [landed[d] for d in order], [far[d] for d in order], made, after
+
+
+def land_kernel(rows, after, out):
+    pass
+
+
+def landed_kernel(chips, info, *refs):
+    near, far, (sides, adjacency, after, mine, other, held) = refs[:chips], refs[chips : 2 * chips], refs[2 * chips :]
+    slots = near[0].shape[0] // 2
+    for distance in range(chips):
+        at = 2 * jnp.bitwise_xor(info[2], distance)
+        for array, first, owner in ((near, 0, at + info[0]), (far, slots, at + 1 - info[0])):
+            where = pl.ds(pl.multiple_of(owner * slots, slots), slots)
+            held[where] = array[distance][first : first + slots]
+    mean_kernel(info, held, sides, adjacency, mine, other)
 
 
 def column_of(row):
@@ -401,27 +483,43 @@
     across = axis_bits("cache", sizes["cache"]) + axis_bits("tr", sizes["tr"])
     along = across[1:3] + across[:1] + across[3:]
     place = 4 * bit_of(across[0]) + 2 * bit_of(across[1]) + bit_of(across[2])
-    info = jnp.stack([lax.axis_index("sub"), place]).astype(jnp.int32)
+    chips = sizes["tr"] * sizes["cache"]
+    chip = lax.axis_index("tr") * sizes["cache"] + lax.axis_index("cache")
+    info = jnp.stack([lax.axis_index("sub"), place, chip]).astype(jnp.int32)
     padded = -(-classes // 32) * 32
     part = feat * 352 // 768 // 16 * 16
     last = feat - 2 * part
 
-    asked = lax.all_to_all(requests, TRAINERS, split_axis=0, concat_axis=0, tiled=True)
-    picked, done = pick_rows(asked, table)
-    fetched = lax.all_to_all(
-        picked.reshape(peer_count, slot_count, feat), TRAINERS, split_axis=0, concat_axis=0, tiled=True
-    ).reshape(peer_count * slot_count, feat)
-
-    adj_low, adj_top, sides, scale_top, grad_hidden, cotangent = beside(
-        peer_count * slot_count, padded, counts, nbr_low.T, fan_low[None], nbr_top.T, fan_top[None],
-        grad_logits.T, w2_self.T, w2_neigh.T, done,
-    )
+    def meanwhile(after):
+        return beside(
+            peer_count * slot_count, padded, counts, nbr_low.T, fan_low[None], nbr_top.T, fan_top[None],
+            grad_logits.T, w2_self.T, w2_neigh.T, after,
+        )
+
+    by_chip = chips == BLOCKS and slot_count % 16 == 0
+    if by_chip:
+        near, far, made, after = fetch(info, requests, table, chips, meanwhile)
+    else:
+        asked = lax.all_to_all(requests, TRAINERS, split_axis=0, concat_axis=0, tiled=True)
+        picked, done = pick_rows(asked, table)
+        fetched = lax.all_to_all(
+            picked.reshape(peer_count, slot_count, feat), TRAINERS, split_axis=0, concat_axis=0, tiled=True
+        ).reshape(peer_count * slot_count, feat)
+        made = meanwhile(done)
+    adj_low, adj_top, sides, scale_top, grad_hidden, cotangent = made
     cotangent_got = swap(cotangent, *CORE_STEP)
 
     low = ((middle, feat), BF16)
-    mine, other = kernel_call(
-        mean_kernel, "mean", [low, low], [SMEM] + [VMEM] * 3, 24, info, fetched, sides, adj_low,
-    )
+    if by_chip:
+        mine, other = kernel_call(
+            functools.partial(landed_kernel, chips), "mean", [low, low], [SMEM] + [VMEM] * (2 * chips + 2) + [ANY], 24,
+            info, *near, *far, sides, adj_low, after,
+            scratch_shapes=[pltpu.VMEM((peer_count * slot_count, feat), BF16)],
+        )
+    else:
+        mine, other = kernel_call(
+            mean_kernel, "mean", [low, low], [SMEM] + [VMEM] * 3, 24, info, fetched, sides, adj_low,
+        )
     got = swap(other, *CORE_STEP)
     half = ((middle, width // 2), BF16)
     hidden, grads, grads_got = [None] * 2, [None] * 2, [None] * 2

time: 135 us -> 127 us (0.941)
  blocking collectives: 13.7 us -> 0 us
  starting transfers between devices: 26.8 us -> 38.8 us
  waiting for transfers between devices: 57.6 us -> 54.8 us
  local copies, waits for them, and re-layouts: 4.17 us -> 1.76 us
    all_to_all x1 -> x0, waiting for transfers between devices: 22.5 us -> none  [on_device(): lax.all_to_all(picked.reshape(peer_count, slot_count, feat), TRAINERS, sp...]
    ppermute x0 -> x14, starting transfers between devices: none -> 21.2 us  [across_chips(): lax.ppermute(array, ('tr', 'cache'), [(i, i ^ distance) for i in range(ch...]
    ppermute x0 -> x14, waiting for transfers between devices: none -> 16 us  [across_chips(): lax.ppermute(array, ('tr', 'cache'), [(i, i ^ distance) for i in range(ch...]
    all_to_all x1 -> x0, blocking collectives: 13.7 us -> none  [on_device(): lax.all_to_all(requests, TRAINERS, split_axis=0, concat_axis=0, tiled=True)]
    ppermute x27 -> x36, starting transfers between devices: 22.8 us -> 17.5 us  [swap(): return lax.ppermute(array, axis, [(i, i ^ distance) for i in range(size)])]
    pallas_call x1 -> x0, Pallas kernels: 5.05 us -> none  [pick_rows(): pl.pallas_call(pick_kernel, out_shape=[jax.ShapeDtypeStruct((total, table...]
    pallas_call x21 -> x39, Pallas kernels: 19 us -> 23.6 us  [kernel_call(): pl.pallas_call(body, out_shape=[jax.ShapeDtypeStruct(*out) for out in out...]
    all_to_all x1 -> x0, starting transfers between devices: 4.03 us -> none  [on_device(): lax.all_to_all(picked.reshape(peer_count, slot_count, feat), TRAINERS, sp...]
  transfers between devices with their start and end apart: 28 -> 50, of which waited for: 15 -> 24; matrix products, arithmetic and copies ran while one was open for 0% -> 0% of each run, Pallas kernels for 17% -> 21%
where the time goes in v4:
time: 127 us
  waiting for transfers between devices  54.8 us (43%)
  starting transfers between devices  38.8 us (31%)
  Pallas kernels  30.6 us (24%)
  local copies, waits for them, and re-layouts  1.76 us (1%)
    ppermute x36, waiting for transfers between devices, swap(): return lax.ppermute(array, axis, [(i, i ^ distance) for i in range(size)])  38.8 us
    pallas_call x39, Pallas kernels, kernel_call(): pl.pallas_call(body, out_shape=[jax.ShapeDtypeStruct(*out) for out in out...  23.6 us
    ppermute x14, starting transfers between devices, across_chips(): lax.ppermute(array, ('tr', 'cache'), [(i, i ^ distance) for i in range(ch...  21.2 us
    ppermute x36, starting transfers between devices, swap(): return lax.ppermute(array, axis, [(i, i ^ distance) for i in range(size)])  17.5 us
    ppermute x14, waiting for transfers between devices, across_chips(): lax.ppermute(array, ('tr', 'cache'), [(i, i ^ distance) for i in range(ch...  16 us
    pallas_call x1, Pallas kernels, beside(): pl.pallas_call(beside_kernel, out_shape=[shape((middle, inputs), BF16), s...  7 us
  transfers between devices with their start and end apart: 50, of which 24 were waited for; matrix products, arithmetic and copies ran while one was open for 0% of the time, Pallas kernels for 21%

profile of v4, /device:TPU:0, one launch (start us, length us, event | category | flops | bytes accessed | tf_op | source)
XLA Modules:
  0.0 127.2 jit_solution(17568632687424823626)
XLA Ops:
  2.5 0.8 collective-permute-done.got
  3.4 3.9 %collective-permute-start.1 = (s32[2,64]{1,0:T(2,128)S(1)}, s32[2,64]{1,0:T(2,128)S(1)}, u32[]{:S(2)}, u32[]{:S(2)}) collective-permute-start(s32[2,64]{1,0:T(2,128)S(1)} %get-tuple-element.48), channel_id=1, source_target_pairs={{0,8},{2,10},{4,12},{6,14},{8,0},{10,2},{12,4},{14,6},{1,9},{3,11}... | collective-permute-start | bytes 1544 | tf_op jit(solution)/shard_map/ppermute | solution.py:272
  7.3 1.3 collective-permute-start.7
  8.5 3.6 %collective-permute-start.6 = (s32[2,64]{1,0:T(2,128)S(1)}, s32[2,64]{1,0:T(2,128)S(1)}, u32[]{:S(2)}, u32[]{:S(2)}) collective-permute-start(s32[2,64]{1,0:T(2,128)S(1)} %get-tuple-element.54), channel_id=1, source_target_pairs={{0,12},{2,14},{4,8},{6,10},{8,4},{10,6},{12,0},{14,2},{1,13},{3,15... | collective-permute-start | bytes 1544 | tf_op jit(solution)/shard_map/ppermute | solution.py:272
  12.6 1.0 collective-permute-start.14
  13.7 3.4 %collective-permute-start.4 = (s32[2,64]{1,0:T(2,128)S(1)}, s32[2,64]{1,0:T(2,128)S(1)}, u32[]{:S(2)}, u32[]{:S(2)}) collective-permute-start(s32[2,64]{1,0:T(2,128)S(1)} %get-tuple-element.52), channel_id=1, source_target_pairs={{0,4},{2,6},{4,0},{6,2},{8,12},{10,14},{12,8},{14,10},{1,5},{3,7},... | collective-permute-start | bytes 1544 | tf_op jit(solution)/shard_map/ppermute | solution.py:272
  17.1 1.0 collective-permute-start.3
  19.6 3.9 %collective-permute-start.12 = (bf16[128,768]{1,0:T(8,128)(2,1)S(1)}, bf16[128,768]{1,0:T(8,128)(2,1)S(1)}, u32[]{:S(2)}, u32[]{:S(2)}) collective-permute-start(bf16[128,768]{1,0:T(8,128)(2,1)S(1)} %serve.10.after), channel_id=1, source_target_pairs={{0,12},{2,14},{4,8},{6,10},{8,4},{10,6},{12,0},{14,2},{1,13},{3,15... | collective-permute-start | bytes 589832 | tf_op jit(solution)/shard_map/ppermute | solution.py:272
  24.0 1.2 collective-permute-start.11
  26.8 7.0 %beside.1 = (bf16[512,1024]{1,0:T(8,128)(2,1)S(1)}, bf16[256,512]{1,0:T(8,128)(2,1)S(1)}, f32[512,2]{1,0:T(8,128)S(1)}, f32[256,1]{1,0:T(8,128)S(1)}, bf16[512,1...) custom-call(s32[16]{0:T(128)S(1)} %copy-done.15, s32[10,512]{1,0:T(8,128)S(1)} %bitcast.18, s32[1,512]{1,0:T(1,128)S(1)} %bitcast.20, ...), custom_call_target="tpu_custom_call" | custom-call | flops 10000000000 | bytes 10000000 | tf_op jit(solution)/shard_map/beside/pallas_call | solution.py:367
  34.9 2.8 %collective-permute-done.14.rows = bf16[128,768]{1,0:T(8,128)(2,1)S(1)} collective-permute-done((bf16[128,768]{1,0:T(8,128)(2,1)S(1)}, bf16[128,768]{1,0:T(8,128)(2,1)S(1)}, u32[]{:S(2)}, u32[]{:S(2)}) %collective-permute-start.14) | collective-permute-done | bytes 196640 | tf_op jit(solution)/shard_map/ppermute | solution.py:272
  38.1 4.7 %collective-permute-done.13.rows = bf16[128,768]{1,0:T(8,128)(2,1)S(1)} collective-permute-done((bf16[128,768]{1,0:T(8,128)(2,1)S(1)}, bf16[128,768]{1,0:T(8,128)(2,1)S(1)}, u32[]{:S(2)}, u32[]{:S(2)}) %collective-permute-start.13) | collective-permute-done | bytes 196640 | tf_op jit(solution)/shard_map/ppermute | solution.py:272
  43.9 1.3 collective-permute-done.10.rows
  45.1 5.1 %collective-permute-done.9.rows = bf16[128,768]{1,0:T(8,128)(2,1)S(1)} collective-permute-done((bf16[128,768]{1,0:T(8,128)(2,1)S(1)}, bf16[128,768]{1,0:T(8,128)(2,1)S(1)}, u32[]{:S(2)}, u32[]{:S(2)}) %collective-permute-start.9) | collective-permute-done | bytes 196640 | tf_op jit(solution)/shard_map/ppermute | solution.py:272
  50.3 2.0 %collective-permute-done.8.rows = bf16[128,768]{1,0:T(8,128)(2,1)S(1)} collective-permute-done((bf16[128,768]{1,0:T(8,128)(2,1)S(1)}, bf16[128,768]{1,0:T(8,128)(2,1)S(1)}, u32[]{:S(2)}, u32[]{:S(2)}) %collective-permute-start.8) | collective-permute-done | bytes 196640 | tf_op jit(solution)/shard_map/ppermute | solution.py:272
  54.6 1.9 %mean.1 = (bf16[512,768]{1,0:T(8,128)(2,1)S(1)}, bf16[512,768]{1,0:T(8,128)(2,1)S(1)}) custom-call(s32[3]{0:T(128)S(1)} %copy-done.1, bf16[128,768]{1,0:T(8,128)(2,1)S(1)} %serve.15.after.refs_0_, bf16[128,768]{1,0:T(8,128)(2,1)S(1)} %land.13.refs_1_.refs_18_, bf16[128,768]{1,0:T(8,128)(2,1)S(1)} %land.11.after.refs_2_, ...), custom_call_target="tpu_custom_call" | custom-call | flops 10000000000 | bytes 10000000 | tf_op jit(solution)/shard_map/mean/pallas_call | solution.py:46
  56.8 1.8 %hidden.2 = (bf16[512,512]{1,0:T(8,128)(2,1)S(1)}, bf16[512,512]{1,0:T(8,128)(2,1)S(1)}) custom-call(s32[3]{0:T(128)S(1)} %copy-done.1, bf16[512,768]{1,0:T(8,128)(2,1)S(1)} %get-tuple-element.58.mine.after, bf16[512,768]{1,0:T(8,128)(2,1)S(1)} %get-tuple-element.59.other, bf16[768,1024]{1,0:T(8,128)(2,1)S(1)} %copy-done.3, bf16[768,1024]{1,0:T(8,128)(2,1)S(1)} %copy-done.4, ...), custom_call_target="tpu_custom_call" | custom-call | flops 10000000000 | bytes 10000000 | tf_op jit(solution)/shard_map/hidden/pallas_call | solution.py:46
  58.9 1.8 %hidden.3 = (bf16[512,512]{1,0:T(8,128)(2,1)S(1)}, bf16[512,512]{1,0:T(8,128)(2,1)S(1)}) custom-call(s32[3]{0:T(128)S(1)} %copy-done.1, bf16[512,768]{1,0:T(8,128)(2,1)S(1)} %get-tuple-element.58.mine.after, bf16[512,768]{1,0:T(8,128)(2,1)S(1)} %get-tuple-element.59.other, bf16[768,1024]{1,0:T(8,128)(2,1)S(1)} %copy-done.3, bf16[768,1024]{1,0:T(8,128)(2,1)S(1)} %copy-done.4, ...), custom_call_target="tpu_custom_call" | custom-call | flops 10000000000 | bytes 10000000 | tf_op jit(solution)/shard_map/hidden/pallas_call | solution.py:46
  61.0 1.1 send_across.1.after
  62.8 2.0 %send_along.1.after = bf16[4,352,128]{2,1,0:T(8,128)(2,1)S(1)} custom-call(s32[3]{0:T(128)S(1)} %copy-done.1, bf16[512,768]{1,0:T(8,128)(2,1)S(1)} %get-tuple-element.58.mine.after, bf16[512,768]{1,0:T(8,128)(2,1)S(1)} %collective-permute-done.23.got, bf16[512,512]{1,0:T(8,128)(2,1)S(1)} %get-tuple-element.66.after.grad, ...), custom_call_target="tpu_custom_call" | custom-call | flops 10000000000 | bytes 10000000 | tf_op jit(solution)/shard_map/send_along/pallas_call | solution.py:46
  64.8 1.0 collective-permute-start.31
  65.8 2.4 %keep.1 = (f32[4,352,128]{2,1,0:T(8,128)S(1)}, f32[4,352,128]{2,1,0:T(8,128)S(1)}) custom-call(s32[3]{0:T(128)S(1)} %copy-done.1, bf16[512,768]{1,0:T(8,128)(2,1)S(1)} %get-tuple-element.58.mine.after, bf16[512,768]{1,0:T(8,128)(2,1)S(1)} %collective-permute-done.23.got, bf16[512,512]{1,0:T(8,128)(2,1)S(1)} %get-tuple-element.66.after.grad, ...), custom_call_target="tpu_custom_call" | custom-call | flops 10000000000 | bytes 10000000 | tf_op jit(solution)/shard_map/keep/pallas_call | solution.py:46
  68.3 2.2 %top.1 = (f32[153,256]{1,0:T(8,128)}, bf16[256,512]{1,0:T(8,128)(2,1)S(1)}, bf16[256,512]{1,0:T(8,128)(2,1)S(1)}, bf16[256,512]{1,0:T(8,128)(2,1)S(1)}, bf16[256,512]{1,0:T(8,128)(2,1)S(1)}) custom-call(s32[3]{0:T(128)S(1)} %copy-done.1, bf16[512,512]{1,0:T(8,128)(2,1)S(1)} %get-tuple-element.62.near, bf16[512,512]{1,0:T(8,128)(2,1)S(1)} %get-tuple-element.63.far, ...), custom_call_target="tpu_custom_call" | custom-call | flops 10000000000 | bytes 10000000 | tf_op jit(solution)/shard_map/top/pallas_call | solution.py:46
  71.0 1.8 %collective-permute-done.26.got = bf16[4,352,128]{2,1,0:T(8,128)(2,1)S(1)} collective-permute-done((bf16[4,352,128]{2,1,0:T(8,128)(2,1)S(1)}, bf16[4,352,128]{2,1,0:T(8,128)(2,1)S(1)}, u32[]{:S(2)}, u32[]{:S(2)}) %collective-permute-start.26) | collective-permute-done | bytes 360480 | tf_op jit(solution)/shard_map/ppermute | solution.py:33
  72.8 0.9 copy-done.16
  73.8 1.1 collective-permute-start.27
  75.4 2.0 %collective-permute-start.34 = (bf16[2,352,128]{2,1,0:T(8,128)(2,1)S(1)}, bf16[2,352,128]{2,1,0:T(8,128)(2,1)S(1)}, u32[]{:S(2)}, u32[]{:S(2)}) collective-permute-start(bf16[2,352,128]{2,1,0:T(8,128)(2,1)S(1)} %get-tuple-element.77.after), channel_id=1, source_target_pairs={{0,8},{4,12},{8,0},{12,4},{1,9},{5,13},{9,1},{13,5},{2,10},{6,14},... | collective-permute-start | bytes 540680 | tf_op jit(solution)/shard_map/ppermute | solution.py:33
  77.4 1.9 %last.1 = (bf16[4,224,128]{2,1,0:T(8,128)(2,1)S(1)}, f32[4,224,128]{2,1,0:T(8,128)S(1)}) custom-call(s32[3]{0:T(128)S(1)} %copy-done.1, bf16[512,768]{1,0:T(8,128)(2,1)S(1)} %get-tuple-element.58.mine.after, bf16[512,768]{1,0:T(8,128)(2,1)S(1)} %collective-permute-done.23.got, bf16[512,512]{1,0:T(8,128)(2,1)S(1)} %get-tuple-element.66.after.grad, ...), custom_call_target="tpu_custom_call" | custom-call | flops 10000000000 | bytes 10000000 | tf_op jit(solution)/shard_map/last/pallas_call | solution.py:46
  79.3 1.1 collective-permute-start.33
  80.4 2.0 %collective-permute-done.27.got = bf16[2,352,128]{2,1,0:T(8,128)(2,1)S(1)} collective-permute-done((bf16[2,352,128]{2,1,0:T(8,128)(2,1)S(1)}, bf16[2,352,128]{2,1,0:T(8,128)(2,1)S(1)}, u32[]{:S(2)}, u32[]{:S(2)}) %collective-permute-start.27) | collective-permute-done | bytes 180256 | tf_op jit(solution)/shard_map/ppermute | solution.py:33
  82.4 0.7 collective-permute-start.32
  83.1 7.9 %collective-permute-done.34.got = bf16[2,352,128]{2,1,0:T(8,128)(2,1)S(1)} collective-permute-done((bf16[2,352,128]{2,1,0:T(8,128)(2,1)S(1)}, bf16[2,352,128]{2,1,0:T(8,128)(2,1)S(1)}, u32[]{:S(2)}, u32[]{:S(2)}) %collective-permute-start.34) | collective-permute-done | bytes 180256 | tf_op jit(solution)/shard_map/ppermute | solution.py:33
  91.1 1.4 %collective-permute-start.37 = (bf16[2,352,128]{2,1,0:T(8,128)(2,1)S(1)}, bf16[2,352,128]{2,1,0:T(8,128)(2,1)S(1)}, u32[]{:S(2)}, u32[]{:S(2)}) collective-permute-start(bf16[2,352,128]{2,1,0:T(8,128)(2,1)S(1)} %add.20.after.mine), channel_id=1, source_target_pairs={{0,2},{2,0},{1,3},{3,1},{4,6},{6,4},{5,7},{7,5},{8,10},{10,8},{9,1... | collective-permute-start | bytes 540680 | tf_op jit(solution)/shard_map/ppermute | solution.py:33
  92.6 1.2 collective-permute-done.32.got
  93.9 0.8 collective-permute-start.35
  94.7 1.9 %collective-permute-done.37.got = bf16[2,352,128]{2,1,0:T(8,128)(2,1)S(1)} collective-permute-done((bf16[2,352,128]{2,1,0:T(8,128)(2,1)S(1)}, bf16[2,352,128]{2,1,0:T(8,128)(2,1)S(1)}, u32[]{:S(2)}, u32[]{:S(2)}) %collective-permute-start.37) | collective-permute-done | bytes 180256 | tf_op jit(solution)/shard_map/ppermute | solution.py:33
  96.8 5.4 %collective-permute-done.36.got = bf16[2,224,128]{2,1,0:T(8,128)(2,1)S(1)} collective-permute-done((bf16[2,224,128]{2,1,0:T(8,128)(2,1)S(1)}, bf16[2,224,128]{2,1,0:T(8,128)(2,1)S(1)}, u32[]{:S(2)}, u32[]{:S(2)}) %collective-permute-start.36) | collective-permute-done | bytes 114720 | tf_op jit(solution)/shard_map/ppermute | solution.py:33
  102.3 2.2 %collective-permute-done.35.far = bf16[2,352,128]{2,1,0:T(8,128)(2,1)S(1)} collective-permute-done((bf16[2,352,128]{2,1,0:T(8,128)(2,1)S(1)}, bf16[2,352,128]{2,1,0:T(8,128)(2,1)S(1)}, u32[]{:S(2)}, u32[]{:S(2)}) %collective-permute-start.35) | collective-permute-done | bytes 180256 | tf_op jit(solution)/shard_map/ppermute | solution.py:33
  104.6 0.8 collective-permute-start.38
  105.4 3.2 %collective-permute-done.41.far = bf16[2,352,128]{2,1,0:T(8,128)(2,1)S(1)} collective-permute-done((bf16[2,352,128]{2,1,0:T(8,128)(2,1)S(1)}, bf16[2,352,128]{2,1,0:T(8,128)(2,1)S(1)}, u32[]{:S(2)}, u32[]{:S(2)}) %collective-permute-start.41) | collective-permute-done | bytes 180256 | tf_op jit(solution)/shard_map/ppermute | solution.py:33
  108.6 1.2 collective-permute-done.45.got
  109.9 2.0 %collective-permute-start.42 = (bf16[4,352,128]{2,1,0:T(8,128)(2,1)S(1)}, bf16[4,352,128]{2,1,0:T(8,128)(2,1)S(1)}, u32[]{:S(2)}, u32[]{:S(2)}) collective-permute-start(bf16[4,352,128]{2,1,0:T(8,128)(2,1)S(1)} %join.4.after.refs_4_), channel_id=1, source_target_pairs={{0,4},{4,0},{8,12},{12,8},{1,5},{5,1},{9,13},{13,9},{2,6},{6,2},{1... | collective-permute-start | bytes 1081352 | tf_op jit(solution)/shard_map/ppermute | solution.py:33
  111.9 4.0 %collective-permute-done.46.far = bf16[2,224,128]{2,1,0:T(8,128)(2,1)S(1)} collective-permute-done((bf16[2,224,128]{2,1,0:T(8,128)(2,1)S(1)}, bf16[2,224,128]{2,1,0:T(8,128)(2,1)S(1)}, u32[]{:S(2)}, u32[]{:S(2)}) %collective-permute-start.46) | collective-permute-done | bytes 114720 | tf_op jit(solution)/shard_map/ppermute | solution.py:33
  115.9 1.5 %collective-permute-start.47 = (bf16[4,224,128]{2,1,0:T(8,128)(2,1)S(1)}, bf16[4,224,128]{2,1,0:T(8,128)(2,1)S(1)}, u32[]{:S(2)}, u32[]{:S(2)}) collective-permute-start(bf16[4,224,128]{2,1,0:T(8,128)(2,1)S(1)} %join.5.refs_8_), channel_id=1, source_target_pairs={{0,2},{2,0},{1,3},{3,1},{4,6},{6,4},{5,7},{7,5},{8,10},{10,8},{9,1... | collective-permute-start | bytes 688136 | tf_op jit(solution)/shard_map/ppermute | solution.py:33
  117.4 2.4 %collective-permute-done.42.refs_5_ = bf16[4,352,128]{2,1,0:T(8,128)(2,1)S(1)} collective-permute-done((bf16[4,352,128]{2,1,0:T(8,128)(2,1)S(1)}, bf16[4,352,128]{2,1,0:T(8,128)(2,1)S(1)}, u32[]{:S(2)}, u32[]{:S(2)}) %collective-permute-start.42) | collective-permute-done | bytes 360480 | tf_op jit(solution)/shard_map/ppermute | solution.py:33
  120.2 1.7 %collective-permute-done.47.refs_9_ = bf16[4,224,128]{2,1,0:T(8,128)(2,1)S(1)} collective-permute-done((bf16[4,224,128]{2,1,0:T(8,128)(2,1)S(1)}, bf16[4,224,128]{2,1,0:T(8,128)(2,1)S(1)}, u32[]{:S(2)}, u32[]{:S(2)}) %collective-permute-start.47) | collective-permute-done | bytes 229408 | tf_op jit(solution)/shard_map/ppermute | solution.py:33
  122.2 1.2 collective-permute-done.49.refs_11_
  123.5 3.6 %place.1 = (bf16[768,1024]{1,0:T(8,128)(2,1)}, bf16[768,1024]{1,0:T(8,128)(2,1)}, bf16[153,1024]{1,0:T(8,128)(2,1)}, bf16[153,1024]{1,0:T(8,128)(2,1)}) custom-call(s32[3]{0:T(128)S(1)} %copy-done.1, bf16[4,352,128]{2,1,0:T(8,128)(2,1)S(1)} %join.3.after.later.refs_0_, bf16[4,352,128]{2,1,0:T(8,128)(2,1)S(1)} %collective-permute-done.38.later.refs_1_, ...), custom_call_target="tpu_custom_call" | custom-call | flops 10000000000 | bytes 10000000 | tf_op jit(solution)/shard_map/place/pallas_call | solution.py:46
  (127 shorter events, 14.7 us)
Async XLA Ops:
  3.4 8.8 %collective-permute-start.1 = (s32[2,64]{1,0:T(2,128)S(1)}, s32[2,64]{1,0:T(2,128)S(1)}, u32[]{:S(2)}, u32[]{:S(2)}) collective-permute-start(s32[2,64]{1,0:T(2,128)S(1)} %get-tuple-element.48), channel_id=1, source_target_pairs={{0,8},{2,10},{4,12},{6,14},{8,0},{10,2},{12,4},{14,6},{1,9},{3,11}... | collective-permute-start | bytes 1544 | tf_op jit(solution)/shard_map/ppermute | solution.py:272
  7.3 9.8 %collective-permute-start.7 = (s32[2,64]{1,0:T(2,128)S(1)}, s32[2,64]{1,0:T(2,128)S(1)}, u32[]{:S(2)}, u32[]{:S(2)}) collective-permute-start(s32[2,64]{1,0:T(2,128)S(1)} %get-tuple-element.55), channel_id=1, source_target_pairs={{0,10},{2,8},{4,14},{6,12},{8,2},{10,0},{12,6},{14,4},{1,11},{3,9}... | collective-permute-start | bytes 1544 | tf_op jit(solution)/shard_map/ppermute | solution.py:272
  8.5 10.0 %collective-permute-start.6 = (s32[2,64]{1,0:T(2,128)S(1)}, s32[2,64]{1,0:T(2,128)S(1)}, u32[]{:S(2)}, u32[]{:S(2)}) collective-permute-start(s32[2,64]{1,0:T(2,128)S(1)} %get-tuple-element.54), channel_id=1, source_target_pairs={{0,12},{2,14},{4,8},{6,10},{8,4},{10,6},{12,0},{14,2},{1,13},{3,15... | collective-permute-start | bytes 1544 | tf_op jit(solution)/shard_map/ppermute | solution.py:272
  12.1 7.5 %collective-permute-start.5 = (s32[2,64]{1,0:T(2,128)S(1)}, s32[2,64]{1,0:T(2,128)S(1)}, u32[]{:S(2)}, u32[]{:S(2)}) collective-permute-start(s32[2,64]{1,0:T(2,128)S(1)} %get-tuple-element.53), channel_id=1, source_target_pairs={{0,14},{2,12},{4,10},{6,8},{8,6},{10,4},{12,2},{14,0},{1,15},{3,13... | collective-permute-start | bytes 1544 | tf_op jit(solution)/shard_map/ppermute | solution.py:272
  12.6 25.1 %collective-permute-start.14 = (bf16[128,768]{1,0:T(8,128)(2,1)S(1)}, bf16[128,768]{1,0:T(8,128)(2,1)S(1)}, u32[]{:S(2)}, u32[]{:S(2)}) collective-permute-start(bf16[128,768]{1,0:T(8,128)(2,1)S(1)} %serve.8.after), channel_id=1, source_target_pairs={{0,8},{2,10},{4,12},{6,14},{8,0},{10,2},{12,4},{14,6},{1,9},{3,11}... | collective-permute-start | bytes 589832 | tf_op jit(solution)/shard_map/ppermute | solution.py:272
  13.7 10.3 %collective-permute-start.4 = (s32[2,64]{1,0:T(2,128)S(1)}, s32[2,64]{1,0:T(2,128)S(1)}, u32[]{:S(2)}, u32[]{:S(2)}) collective-permute-start(s32[2,64]{1,0:T(2,128)S(1)} %get-tuple-element.52), channel_id=1, source_target_pairs={{0,4},{2,6},{4,0},{6,2},{8,12},{10,14},{12,8},{14,10},{1,5},{3,7},... | collective-permute-start | bytes 1544 | tf_op jit(solution)/shard_map/ppermute | solution.py:272
  17.1 8.6 %collective-permute-start.3 = (s32[2,64]{1,0:T(2,128)S(1)}, s32[2,64]{1,0:T(2,128)S(1)}, u32[]{:S(2)}, u32[]{:S(2)}) collective-permute-start(s32[2,64]{1,0:T(2,128)S(1)} %get-tuple-element.51), channel_id=1, source_target_pairs={{0,6},{2,4},{4,2},{6,0},{8,14},{10,12},{12,10},{14,8},{1,7},{3,5},... | collective-permute-start | bytes 1544 | tf_op jit(solution)/shard_map/ppermute | solution.py:272
  18.6 24.3 %collective-permute-start.13 = (bf16[128,768]{1,0:T(8,128)(2,1)S(1)}, bf16[128,768]{1,0:T(8,128)(2,1)S(1)}, u32[]{:S(2)}, u32[]{:S(2)}) collective-permute-start(bf16[128,768]{1,0:T(8,128)(2,1)S(1)} %serve.9.after), channel_id=1, source_target_pairs={{0,10},{2,8},{4,14},{6,12},{8,2},{10,0},{12,6},{14,4},{1,11},{3,9}... | collective-permute-start | bytes 589832 | tf_op jit(solution)/shard_map/ppermute | solution.py:272
  19.6 23.7 %collective-permute-start.12 = (bf16[128,768]{1,0:T(8,128)(2,1)S(1)}, bf16[128,768]{1,0:T(8,128)(2,1)S(1)}, u32[]{:S(2)}, u32[]{:S(2)}) collective-permute-start(bf16[128,768]{1,0:T(8,128)(2,1)S(1)} %serve.10.after), channel_id=1, source_target_pairs={{0,12},{2,14},{4,8},{6,10},{8,4},{10,6},{12,0},{14,2},{1,13},{3,15... | collective-permute-start | bytes 589832 | tf_op jit(solution)/shard_map/ppermute | solution.py:272
  24.0 19.4 %collective-permute-start.11 = (bf16[128,768]{1,0:T(8,128)(2,1)S(1)}, bf16[128,768]{1,0:T(8,128)(2,1)S(1)}, u32[]{:S(2)}, u32[]{:S(2)}) collective-permute-start(bf16[128,768]{1,0:T(8,128)(2,1)S(1)} %serve.11.after), channel_id=1, source_target_pairs={{0,14},{2,12},{4,10},{6,8},{8,6},{10,4},{12,2},{14,0},{1,15},{3,13... | collective-permute-start | bytes 589832 | tf_op jit(solution)/shard_map/ppermute | solution.py:272
  25.8 8.0 %collective-permute-start.2 = (s32[2,64]{1,0:T(2,128)S(1)}, s32[2,64]{1,0:T(2,128)S(1)}, u32[]{:S(2)}, u32[]{:S(2)}) collective-permute-start(s32[2,64]{1,0:T(2,128)S(1)} %get-tuple-element.50), channel_id=1, source_target_pairs={{0,2},{2,0},{4,6},{6,4},{8,10},{10,8},{12,14},{14,12},{1,3},{3,1},... | collective-permute-start | bytes 1544 | tf_op jit(solution)/shard_map/ppermute | solution.py:272
  33.8 11.3 %collective-permute-start.10 = (bf16[128,768]{1,0:T(8,128)(2,1)S(1)}, bf16[128,768]{1,0:T(8,128)(2,1)S(1)}, u32[]{:S(2)}, u32[]{:S(2)}) collective-permute-start(bf16[128,768]{1,0:T(8,128)(2,1)S(1)} %serve.12.after), channel_id=1, source_target_pairs={{0,4},{2,6},{4,0},{6,2},{8,12},{10,14},{12,8},{14,10},{1,5},{3,7},... | collective-permute-start | bytes 589832 | tf_op jit(solution)/shard_map/ppermute | solution.py:272
  37.7 12.5 %collective-permute-start.9 = (bf16[128,768]{1,0:T(8,128)(2,1)S(1)}, bf16[128,768]{1,0:T(8,128)(2,1)S(1)}, u32[]{:S(2)}, u32[]{:S(2)}) collective-permute-start(bf16[128,768]{1,0:T(8,128)(2,1)S(1)} %serve.13.done), channel_id=1, source_target_pairs={{0,6},{2,4},{4,2},{6,0},{8,14},{10,12},{12,10},{14,8},{1,7},{3,5},... | collective-permute-start | bytes 589832 | tf_op jit(solution)/shard_map/ppermute | solution.py:272
  42.8 9.4 %collective-permute-start.8 = (bf16[128,768]{1,0:T(8,128)(2,1)S(1)}, bf16[128,768]{1,0:T(8,128)(2,1)S(1)}, u32[]{:S(2)}, u32[]{:S(2)}) collective-permute-start(bf16[128,768]{1,0:T(8,128)(2,1)S(1)} %serve.14.after), channel_id=1, source_target_pairs={{0,2},{2,0},{4,6},{6,4},{8,10},{10,8},{12,14},{14,12},{1,3},{3,1},... | collective-permute-start | bytes 589832 | tf_op jit(solution)/shard_map/ppermute | solution.py:272
  43.4 8.9 %collective-permute-start.15 = (bf16[128,768]{1,0:T(8,128)(2,1)S(1)}, bf16[128,768]{1,0:T(8,128)(2,1)S(1)}, u32[]{:S(2)}, u32[]{:S(2)}) collective-permute-start(bf16[128,768]{1,0:T(8,128)(2,1)S(1)} %serve.15.after.refs_0_), channel_id=1, source_target_pairs={{0,1},{1,0},{2,3},{3,2},{4,5},{5,4},{6,7},{7,6},{8,9},{9,8},{10,11... | collective-permute-start | bytes 589832 | tf_op jit(solution)/shard_map/ppermute | solution.py:33
  43.4 9.5 %collective-permute-start.21 = (bf16[128,768]{1,0:T(8,128)(2,1)S(1)}, bf16[128,768]{1,0:T(8,128)(2,1)S(1)}, u32[]{:S(2)}, u32[]{:S(2)}) collective-permute-start(bf16[128,768]{1,0:T(8,128)(2,1)S(1)} %land.9.after.refs_6_), channel_id=1, source_target_pairs={{0,1},{1,0},{2,3},{3,2},{4,5},{5,4},{6,7},{7,6},{8,9},{9,8},{10,11... | collective-permute-start | bytes 589832 | tf_op jit(solution)/shard_map/ppermute | solution.py:33
  45.1 7.6 %collective-permute-start.22 = (bf16[128,768]{1,0:T(8,128)(2,1)S(1)}, bf16[128,768]{1,0:T(8,128)(2,1)S(1)}, u32[]{:S(2)}, u32[]{:S(2)}) collective-permute-start(bf16[128,768]{1,0:T(8,128)(2,1)S(1)} %land.10.after.refs_7_), channel_id=1, source_target_pairs={{0,1},{1,0},{2,3},{3,2},{4,5},{5,4},{6,7},{7,6},{8,9},{9,8},{10,11... | collective-permute-start | bytes 589832 | tf_op jit(solution)/shard_map/ppermute | solution.py:33
  50.3 3.0 %collective-permute-start.20 = (bf16[128,768]{1,0:T(8,128)(2,1)S(1)}, bf16[128,768]{1,0:T(8,128)(2,1)S(1)}, u32[]{:S(2)}, u32[]{:S(2)}) collective-permute-start(bf16[128,768]{1,0:T(8,128)(2,1)S(1)} %land.8.after.refs_5_), channel_id=1, source_target_pairs={{0,1},{1,0},{2,3},{3,2},{4,5},{5,4},{6,7},{7,6},{8,9},{9,8},{10,11... | collective-permute-start | bytes 589832 | tf_op jit(solution)/shard_map/ppermute | solution.py:33
  52.3 2.0 %collective-permute-start.18 = (bf16[128,768]{1,0:T(8,128)(2,1)S(1)}, bf16[128,768]{1,0:T(8,128)(2,1)S(1)}, u32[]{:S(2)}, u32[]{:S(2)}) collective-permute-start(bf16[128,768]{1,0:T(8,128)(2,1)S(1)} %land.12.after.refs_3_), channel_id=1, source_target_pairs={{0,1},{1,0},{2,3},{3,2},{4,5},{5,4},{6,7},{7,6},{8,9},{9,8},{10,11... | collective-permute-start | bytes 589832 | tf_op jit(solution)/shard_map/ppermute | solution.py:33
  52.8 1.5 %collective-permute-start.16 = (bf16[128,768]{1,0:T(8,128)(2,1)S(1)}, bf16[128,768]{1,0:T(8,128)(2,1)S(1)}, u32[]{:S(2)}, u32[]{:S(2)}) collective-permute-start(bf16[128,768]{1,0:T(8,128)(2,1)S(1)} %land.13.refs_1_.refs_18_), channel_id=1, source_target_pairs={{0,1},{1,0},{2,3},{3,2},{4,5},{5,4},{6,7},{7,6},{8,9},{9,8},{10,11... | collective-permute-start | bytes 589832 | tf_op jit(solution)/shard_map/ppermute | solution.py:33
  52.9 1.7 %collective-permute-start.17 = (bf16[128,768]{1,0:T(8,128)(2,1)S(1)}, bf16[128,768]{1,0:T(8,128)(2,1)S(1)}, u32[]{:S(2)}, u32[]{:S(2)}) collective-permute-start(bf16[128,768]{1,0:T(8,128)(2,1)S(1)} %land.11.after.refs_2_), channel_id=1, source_target_pairs={{0,1},{1,0},{2,3},{3,2},{4,5},{5,4},{6,7},{7,6},{8,9},{9,8},{10,11... | collective-permute-start | bytes 589832 | tf_op jit(solution)/shard_map/ppermute | solution.py:33
  53.3 24.1 %collective-permute-start.28 = (bf16[256,160]{1,0:T(8,128)(2,1)S(1)}, bf16[256,160]{1,0:T(8,128)(2,1)S(1)}, u32[]{:S(2)}, u32[]{:S(2)}) collective-permute-start(bf16[256,160]{1,0:T(8,128)(2,1)S(1)} %get-tuple-element.72.cot), channel_id=1, source_target_pairs={{0,1},{1,0},{2,3},{3,2},{4,5},{5,4},{6,7},{7,6},{8,9},{9,8},{10,11... | collective-permute-start | bytes 245768 | tf_op jit(solution)/shard_map/ppermute | solution.py:33
  56.5 4.6 %collective-permute-start.23 = (bf16[512,768]{1,0:T(8,128)(2,1)S(1)}, bf16[512,768]{1,0:T(8,128)(2,1)S(1)}, u32[]{:S(2)}, u32[]{:S(2)}) collective-permute-start(bf16[512,768]{1,0:T(8,128)(2,1)S(1)} %get-tuple-element.59.other), channel_id=1, source_target_pairs={{0,1},{1,0},{2,3},{3,2},{4,5},{5,4},{6,7},{7,6},{8,9},{9,8},{10,11... | collective-permute-start | bytes 2359304 | tf_op jit(solution)/shard_map/ppermute | solution.py:33
  58.6 2.4 %collective-permute-start.25 = (bf16[512,512]{1,0:T(8,128)(2,1)S(1)}, bf16[512,512]{1,0:T(8,128)(2,1)S(1)}, u32[]{:S(2)}, u32[]{:S(2)}) collective-permute-start(bf16[512,512]{1,0:T(8,128)(2,1)S(1)} %get-tuple-element.61.after.grad.far), channel_id=1, source_target_pairs={{0,1},{1,0},{2,3},{3,2},{4,5},{5,4},{6,7},{7,6},{8,9},{9,8},{10,11... | collective-permute-start | bytes 1572872 | tf_op jit(solution)/shard_map/ppermute | solution.py:33
  60.7 2.1 %collective-permute-start.24 = (bf16[512,512]{1,0:T(8,128)(2,1)S(1)}, bf16[512,512]{1,0:T(8,128)(2,1)S(1)}, u32[]{:S(2)}, u32[]{:S(2)}) collective-permute-start(bf16[512,512]{1,0:T(8,128)(2,1)S(1)} %get-tuple-element.66.after.grad), channel_id=1, source_target_pairs={{0,1},{1,0},{2,3},{3,2},{4,5},{5,4},{6,7},{7,6},{8,9},{9,8},{10,11... | collective-permute-start | bytes 1572872 | tf_op jit(solution)/shard_map/ppermute | solution.py:33
  62.2 10.7 %collective-permute-start.26 = (bf16[4,352,128]{2,1,0:T(8,128)(2,1)S(1)}, bf16[4,352,128]{2,1,0:T(8,128)(2,1)S(1)}, u32[]{:S(2)}, u32[]{:S(2)}) collective-permute-start(bf16[4,352,128]{2,1,0:T(8,128)(2,1)S(1)} %send_across.1.after), channel_id=1, source_target_pairs={{0,2},{2,0},{1,3},{3,1},{4,6},{6,4},{5,7},{7,5},{8,10},{10,8},{9,1... | collective-permute-start | bytes 1081352 | tf_op jit(solution)/shard_map/ppermute | solution.py:33
  64.8 10.5 %collective-permute-start.31 = (bf16[4,352,128]{2,1,0:T(8,128)(2,1)S(1)}, bf16[4,352,128]{2,1,0:T(8,128)(2,1)S(1)}, u32[]{:S(2)}, u32[]{:S(2)}) collective-permute-start(bf16[4,352,128]{2,1,0:T(8,128)(2,1)S(1)} %send_along.1.after), channel_id=1, source_target_pairs={{0,4},{4,0},{8,12},{12,8},{1,5},{5,1},{9,13},{13,9},{2,6},{6,2},{1... | collective-permute-start | bytes 1081352 | tf_op jit(solution)/shard_map/ppermute | solution.py:33
  70.5 6.9 %collective-permute-start.29 = (bf16[256,512]{1,0:T(8,128)(2,1)S(1)}, bf16[256,512]{1,0:T(8,128)(2,1)S(1)}, u32[]{:S(2)}, u32[]{:S(2)}) collective-permute-start(bf16[256,512]{1,0:T(8,128)(2,1)S(1)} %get-tuple-element.74), channel_id=1, source_target_pairs={{0,1},{1,0},{2,3},{3,2},{4,5},{5,4},{6,7},{7,6},{8,9},{9,8},{10,11... | collective-permute-start | bytes 786440 | tf_op jit(solution)/shard_map/ppermute | solution.py:33
  70.5 6.9 %collective-permute-start.30 = (bf16[256,512]{1,0:T(8,128)(2,1)S(1)}, bf16[256,512]{1,0:T(8,128)(2,1)S(1)}, u32[]{:S(2)}, u32[]{:S(2)}) collective-permute-start(bf16[256,512]{1,0:T(8,128)(2,1)S(1)} %get-tuple-element.76), channel_id=1, source_target_pairs={{0,1},{1,0},{2,3},{3,2},{4,5},{5,4},{6,7},{7,6},{8,9},{9,8},{10,11... | collective-permute-start | bytes 786440 | tf_op jit(solution)/shard_map/ppermute | solution.py:33
  73.8 8.6 %collective-permute-start.27 = (bf16[2,352,128]{2,1,0:T(8,128)(2,1)S(1)}, bf16[2,352,128]{2,1,0:T(8,128)(2,1)S(1)}, u32[]{:S(2)}, u32[]{:S(2)}) collective-permute-start(bf16[2,352,128]{2,1,0:T(8,128)(2,1)S(1)} %get-tuple-element.70.after), channel_id=1, source_target_pairs={{0,4},{4,0},{8,12},{12,8},{1,5},{5,1},{9,13},{13,9},{2,6},{6,2},{1... | collective-permute-start | bytes 540680 | tf_op jit(solution)/shard_map/ppermute | solution.py:33
  75.4 15.6 %collective-permute-start.34 = (bf16[2,352,128]{2,1,0:T(8,128)(2,1)S(1)}, bf16[2,352,128]{2,1,0:T(8,128)(2,1)S(1)}, u32[]{:S(2)}, u32[]{:S(2)}) collective-permute-start(bf16[2,352,128]{2,1,0:T(8,128)(2,1)S(1)} %get-tuple-element.77.after), channel_id=1, source_target_pairs={{0,8},{4,12},{8,0},{12,4},{1,9},{5,13},{9,1},{13,5},{2,10},{6,14},... | collective-permute-start | bytes 540680 | tf_op jit(solution)/shard_map/ppermute | solution.py:33
  79.3 13.2 %collective-permute-start.33 = (bf16[4,224,128]{2,1,0:T(8,128)(2,1)S(1)}, bf16[4,224,128]{2,1,0:T(8,128)(2,1)S(1)}, u32[]{:S(2)}, u32[]{:S(2)}) collective-permute-start(bf16[4,224,128]{2,1,0:T(8,128)(2,1)S(1)} %get-tuple-element.79), channel_id=1, source_target_pairs={{0,2},{2,0},{1,3},{3,1},{4,6},{6,4},{5,7},{7,5},{8,10},{10,8},{9,1... | collective-permute-start | bytes 688136 | tf_op jit(solution)/shard_map/ppermute | solution.py:33
  82.4 11.4 %collective-permute-start.32 = (bf16[2,352,128]{2,1,0:T(8,128)(2,1)S(1)}, bf16[2,352,128]{2,1,0:T(8,128)(2,1)S(1)}, u32[]{:S(2)}, u32[]{:S(2)}) collective-permute-start(bf16[2,352,128]{2,1,0:T(8,128)(2,1)S(1)} %add.19.after.mine), channel_id=1, source_target_pairs={{0,8},{4,12},{8,0},{12,4},{1,9},{5,13},{9,1},{13,5},{2,10},{6,14},... | collective-permute-start | bytes 540680 | tf_op jit(solution)/shard_map/ppermute | solution.py:33
  91.1 5.6 %collective-permute-start.37 = (bf16[2,352,128]{2,1,0:T(8,128)(2,1)S(1)}, bf16[2,352,128]{2,1,0:T(8,128)(2,1)S(1)}, u32[]{:S(2)}, u32[]{:S(2)}) collective-permute-start(bf16[2,352,128]{2,1,0:T(8,128)(2,1)S(1)} %add.20.after.mine), channel_id=1, source_target_pairs={{0,2},{2,0},{1,3},{3,1},{4,6},{6,4},{5,7},{7,5},{8,10},{10,8},{9,1... | collective-permute-start | bytes 540680 | tf_op jit(solution)/shard_map/ppermute | solution.py:33
  92.5 9.7 %collective-permute-start.36 = (bf16[2,224,128]{2,1,0:T(8,128)(2,1)S(1)}, bf16[2,224,128]{2,1,0:T(8,128)(2,1)S(1)}, u32[]{:S(2)}, u32[]{:S(2)}) collective-permute-start(bf16[2,224,128]{2,1,0:T(8,128)(2,1)S(1)} %get-tuple-element.81.after), channel_id=1, source_target_pairs={{0,4},{4,0},{8,12},{12,8},{1,5},{5,1},{9,13},{13,9},{2,6},{6,2},{1... | collective-permute-start | bytes 344072 | tf_op jit(solution)/shard_map/ppermute | solution.py:33
  93.9 10.6 %collective-permute-start.35 = (bf16[2,352,128]{2,1,0:T(8,128)(2,1)S(1)}, bf16[2,352,128]{2,1,0:T(8,128)(2,1)S(1)}, u32[]{:S(2)}, u32[]{:S(2)}) collective-permute-start(bf16[2,352,128]{2,1,0:T(8,128)(2,1)S(1)} %meet.3.after.near), channel_id=1, source_target_pairs={{0,4},{4,0},{8,12},{12,8},{1,5},{5,1},{9,13},{13,9},{2,6},{6,2},{1... | collective-permute-start | bytes 540680 | tf_op jit(solution)/shard_map/ppermute | solution.py:33
  96.7 11.8 %collective-permute-start.41 = (bf16[2,352,128]{2,1,0:T(8,128)(2,1)S(1)}, bf16[2,352,128]{2,1,0:T(8,128)(2,1)S(1)}, u32[]{:S(2)}, u32[]{:S(2)}) collective-permute-start(bf16[2,352,128]{2,1,0:T(8,128)(2,1)S(1)} %meet.4.after.near), channel_id=1, source_target_pairs={{0,8},{4,12},{8,0},{12,4},{1,9},{5,13},{9,1},{13,5},{2,10},{6,14},... | collective-permute-start | bytes 540680 | tf_op jit(solution)/shard_map/ppermute | solution.py:33
  102.2 7.5 %collective-permute-start.45 = (bf16[2,224,128]{2,1,0:T(8,128)(2,1)S(1)}, bf16[2,224,128]{2,1,0:T(8,128)(2,1)S(1)}, u32[]{:S(2)}, u32[]{:S(2)}) collective-permute-start(bf16[2,224,128]{2,1,0:T(8,128)(2,1)S(1)} %add.21.after.later.mine), channel_id=1, source_target_pairs={{0,8},{4,12},{8,0},{12,4},{1,9},{5,13},{9,1},{13,5},{2,10},{6,14},... | collective-permute-start | bytes 344072 | tf_op jit(solution)/shard_map/ppermute | solution.py:33
  104.6 11.3 %collective-permute-start.38 = (bf16[4,352,128]{2,1,0:T(8,128)(2,1)S(1)}, bf16[4,352,128]{2,1,0:T(8,128)(2,1)S(1)}, u32[]{:S(2)}, u32[]{:S(2)}) collective-permute-start(bf16[4,352,128]{2,1,0:T(8,128)(2,1)S(1)} %join.3.after.later.refs_0_), channel_id=1, source_target_pairs={{0,2},{2,0},{1,3},{3,1},{4,6},{6,4},{5,7},{7,5},{8,10},{10,8},{9,1... | collective-permute-start | bytes 1081352 | tf_op jit(solution)/shard_map/ppermute | solution.py:33
  109.8 6.1 %collective-permute-start.46 = (bf16[2,224,128]{2,1,0:T(8,128)(2,1)S(1)}, bf16[2,224,128]{2,1,0:T(8,128)(2,1)S(1)}, u32[]{:S(2)}, u32[]{:S(2)}) collective-permute-start(bf16[2,224,128]{2,1,0:T(8,128)(2,1)S(1)} %meet.5.near.after), channel_id=1, source_target_pairs={{0,4},{4,0},{8,12},{12,8},{1,5},{5,1},{9,13},{13,9},{2,6},{6,2},{1... | collective-permute-start | bytes 344072 | tf_op jit(solution)/shard_map/ppermute | solution.py:33
  109.9 9.8 %collective-permute-start.42 = (bf16[4,352,128]{2,1,0:T(8,128)(2,1)S(1)}, bf16[4,352,128]{2,1,0:T(8,128)(2,1)S(1)}, u32[]{:S(2)}, u32[]{:S(2)}) collective-permute-start(bf16[4,352,128]{2,1,0:T(8,128)(2,1)S(1)} %join.4.after.refs_4_), channel_id=1, source_target_pairs={{0,4},{4,0},{8,12},{12,8},{1,5},{5,1},{9,13},{13,9},{2,6},{6,2},{1... | collective-permute-start | bytes 1081352 | tf_op jit(solution)/shard_map/ppermute | solution.py:33
  111.9 8.3 %collective-permute-start.43 = (bf16[4,352,128]{2,1,0:T(8,128)(2,1)S(1)}, bf16[4,352,128]{2,1,0:T(8,128)(2,1)S(1)}, u32[]{:S(2)}, u32[]{:S(2)}) collective-permute-start(bf16[4,352,128]{2,1,0:T(8,128)(2,1)S(1)} %join.4.after.refs_4_), channel_id=1, source_target_pairs={{0,1},{1,0},{2,3},{3,2},{4,5},{5,4},{6,7},{7,6},{8,9},{9,8},{10,11... | collective-permute-start | bytes 1081352 | tf_op jit(solution)/shard_map/ppermute | solution.py:33
  115.9 6.1 %collective-permute-start.47 = (bf16[4,224,128]{2,1,0:T(8,128)(2,1)S(1)}, bf16[4,224,128]{2,1,0:T(8,128)(2,1)S(1)}, u32[]{:S(2)}, u32[]{:S(2)}) collective-permute-start(bf16[4,224,128]{2,1,0:T(8,128)(2,1)S(1)} %join.5.refs_8_), channel_id=1, source_target_pairs={{0,2},{2,0},{1,3},{3,1},{4,6},{6,4},{5,7},{7,5},{8,10},{10,8},{9,1... | collective-permute-start | bytes 688136 | tf_op jit(solution)/shard_map/ppermute | solution.py:33
  117.4 4.6 %collective-permute-start.39 = (bf16[4,352,128]{2,1,0:T(8,128)(2,1)S(1)}, bf16[4,352,128]{2,1,0:T(8,128)(2,1)S(1)}, u32[]{:S(2)}, u32[]{:S(2)}) collective-permute-start(bf16[4,352,128]{2,1,0:T(8,128)(2,1)S(1)} %join.3.after.later.refs_0_), channel_id=1, source_target_pairs={{0,1},{1,0},{2,3},{3,2},{4,5},{5,4},{6,7},{7,6},{8,9},{9,8},{10,11... | collective-permute-start | bytes 1081352 | tf_op jit(solution)/shard_map/ppermute | solution.py:33
  119.7 2.5 %collective-permute-start.44 = (bf16[4,352,128]{2,1,0:T(8,128)(2,1)S(1)}, bf16[4,352,128]{2,1,0:T(8,128)(2,1)S(1)}, u32[]{:S(2)}, u32[]{:S(2)}) collective-permute-start(bf16[4,352,128]{2,1,0:T(8,128)(2,1)S(1)} %collective-permute-done.42.refs_5_), channel_id=1, source_target_pairs={{0,1},{1,0},{2,3},{3,2},{4,5},{5,4},{6,7},{7,6},{8,9},{9,8},{10,11... | collective-permute-start | bytes 1081352 | tf_op jit(solution)/shard_map/ppermute | solution.py:33
  119.7 2.5 %collective-permute-start.40 = (bf16[4,352,128]{2,1,0:T(8,128)(2,1)S(1)}, bf16[4,352,128]{2,1,0:T(8,128)(2,1)S(1)}, u32[]{:S(2)}, u32[]{:S(2)}) collective-permute-start(bf16[4,352,128]{2,1,0:T(8,128)(2,1)S(1)} %collective-permute-done.38.later.refs_1_), channel_id=1, source_target_pairs={{0,1},{1,0},{2,3},{3,2},{4,5},{5,4},{6,7},{7,6},{8,9},{9,8},{10,11... | collective-permute-start | bytes 1081352 | tf_op jit(solution)/shard_map/ppermute | solution.py:33
  120.2 2.0 %collective-permute-start.48 = (bf16[4,224,128]{2,1,0:T(8,128)(2,1)S(1)}, bf16[4,224,128]{2,1,0:T(8,128)(2,1)S(1)}, u32[]{:S(2)}, u32[]{:S(2)}) collective-permute-start(bf16[4,224,128]{2,1,0:T(8,128)(2,1)S(1)} %join.5.refs_8_), channel_id=1, source_target_pairs={{0,1},{1,0},{2,3},{3,2},{4,5},{5,4},{6,7},{7,6},{8,9},{9,8},{10,11... | collective-permute-start | bytes 688136 | tf_op jit(solution)/shard_map/ppermute | solution.py:33
  122.0 1.5 %collective-permute-start.49 = (bf16[4,224,128]{2,1,0:T(8,128)(2,1)S(1)}, bf16[4,224,128]{2,1,0:T(8,128)(2,1)S(1)}, u32[]{:S(2)}, u32[]{:S(2)}) collective-permute-start(bf16[4,224,128]{2,1,0:T(8,128)(2,1)S(1)} %collective-permute-done.47.refs_9_), channel_id=1, source_target_pairs={{0,1},{1,0},{2,3},{3,2},{4,5},{5,4},{6,7},{7,6},{8,9},{9,8},{10,11... | collective-permute-start | bytes 688136 | tf_op jit(solution)/shard_map/ppermute | solution.py:33
  (19 other events, 37.8 us)

commit v5 on v4

--- a/solution.py
+++ b/solution.py
@@ -8,10 +8,10 @@
 from jax.sharding import PartitionSpec as P
 
 LANES = 128
-GROUPS = ((4, 5, 6, 7), (2, 3, 1, 0))
+GROUPS = ((5, 4, 7, 6), (3, 1, 2, 0))
 ASK = 0
-BESIDE = 3
-LANDINGS = (0, 4, 5, 6, 7, 2, 3, 1)
+BESIDE = 1
+LANDINGS = (0, 5, 4, 7, 3, 6, 1, 2)
 CORE_STEP = ("sub", 2, 1)
 BLOCKS = 8
 TRAINERS = ("tr", "cache", "sub")

time: 127 us -> 126 us (level)
  waiting for transfers between devices: 54.8 us -> 51.6 us
    ppermute x14, waiting for transfers between devices: 16 us -> 11.9 us  [across_chips(): lax.ppermute(array, ('tr', 'cache'), [(i, i ^ distance) for i in range(ch...]
    ppermute x14, starting transfers between devices: 21.2 us -> 22.8 us  [across_chips(): lax.ppermute(array, ('tr', 'cache'), [(i, i ^ distance) for i in range(ch...]
where the time goes in v5:
time: 126 us; the launch traced here: 125 us
  waiting for transfers between devices  51.6 us (41%)
  starting transfers between devices  39.7 us (32%)
  Pallas kernels  30.7 us (24%)
  local copies, waits for them, and re-layouts  2.11 us (2%)
    ppermute x36, waiting for transfers between devices, swap(): return lax.ppermute(array, axis, [(i, i ^ distance) for i in range(size)])  39.7 us
    pallas_call x39, Pallas kernels, kernel_call(): pl.pallas_call(body, out_shape=[jax.ShapeDtypeStruct(*out) for out in out...  23.6 us
    ppermute x14, starting transfers between devices, across_chips(): lax.ppermute(array, ('tr', 'cache'), [(i, i ^ distance) for i in range(ch...  22.8 us
    ppermute x36, starting transfers between devices, swap(): return lax.ppermute(array, axis, [(i, i ^ distance) for i in range(size)])  16.9 us
    ppermute x14, waiting for transfers between devices, across_chips(): lax.ppermute(array, ('tr', 'cache'), [(i, i ^ distance) for i in range(ch...  11.9 us
    pallas_call x1, Pallas kernels, beside(): pl.pallas_call(beside_kernel, out_shape=[shape((middle, inputs), BF16), s...  7.01 us
  transfers between devices with their start and end apart: 50, of which 24 were waited for; matrix products, arithmetic and copies ran while one was open for 0% of the time, Pallas kernels for 21%

profile of v5, /device:TPU:0, one launch (start us, length us, event | category | flops | bytes accessed | tf_op | source)
XLA Modules:
  0.0 125.3 jit_solution(8656429790700237849)
XLA Ops:
  0.7 0.7 copy-done.12
  2.5 0.8 collective-permute-done.got
  3.4 4.9 %collective-permute-start.1 = (s32[2,64]{1,0:T(2,128)S(1)}, s32[2,64]{1,0:T(2,128)S(1)}, u32[]{:S(2)}, u32[]{:S(2)}) collective-permute-start(s32[2,64]{1,0:T(2,128)S(1)} %get-tuple-element.48), channel_id=1, source_target_pairs={{0,10},{2,8},{4,14},{6,12},{8,2},{10,0},{12,6},{14,4},{1,11},{3,9}... | collective-permute-start | bytes 1544 | tf_op jit(solution)/shard_map/ppermute | solution.py:272
  8.5 3.6 %collective-permute-start.6 = (s32[2,64]{1,0:T(2,128)S(1)}, s32[2,64]{1,0:T(2,128)S(1)}, u32[]{:S(2)}, u32[]{:S(2)}) collective-permute-start(s32[2,64]{1,0:T(2,128)S(1)} %get-tuple-element.54), channel_id=1, source_target_pairs={{0,14},{2,12},{4,10},{6,8},{8,6},{10,4},{12,2},{14,0},{1,15},{3,13... | collective-permute-start | bytes 1544 | tf_op jit(solution)/shard_map/ppermute | solution.py:272
  12.6 2.0 %collective-permute-start.13 = (bf16[128,768]{1,0:T(8,128)(2,1)S(1)}, bf16[128,768]{1,0:T(8,128)(2,1)S(1)}, u32[]{:S(2)}, u32[]{:S(2)}) collective-permute-start(bf16[128,768]{1,0:T(8,128)(2,1)S(1)} %serve.8.after), channel_id=1, source_target_pairs={{0,10},{2,8},{4,14},{6,12},{8,2},{10,0},{12,6},{14,4},{1,11},{3,9}... | collective-permute-start | bytes 589832 | tf_op jit(solution)/shard_map/ppermute | solution.py:272
  14.6 3.3 %collective-permute-start.4 = (s32[2,64]{1,0:T(2,128)S(1)}, s32[2,64]{1,0:T(2,128)S(1)}, u32[]{:S(2)}, u32[]{:S(2)}) collective-permute-start(s32[2,64]{1,0:T(2,128)S(1)} %get-tuple-element.52), channel_id=1, source_target_pairs={{0,6},{2,4},{4,2},{6,0},{8,14},{10,12},{12,10},{14,8},{1,7},{3,5},... | collective-permute-start | bytes 1544 | tf_op jit(solution)/shard_map/ppermute | solution.py:272
  18.0 1.5 %collective-permute-start.3 = (s32[2,64]{1,0:T(2,128)S(1)}, s32[2,64]{1,0:T(2,128)S(1)}, u32[]{:S(2)}, u32[]{:S(2)}) collective-permute-start(s32[2,64]{1,0:T(2,128)S(1)} %get-tuple-element.51), channel_id=1, source_target_pairs={{0,2},{2,0},{4,6},{6,4},{8,10},{10,8},{12,14},{14,12},{1,3},{3,1},... | collective-permute-start | bytes 1544 | tf_op jit(solution)/shard_map/ppermute | solution.py:272
  20.5 2.5 %collective-permute-start.11 = (bf16[128,768]{1,0:T(8,128)(2,1)S(1)}, bf16[128,768]{1,0:T(8,128)(2,1)S(1)}, u32[]{:S(2)}, u32[]{:S(2)}) collective-permute-start(bf16[128,768]{1,0:T(8,128)(2,1)S(1)} %serve.10.after), channel_id=1, source_target_pairs={{0,14},{2,12},{4,10},{6,8},{8,6},{10,4},{12,2},{14,0},{1,15},{3,13... | collective-permute-start | bytes 589832 | tf_op jit(solution)/shard_map/ppermute | solution.py:272
  23.5 1.5 %collective-permute-start.9 = (bf16[128,768]{1,0:T(8,128)(2,1)S(1)}, bf16[128,768]{1,0:T(8,128)(2,1)S(1)}, u32[]{:S(2)}, u32[]{:S(2)}) collective-permute-start(bf16[128,768]{1,0:T(8,128)(2,1)S(1)} %serve.11.after), channel_id=1, source_target_pairs={{0,12},{2,14},{4,8},{6,10},{8,4},{10,6},{12,0},{14,2},{1,13},{3,15... | collective-permute-start | bytes 589832 | tf_op jit(solution)/shard_map/ppermute | solution.py:272
  26.7 7.0 %beside.1 = (bf16[512,1024]{1,0:T(8,128)(2,1)S(1)}, bf16[256,512]{1,0:T(8,128)(2,1)S(1)}, f32[512,2]{1,0:T(8,128)S(1)}, f32[256,1]{1,0:T(8,128)S(1)}, bf16[512,1...) custom-call(s32[16]{0:T(128)S(1)} %copy-done.15, s32[10,512]{1,0:T(8,128)S(1)} %bitcast.18, s32[1,512]{1,0:T(1,128)S(1)} %bitcast.20, ...), custom_call_target="tpu_custom_call" | custom-call | flops 10000000000 | bytes 10000000 | tf_op jit(solution)/shard_map/beside/pallas_call | solution.py:367
  33.7 2.5 %collective-permute-start.10 = (bf16[128,768]{1,0:T(8,128)(2,1)S(1)}, bf16[128,768]{1,0:T(8,128)(2,1)S(1)}, u32[]{:S(2)}, u32[]{:S(2)}) collective-permute-start(bf16[128,768]{1,0:T(8,128)(2,1)S(1)} %serve.12.after), channel_id=1, source_target_pairs={{0,6},{2,4},{4,2},{6,0},{8,14},{10,12},{12,10},{14,8},{1,7},{3,5},... | collective-permute-start | bytes 589832 | tf_op jit(solution)/shard_map/ppermute | solution.py:272
  37.2 1.4 %collective-permute-done.13.rows = bf16[128,768]{1,0:T(8,128)(2,1)S(1)} collective-permute-done((bf16[128,768]{1,0:T(8,128)(2,1)S(1)}, bf16[128,768]{1,0:T(8,128)(2,1)S(1)}, u32[]{:S(2)}, u32[]{:S(2)}) %collective-permute-start.13) | collective-permute-done | bytes 196640 | tf_op jit(solution)/shard_map/ppermute | solution.py:272
  39.1 2.7 %collective-permute-done.12.rows = bf16[128,768]{1,0:T(8,128)(2,1)S(1)} collective-permute-done((bf16[128,768]{1,0:T(8,128)(2,1)S(1)}, bf16[128,768]{1,0:T(8,128)(2,1)S(1)}, u32[]{:S(2)}, u32[]{:S(2)}) %collective-permute-start.12) | collective-permute-done | bytes 196640 | tf_op jit(solution)/shard_map/ppermute | solution.py:272
  41.9 4.2 %collective-permute-done.10.rows = bf16[128,768]{1,0:T(8,128)(2,1)S(1)} collective-permute-done((bf16[128,768]{1,0:T(8,128)(2,1)S(1)}, bf16[128,768]{1,0:T(8,128)(2,1)S(1)}, u32[]{:S(2)}, u32[]{:S(2)}) %collective-permute-start.10) | collective-permute-done | bytes 196640 | tf_op jit(solution)/shard_map/ppermute | solution.py:272
  46.6 1.6 %collective-permute-done.8.rows = bf16[128,768]{1,0:T(8,128)(2,1)S(1)} collective-permute-done((bf16[128,768]{1,0:T(8,128)(2,1)S(1)}, bf16[128,768]{1,0:T(8,128)(2,1)S(1)}, u32[]{:S(2)}, u32[]{:S(2)}) %collective-permute-start.8) | collective-permute-done | bytes 196640 | tf_op jit(solution)/shard_map/ppermute | solution.py:272
  48.2 2.0 %collective-permute-done.14.rows = bf16[128,768]{1,0:T(8,128)(2,1)S(1)} collective-permute-done((bf16[128,768]{1,0:T(8,128)(2,1)S(1)}, bf16[128,768]{1,0:T(8,128)(2,1)S(1)}, u32[]{:S(2)}, u32[]{:S(2)}) %collective-permute-start.14) | collective-permute-done | bytes 196640 | tf_op jit(solution)/shard_map/ppermute | solution.py:272
  52.5 1.9 %mean.1 = (bf16[512,768]{1,0:T(8,128)(2,1)S(1)}, bf16[512,768]{1,0:T(8,128)(2,1)S(1)}) custom-call(s32[3]{0:T(128)S(1)} %copy-done.1, bf16[128,768]{1,0:T(8,128)(2,1)S(1)} %serve.15.after.refs_0_, bf16[128,768]{1,0:T(8,128)(2,1)S(1)} %land.12.after.refs_1_, bf16[128,768]{1,0:T(8,128)(2,1)S(1)} %land.13.refs_2_.refs_18_, ...), custom_call_target="tpu_custom_call" | custom-call | flops 10000000000 | bytes 10000000 | tf_op jit(solution)/shard_map/mean/pallas_call | solution.py:46
  54.7 1.8 %hidden.2 = (bf16[512,512]{1,0:T(8,128)(2,1)S(1)}, bf16[512,512]{1,0:T(8,128)(2,1)S(1)}) custom-call(s32[3]{0:T(128)S(1)} %copy-done.1, bf16[512,768]{1,0:T(8,128)(2,1)S(1)} %get-tuple-element.58.mine.after, bf16[512,768]{1,0:T(8,128)(2,1)S(1)} %get-tuple-element.59.other, bf16[768,1024]{1,0:T(8,128)(2,1)S(1)} %copy-done.3, bf16[768,1024]{1,0:T(8,128)(2,1)S(1)} %copy-done.4, ...), custom_call_target="tpu_custom_call" | custom-call | flops 10000000000 | bytes 10000000 | tf_op jit(solution)/shard_map/hidden/pallas_call | solution.py:46
  56.8 1.8 %hidden.3 = (bf16[512,512]{1,0:T(8,128)(2,1)S(1)}, bf16[512,512]{1,0:T(8,128)(2,1)S(1)}) custom-call(s32[3]{0:T(128)S(1)} %copy-done.1, bf16[512,768]{1,0:T(8,128)(2,1)S(1)} %get-tuple-element.58.mine.after, bf16[512,768]{1,0:T(8,128)(2,1)S(1)} %get-tuple-element.59.other, bf16[768,1024]{1,0:T(8,128)(2,1)S(1)} %copy-done.3, bf16[768,1024]{1,0:T(8,128)(2,1)S(1)} %copy-done.4, ...), custom_call_target="tpu_custom_call" | custom-call | flops 10000000000 | bytes 10000000 | tf_op jit(solution)/shard_map/hidden/pallas_call | solution.py:46
  58.9 1.1 send_across.1.after
  60.8 2.0 %send_along.1.after = bf16[4,352,128]{2,1,0:T(8,128)(2,1)S(1)} custom-call(s32[3]{0:T(128)S(1)} %copy-done.1, bf16[512,768]{1,0:T(8,128)(2,1)S(1)} %get-tuple-element.58.mine.after, bf16[512,768]{1,0:T(8,128)(2,1)S(1)} %collective-permute-done.23.got, bf16[512,512]{1,0:T(8,128)(2,1)S(1)} %get-tuple-element.66.after.grad, ...), custom_call_target="tpu_custom_call" | custom-call | flops 10000000000 | bytes 10000000 | tf_op jit(solution)/shard_map/send_along/pallas_call | solution.py:46
  62.8 1.2 collective-permute-start.31
  64.0 2.4 %keep.1 = (f32[4,352,128]{2,1,0:T(8,128)S(1)}, f32[4,352,128]{2,1,0:T(8,128)S(1)}) custom-call(s32[3]{0:T(128)S(1)} %copy-done.1, bf16[512,768]{1,0:T(8,128)(2,1)S(1)} %get-tuple-element.58.mine.after, bf16[512,768]{1,0:T(8,128)(2,1)S(1)} %collective-permute-done.23.got, bf16[512,512]{1,0:T(8,128)(2,1)S(1)} %get-tuple-element.66.after.grad, ...), custom_call_target="tpu_custom_call" | custom-call | flops 10000000000 | bytes 10000000 | tf_op jit(solution)/shard_map/keep/pallas_call | solution.py:46
  66.4 2.2 %top.1 = (f32[153,256]{1,0:T(8,128)}, bf16[256,512]{1,0:T(8,128)(2,1)S(1)}, bf16[256,512]{1,0:T(8,128)(2,1)S(1)}, bf16[256,512]{1,0:T(8,128)(2,1)S(1)}, bf16[256,512]{1,0:T(8,128)(2,1)S(1)}) custom-call(s32[3]{0:T(128)S(1)} %copy-done.1, bf16[512,512]{1,0:T(8,128)(2,1)S(1)} %get-tuple-element.62.near, bf16[512,512]{1,0:T(8,128)(2,1)S(1)} %get-tuple-element.63.far, ...), custom_call_target="tpu_custom_call" | custom-call | flops 10000000000 | bytes 10000000 | tf_op jit(solution)/shard_map/top/pallas_call | solution.py:46
  69.1 1.7 %collective-permute-done.26.got = bf16[4,352,128]{2,1,0:T(8,128)(2,1)S(1)} collective-permute-done((bf16[4,352,128]{2,1,0:T(8,128)(2,1)S(1)}, bf16[4,352,128]{2,1,0:T(8,128)(2,1)S(1)}, u32[]{:S(2)}, u32[]{:S(2)}) %collective-permute-start.26) | collective-permute-done | bytes 360480 | tf_op jit(solution)/shard_map/ppermute | solution.py:33
  70.8 0.9 copy-done.16
  71.7 1.2 collective-permute-start.27
  73.3 1.7 %collective-permute-start.34 = (bf16[2,352,128]{2,1,0:T(8,128)(2,1)S(1)}, bf16[2,352,128]{2,1,0:T(8,128)(2,1)S(1)}, u32[]{:S(2)}, u32[]{:S(2)}) collective-permute-start(bf16[2,352,128]{2,1,0:T(8,128)(2,1)S(1)} %get-tuple-element.77.after), channel_id=1, source_target_pairs={{0,8},{4,12},{8,0},{12,4},{1,9},{5,13},{9,1},{13,5},{2,10},{6,14},... | collective-permute-start | bytes 540680 | tf_op jit(solution)/shard_map/ppermute | solution.py:33
  75.0 1.9 %last.1 = (bf16[4,224,128]{2,1,0:T(8,128)(2,1)S(1)}, f32[4,224,128]{2,1,0:T(8,128)S(1)}) custom-call(s32[3]{0:T(128)S(1)} %copy-done.1, bf16[512,768]{1,0:T(8,128)(2,1)S(1)} %get-tuple-element.58.mine.after, bf16[512,768]{1,0:T(8,128)(2,1)S(1)} %collective-permute-done.23.got, bf16[512,512]{1,0:T(8,128)(2,1)S(1)} %get-tuple-element.66.after.grad, ...), custom_call_target="tpu_custom_call" | custom-call | flops 10000000000 | bytes 10000000 | tf_op jit(solution)/shard_map/last/pallas_call | solution.py:46
  76.9 1.1 collective-permute-start.33
  78.0 2.2 %collective-permute-done.27.got = bf16[2,352,128]{2,1,0:T(8,128)(2,1)S(1)} collective-permute-done((bf16[2,352,128]{2,1,0:T(8,128)(2,1)S(1)}, bf16[2,352,128]{2,1,0:T(8,128)(2,1)S(1)}, u32[]{:S(2)}, u32[]{:S(2)}) %collective-permute-start.27) | collective-permute-done | bytes 180256 | tf_op jit(solution)/shard_map/ppermute | solution.py:33
  80.7 8.3 %collective-permute-done.34.got = bf16[2,352,128]{2,1,0:T(8,128)(2,1)S(1)} collective-permute-done((bf16[2,352,128]{2,1,0:T(8,128)(2,1)S(1)}, bf16[2,352,128]{2,1,0:T(8,128)(2,1)S(1)}, u32[]{:S(2)}, u32[]{:S(2)}) %collective-permute-start.34) | collective-permute-done | bytes 180256 | tf_op jit(solution)/shard_map/ppermute | solution.py:33
  89.1 1.3 %collective-permute-start.37 = (bf16[2,352,128]{2,1,0:T(8,128)(2,1)S(1)}, bf16[2,352,128]{2,1,0:T(8,128)(2,1)S(1)}, u32[]{:S(2)}, u32[]{:S(2)}) collective-permute-start(bf16[2,352,128]{2,1,0:T(8,128)(2,1)S(1)} %add.20.after.mine), channel_id=1, source_target_pairs={{0,2},{2,0},{1,3},{3,1},{4,6},{6,4},{5,7},{7,5},{8,10},{10,8},{9,1... | collective-permute-start | bytes 540680 | tf_op jit(solution)/shard_map/ppermute | solution.py:33
  90.6 1.1 collective-permute-done.32.got
  91.7 1.0 collective-permute-start.35
  92.7 2.0 %collective-permute-done.37.got = bf16[2,352,128]{2,1,0:T(8,128)(2,1)S(1)} collective-permute-done((bf16[2,352,128]{2,1,0:T(8,128)(2,1)S(1)}, bf16[2,352,128]{2,1,0:T(8,128)(2,1)S(1)}, u32[]{:S(2)}, u32[]{:S(2)}) %collective-permute-start.37) | collective-permute-done | bytes 180256 | tf_op jit(solution)/shard_map/ppermute | solution.py:33
  94.8 4.7 %collective-permute-done.36.got = bf16[2,224,128]{2,1,0:T(8,128)(2,1)S(1)} collective-permute-done((bf16[2,224,128]{2,1,0:T(8,128)(2,1)S(1)}, bf16[2,224,128]{2,1,0:T(8,128)(2,1)S(1)}, u32[]{:S(2)}, u32[]{:S(2)}) %collective-permute-start.36) | collective-permute-done | bytes 114720 | tf_op jit(solution)/shard_map/ppermute | solution.py:33
  99.6 2.2 %collective-permute-done.35.far = bf16[2,352,128]{2,1,0:T(8,128)(2,1)S(1)} collective-permute-done((bf16[2,352,128]{2,1,0:T(8,128)(2,1)S(1)}, bf16[2,352,128]{2,1,0:T(8,128)(2,1)S(1)}, u32[]{:S(2)}, u32[]{:S(2)}) %collective-permute-start.35) | collective-permute-done | bytes 180256 | tf_op jit(solution)/shard_map/ppermute | solution.py:33
  101.9 0.9 collective-permute-start.38
  102.8 3.8 %collective-permute-done.41.far = bf16[2,352,128]{2,1,0:T(8,128)(2,1)S(1)} collective-permute-done((bf16[2,352,128]{2,1,0:T(8,128)(2,1)S(1)}, bf16[2,352,128]{2,1,0:T(8,128)(2,1)S(1)}, u32[]{:S(2)}, u32[]{:S(2)}) %collective-permute-start.41) | collective-permute-done | bytes 180256 | tf_op jit(solution)/shard_map/ppermute | solution.py:33
  106.6 1.2 collective-permute-done.45.got
  107.9 2.0 %collective-permute-start.42 = (bf16[4,352,128]{2,1,0:T(8,128)(2,1)S(1)}, bf16[4,352,128]{2,1,0:T(8,128)(2,1)S(1)}, u32[]{:S(2)}, u32[]{:S(2)}) collective-permute-start(bf16[4,352,128]{2,1,0:T(8,128)(2,1)S(1)} %join.4.after.refs_4_), channel_id=1, source_target_pairs={{0,4},{4,0},{8,12},{12,8},{1,5},{5,1},{9,13},{13,9},{2,6},{6,2},{1... | collective-permute-start | bytes 1081352 | tf_op jit(solution)/shard_map/ppermute | solution.py:33
  109.9 4.1 %collective-permute-done.46.far = bf16[2,224,128]{2,1,0:T(8,128)(2,1)S(1)} collective-permute-done((bf16[2,224,128]{2,1,0:T(8,128)(2,1)S(1)}, bf16[2,224,128]{2,1,0:T(8,128)(2,1)S(1)}, u32[]{:S(2)}, u32[]{:S(2)}) %collective-permute-start.46) | collective-permute-done | bytes 114720 | tf_op jit(solution)/shard_map/ppermute | solution.py:33
  114.0 1.0 collective-permute-start.47
  115.0 2.8 %collective-permute-done.42.refs_5_ = bf16[4,352,128]{2,1,0:T(8,128)(2,1)S(1)} collective-permute-done((bf16[4,352,128]{2,1,0:T(8,128)(2,1)S(1)}, bf16[4,352,128]{2,1,0:T(8,128)(2,1)S(1)}, u32[]{:S(2)}, u32[]{:S(2)}) %collective-permute-start.42) | collective-permute-done | bytes 360480 | tf_op jit(solution)/shard_map/ppermute | solution.py:33
  118.4 1.7 %collective-permute-done.47.refs_9_ = bf16[4,224,128]{2,1,0:T(8,128)(2,1)S(1)} collective-permute-done((bf16[4,224,128]{2,1,0:T(8,128)(2,1)S(1)}, bf16[4,224,128]{2,1,0:T(8,128)(2,1)S(1)}, u32[]{:S(2)}, u32[]{:S(2)}) %collective-permute-start.47) | collective-permute-done | bytes 229408 | tf_op jit(solution)/shard_map/ppermute | solution.py:33
  120.4 1.2 collective-permute-done.49.refs_11_
  121.6 3.6 %place.1 = (bf16[768,1024]{1,0:T(8,128)(2,1)}, bf16[768,1024]{1,0:T(8,128)(2,1)}, bf16[153,1024]{1,0:T(8,128)(2,1)}, bf16[153,1024]{1,0:T(8,128)(2,1)}) custom-call(s32[3]{0:T(128)S(1)} %copy-done.1, bf16[4,352,128]{2,1,0:T(8,128)(2,1)S(1)} %join.3.after.later.refs_0_, bf16[4,352,128]{2,1,0:T(8,128)(2,1)S(1)} %collective-permute-done.38.later.refs_1_, ...), custom_call_target="tpu_custom_call" | custom-call | flops 10000000000 | bytes 10000000 | tf_op jit(solution)/shard_map/place/pallas_call | solution.py:46
  (127 shorter events, 13.9 us)
Async XLA Ops:
  3.4 8.8 %collective-permute-start.1 = (s32[2,64]{1,0:T(2,128)S(1)}, s32[2,64]{1,0:T(2,128)S(1)}, u32[]{:S(2)}, u32[]{:S(2)}) collective-permute-start(s32[2,64]{1,0:T(2,128)S(1)} %get-tuple-element.48), channel_id=1, source_target_pairs={{0,10},{2,8},{4,14},{6,12},{8,2},{10,0},{12,6},{14,4},{1,11},{3,9}... | collective-permute-start | bytes 1544 | tf_op jit(solution)/shard_map/ppermute | solution.py:272
  8.2 9.8 %collective-permute-start.7 = (s32[2,64]{1,0:T(2,128)S(1)}, s32[2,64]{1,0:T(2,128)S(1)}, u32[]{:S(2)}, u32[]{:S(2)}) collective-permute-start(s32[2,64]{1,0:T(2,128)S(1)} %get-tuple-element.55), channel_id=1, source_target_pairs={{0,8},{2,10},{4,12},{6,14},{8,0},{10,2},{12,4},{14,6},{1,9},{3,11}... | collective-permute-start | bytes 1544 | tf_op jit(solution)/shard_map/ppermute | solution.py:272
  8.5 11.4 %collective-permute-start.6 = (s32[2,64]{1,0:T(2,128)S(1)}, s32[2,64]{1,0:T(2,128)S(1)}, u32[]{:S(2)}, u32[]{:S(2)}) collective-permute-start(s32[2,64]{1,0:T(2,128)S(1)} %get-tuple-element.54), channel_id=1, source_target_pairs={{0,14},{2,12},{4,10},{6,8},{8,6},{10,4},{12,2},{14,0},{1,15},{3,13... | collective-permute-start | bytes 1544 | tf_op jit(solution)/shard_map/ppermute | solution.py:272
  12.1 8.4 %collective-permute-start.5 = (s32[2,64]{1,0:T(2,128)S(1)}, s32[2,64]{1,0:T(2,128)S(1)}, u32[]{:S(2)}, u32[]{:S(2)}) collective-permute-start(s32[2,64]{1,0:T(2,128)S(1)} %get-tuple-element.53), channel_id=1, source_target_pairs={{0,12},{2,14},{4,8},{6,10},{8,4},{10,6},{12,0},{14,2},{1,13},{3,15... | collective-permute-start | bytes 1544 | tf_op jit(solution)/shard_map/ppermute | solution.py:272
  12.6 26.0 %collective-permute-start.13 = (bf16[128,768]{1,0:T(8,128)(2,1)S(1)}, bf16[128,768]{1,0:T(8,128)(2,1)S(1)}, u32[]{:S(2)}, u32[]{:S(2)}) collective-permute-start(bf16[128,768]{1,0:T(8,128)(2,1)S(1)} %serve.8.after), channel_id=1, source_target_pairs={{0,10},{2,8},{4,14},{6,12},{8,2},{10,0},{12,6},{14,4},{1,11},{3,9}... | collective-permute-start | bytes 589832 | tf_op jit(solution)/shard_map/ppermute | solution.py:272
  14.6 8.9 %collective-permute-start.4 = (s32[2,64]{1,0:T(2,128)S(1)}, s32[2,64]{1,0:T(2,128)S(1)}, u32[]{:S(2)}, u32[]{:S(2)}) collective-permute-start(s32[2,64]{1,0:T(2,128)S(1)} %get-tuple-element.52), channel_id=1, source_target_pairs={{0,6},{2,4},{4,2},{6,0},{8,14},{10,12},{12,10},{14,8},{1,7},{3,5},... | collective-permute-start | bytes 1544 | tf_op jit(solution)/shard_map/ppermute | solution.py:272
  18.0 7.6 %collective-permute-start.3 = (s32[2,64]{1,0:T(2,128)S(1)}, s32[2,64]{1,0:T(2,128)S(1)}, u32[]{:S(2)}, u32[]{:S(2)}) collective-permute-start(s32[2,64]{1,0:T(2,128)S(1)} %get-tuple-element.51), channel_id=1, source_target_pairs={{0,2},{2,0},{4,6},{6,4},{8,10},{10,8},{12,14},{14,12},{1,3},{3,1},... | collective-permute-start | bytes 1544 | tf_op jit(solution)/shard_map/ppermute | solution.py:272
  20.0 21.9 %collective-permute-start.12 = (bf16[128,768]{1,0:T(8,128)(2,1)S(1)}, bf16[128,768]{1,0:T(8,128)(2,1)S(1)}, u32[]{:S(2)}, u32[]{:S(2)}) collective-permute-start(bf16[128,768]{1,0:T(8,128)(2,1)S(1)} %serve.9.after), channel_id=1, source_target_pairs={{0,8},{2,10},{4,12},{6,14},{8,0},{10,2},{12,4},{14,6},{1,9},{3,11}... | collective-permute-start | bytes 589832 | tf_op jit(solution)/shard_map/ppermute | solution.py:272
  20.5 21.3 %collective-permute-start.11 = (bf16[128,768]{1,0:T(8,128)(2,1)S(1)}, bf16[128,768]{1,0:T(8,128)(2,1)S(1)}, u32[]{:S(2)}, u32[]{:S(2)}) collective-permute-start(bf16[128,768]{1,0:T(8,128)(2,1)S(1)} %serve.10.after), channel_id=1, source_target_pairs={{0,14},{2,12},{4,10},{6,8},{8,6},{10,4},{12,2},{14,0},{1,15},{3,13... | collective-permute-start | bytes 589832 | tf_op jit(solution)/shard_map/ppermute | solution.py:272
  23.5 22.6 %collective-permute-start.9 = (bf16[128,768]{1,0:T(8,128)(2,1)S(1)}, bf16[128,768]{1,0:T(8,128)(2,1)S(1)}, u32[]{:S(2)}, u32[]{:S(2)}) collective-permute-start(bf16[128,768]{1,0:T(8,128)(2,1)S(1)} %serve.11.after), channel_id=1, source_target_pairs={{0,12},{2,14},{4,8},{6,10},{8,4},{10,6},{12,0},{14,2},{1,13},{3,15... | collective-permute-start | bytes 589832 | tf_op jit(solution)/shard_map/ppermute | solution.py:272
  25.7 8.0 %collective-permute-start.2 = (s32[2,64]{1,0:T(2,128)S(1)}, s32[2,64]{1,0:T(2,128)S(1)}, u32[]{:S(2)}, u32[]{:S(2)}) collective-permute-start(s32[2,64]{1,0:T(2,128)S(1)} %get-tuple-element.50), channel_id=1, source_target_pairs={{0,4},{2,6},{4,0},{6,2},{8,12},{10,14},{12,8},{14,10},{1,5},{3,7},... | collective-permute-start | bytes 1544 | tf_op jit(solution)/shard_map/ppermute | solution.py:272
  33.7 12.4 %collective-permute-start.10 = (bf16[128,768]{1,0:T(8,128)(2,1)S(1)}, bf16[128,768]{1,0:T(8,128)(2,1)S(1)}, u32[]{:S(2)}, u32[]{:S(2)}) collective-permute-start(bf16[128,768]{1,0:T(8,128)(2,1)S(1)} %serve.12.after), channel_id=1, source_target_pairs={{0,6},{2,4},{4,2},{6,0},{8,14},{10,12},{12,10},{14,8},{1,7},{3,5},... | collective-permute-start | bytes 589832 | tf_op jit(solution)/shard_map/ppermute | solution.py:272
  38.7 9.5 %collective-permute-start.8 = (bf16[128,768]{1,0:T(8,128)(2,1)S(1)}, bf16[128,768]{1,0:T(8,128)(2,1)S(1)}, u32[]{:S(2)}, u32[]{:S(2)}) collective-permute-start(bf16[128,768]{1,0:T(8,128)(2,1)S(1)} %serve.13.done), channel_id=1, source_target_pairs={{0,2},{2,0},{4,6},{6,4},{8,10},{10,8},{12,14},{14,12},{1,3},{3,1},... | collective-permute-start | bytes 589832 | tf_op jit(solution)/shard_map/ppermute | solution.py:272
  41.8 8.3 %collective-permute-start.14 = (bf16[128,768]{1,0:T(8,128)(2,1)S(1)}, bf16[128,768]{1,0:T(8,128)(2,1)S(1)}, u32[]{:S(2)}, u32[]{:S(2)}) collective-permute-start(bf16[128,768]{1,0:T(8,128)(2,1)S(1)} %serve.14.after), channel_id=1, source_target_pairs={{0,4},{2,6},{4,0},{6,2},{8,12},{10,14},{12,8},{14,10},{1,5},{3,7},... | collective-permute-start | bytes 589832 | tf_op jit(solution)/shard_map/ppermute | solution.py:272
  41.8 8.4 %collective-permute-start.15 = (bf16[128,768]{1,0:T(8,128)(2,1)S(1)}, bf16[128,768]{1,0:T(8,128)(2,1)S(1)}, u32[]{:S(2)}, u32[]{:S(2)}) collective-permute-start(bf16[128,768]{1,0:T(8,128)(2,1)S(1)} %serve.15.after.refs_0_), channel_id=1, source_target_pairs={{0,1},{1,0},{2,3},{3,2},{4,5},{5,4},{6,7},{7,6},{8,9},{9,8},{10,11... | collective-permute-start | bytes 589832 | tf_op jit(solution)/shard_map/ppermute | solution.py:33
  46.1 4.6 %collective-permute-start.22 = (bf16[128,768]{1,0:T(8,128)(2,1)S(1)}, bf16[128,768]{1,0:T(8,128)(2,1)S(1)}, u32[]{:S(2)}, u32[]{:S(2)}) collective-permute-start(bf16[128,768]{1,0:T(8,128)(2,1)S(1)} %land.9.after.refs_7_), channel_id=1, source_target_pairs={{0,1},{1,0},{2,3},{3,2},{4,5},{5,4},{6,7},{7,6},{8,9},{9,8},{10,11... | collective-permute-start | bytes 589832 | tf_op jit(solution)/shard_map/ppermute | solution.py:33
  46.1 4.7 %collective-permute-start.19 = (bf16[128,768]{1,0:T(8,128)(2,1)S(1)}, bf16[128,768]{1,0:T(8,128)(2,1)S(1)}, u32[]{:S(2)}, u32[]{:S(2)}) collective-permute-start(bf16[128,768]{1,0:T(8,128)(2,1)S(1)} %land.8.after.refs_4_), channel_id=1, source_target_pairs={{0,1},{1,0},{2,3},{3,2},{4,5},{5,4},{6,7},{7,6},{8,9},{9,8},{10,11... | collective-permute-start | bytes 589832 | tf_op jit(solution)/shard_map/ppermute | solution.py:33
  48.2 3.0 %collective-permute-start.20 = (bf16[128,768]{1,0:T(8,128)(2,1)S(1)}, bf16[128,768]{1,0:T(8,128)(2,1)S(1)}, u32[]{:S(2)}, u32[]{:S(2)}) collective-permute-start(bf16[128,768]{1,0:T(8,128)(2,1)S(1)} %land.7.after.refs_5_), channel_id=1, source_target_pairs={{0,1},{1,0},{2,3},{3,2},{4,5},{5,4},{6,7},{7,6},{8,9},{9,8},{10,11... | collective-permute-start | bytes 589832 | tf_op jit(solution)/shard_map/ppermute | solution.py:33
  50.2 1.7 %collective-permute-start.16 = (bf16[128,768]{1,0:T(8,128)(2,1)S(1)}, bf16[128,768]{1,0:T(8,128)(2,1)S(1)}, u32[]{:S(2)}, u32[]{:S(2)}) collective-permute-start(bf16[128,768]{1,0:T(8,128)(2,1)S(1)} %land.12.after.refs_1_), channel_id=1, source_target_pairs={{0,1},{1,0},{2,3},{3,2},{4,5},{5,4},{6,7},{7,6},{8,9},{9,8},{10,11... | collective-permute-start | bytes 589832 | tf_op jit(solution)/shard_map/ppermute | solution.py:33
  50.2 1.7 %collective-permute-start.17 = (bf16[128,768]{1,0:T(8,128)(2,1)S(1)}, bf16[128,768]{1,0:T(8,128)(2,1)S(1)}, u32[]{:S(2)}, u32[]{:S(2)}) collective-permute-start(bf16[128,768]{1,0:T(8,128)(2,1)S(1)} %land.13.refs_2_.refs_18_), channel_id=1, source_target_pairs={{0,1},{1,0},{2,3},{3,2},{4,5},{5,4},{6,7},{7,6},{8,9},{9,8},{10,11... | collective-permute-start | bytes 589832 | tf_op jit(solution)/shard_map/ppermute | solution.py:33
  50.8 1.7 %collective-permute-start.18 = (bf16[128,768]{1,0:T(8,128)(2,1)S(1)}, bf16[128,768]{1,0:T(8,128)(2,1)S(1)}, u32[]{:S(2)}, u32[]{:S(2)}) collective-permute-start(bf16[128,768]{1,0:T(8,128)(2,1)S(1)} %land.10.after.refs_3_), channel_id=1, source_target_pairs={{0,1},{1,0},{2,3},{3,2},{4,5},{5,4},{6,7},{7,6},{8,9},{9,8},{10,11... | collective-permute-start | bytes 589832 | tf_op jit(solution)/shard_map/ppermute | solution.py:33
  51.2 23.8 %collective-permute-start.28 = (bf16[256,160]{1,0:T(8,128)(2,1)S(1)}, bf16[256,160]{1,0:T(8,128)(2,1)S(1)}, u32[]{:S(2)}, u32[]{:S(2)}) collective-permute-start(bf16[256,160]{1,0:T(8,128)(2,1)S(1)} %get-tuple-element.72.cot), channel_id=1, source_target_pairs={{0,1},{1,0},{2,3},{3,2},{4,5},{5,4},{6,7},{7,6},{8,9},{9,8},{10,11... | collective-permute-start | bytes 245768 | tf_op jit(solution)/shard_map/ppermute | solution.py:33
  54.4 4.6 %collective-permute-start.23 = (bf16[512,768]{1,0:T(8,128)(2,1)S(1)}, bf16[512,768]{1,0:T(8,128)(2,1)S(1)}, u32[]{:S(2)}, u32[]{:S(2)}) collective-permute-start(bf16[512,768]{1,0:T(8,128)(2,1)S(1)} %get-tuple-element.59.other), channel_id=1, source_target_pairs={{0,1},{1,0},{2,3},{3,2},{4,5},{5,4},{6,7},{7,6},{8,9},{9,8},{10,11... | collective-permute-start | bytes 2359304 | tf_op jit(solution)/shard_map/ppermute | solution.py:33
  56.5 2.4 %collective-permute-start.25 = (bf16[512,512]{1,0:T(8,128)(2,1)S(1)}, bf16[512,512]{1,0:T(8,128)(2,1)S(1)}, u32[]{:S(2)}, u32[]{:S(2)}) collective-permute-start(bf16[512,512]{1,0:T(8,128)(2,1)S(1)} %get-tuple-element.61.after.grad.far), channel_id=1, source_target_pairs={{0,1},{1,0},{2,3},{3,2},{4,5},{5,4},{6,7},{7,6},{8,9},{9,8},{10,11... | collective-permute-start | bytes 1572872 | tf_op jit(solution)/shard_map/ppermute | solution.py:33
  58.6 2.1 %collective-permute-start.24 = (bf16[512,512]{1,0:T(8,128)(2,1)S(1)}, bf16[512,512]{1,0:T(8,128)(2,1)S(1)}, u32[]{:S(2)}, u32[]{:S(2)}) collective-permute-start(bf16[512,512]{1,0:T(8,128)(2,1)S(1)} %get-tuple-element.66.after.grad), channel_id=1, source_target_pairs={{0,1},{1,0},{2,3},{3,2},{4,5},{5,4},{6,7},{7,6},{8,9},{9,8},{10,11... | collective-permute-start | bytes 1572872 | tf_op jit(solution)/shard_map/ppermute | solution.py:33
  60.1 10.7 %collective-permute-start.26 = (bf16[4,352,128]{2,1,0:T(8,128)(2,1)S(1)}, bf16[4,352,128]{2,1,0:T(8,128)(2,1)S(1)}, u32[]{:S(2)}, u32[]{:S(2)}) collective-permute-start(bf16[4,352,128]{2,1,0:T(8,128)(2,1)S(1)} %send_across.1.after), channel_id=1, source_target_pairs={{0,2},{2,0},{1,3},{3,1},{4,6},{6,4},{5,7},{7,5},{8,10},{10,8},{9,1... | collective-permute-start | bytes 1081352 | tf_op jit(solution)/shard_map/ppermute | solution.py:33
  62.8 10.5 %collective-permute-start.31 = (bf16[4,352,128]{2,1,0:T(8,128)(2,1)S(1)}, bf16[4,352,128]{2,1,0:T(8,128)(2,1)S(1)}, u32[]{:S(2)}, u32[]{:S(2)}) collective-permute-start(bf16[4,352,128]{2,1,0:T(8,128)(2,1)S(1)} %send_along.1.after), channel_id=1, source_target_pairs={{0,4},{4,0},{8,12},{12,8},{1,5},{5,1},{9,13},{13,9},{2,6},{6,2},{1... | collective-permute-start | bytes 1081352 | tf_op jit(solution)/shard_map/ppermute | solution.py:33
  68.6 6.4 %collective-permute-start.29 = (bf16[256,512]{1,0:T(8,128)(2,1)S(1)}, bf16[256,512]{1,0:T(8,128)(2,1)S(1)}, u32[]{:S(2)}, u32[]{:S(2)}) collective-permute-start(bf16[256,512]{1,0:T(8,128)(2,1)S(1)} %get-tuple-element.74), channel_id=1, source_target_pairs={{0,1},{1,0},{2,3},{3,2},{4,5},{5,4},{6,7},{7,6},{8,9},{9,8},{10,11... | collective-permute-start | bytes 786440 | tf_op jit(solution)/shard_map/ppermute | solution.py:33
  68.6 6.4 %collective-permute-start.30 = (bf16[256,512]{1,0:T(8,128)(2,1)S(1)}, bf16[256,512]{1,0:T(8,128)(2,1)S(1)}, u32[]{:S(2)}, u32[]{:S(2)}) collective-permute-start(bf16[256,512]{1,0:T(8,128)(2,1)S(1)} %get-tuple-element.76), channel_id=1, source_target_pairs={{0,1},{1,0},{2,3},{3,2},{4,5},{5,4},{6,7},{7,6},{8,9},{9,8},{10,11... | collective-permute-start | bytes 786440 | tf_op jit(solution)/shard_map/ppermute | solution.py:33
  71.7 8.5 %collective-permute-start.27 = (bf16[2,352,128]{2,1,0:T(8,128)(2,1)S(1)}, bf16[2,352,128]{2,1,0:T(8,128)(2,1)S(1)}, u32[]{:S(2)}, u32[]{:S(2)}) collective-permute-start(bf16[2,352,128]{2,1,0:T(8,128)(2,1)S(1)} %get-tuple-element.70.after), channel_id=1, source_target_pairs={{0,4},{4,0},{8,12},{12,8},{1,5},{5,1},{9,13},{13,9},{2,6},{6,2},{1... | collective-permute-start | bytes 540680 | tf_op jit(solution)/shard_map/ppermute | solution.py:33
  73.3 15.8 %collective-permute-start.34 = (bf16[2,352,128]{2,1,0:T(8,128)(2,1)S(1)}, bf16[2,352,128]{2,1,0:T(8,128)(2,1)S(1)}, u32[]{:S(2)}, u32[]{:S(2)}) collective-permute-start(bf16[2,352,128]{2,1,0:T(8,128)(2,1)S(1)} %get-tuple-element.77.after), channel_id=1, source_target_pairs={{0,8},{4,12},{8,0},{12,4},{1,9},{5,13},{9,1},{13,5},{2,10},{6,14},... | collective-permute-start | bytes 540680 | tf_op jit(solution)/shard_map/ppermute | solution.py:33
  76.9 13.5 %collective-permute-start.33 = (bf16[4,224,128]{2,1,0:T(8,128)(2,1)S(1)}, bf16[4,224,128]{2,1,0:T(8,128)(2,1)S(1)}, u32[]{:S(2)}, u32[]{:S(2)}) collective-permute-start(bf16[4,224,128]{2,1,0:T(8,128)(2,1)S(1)} %get-tuple-element.79), channel_id=1, source_target_pairs={{0,2},{2,0},{1,3},{3,1},{4,6},{6,4},{5,7},{7,5},{8,10},{10,8},{9,1... | collective-permute-start | bytes 688136 | tf_op jit(solution)/shard_map/ppermute | solution.py:33
  80.3 11.4 %collective-permute-start.32 = (bf16[2,352,128]{2,1,0:T(8,128)(2,1)S(1)}, bf16[2,352,128]{2,1,0:T(8,128)(2,1)S(1)}, u32[]{:S(2)}, u32[]{:S(2)}) collective-permute-start(bf16[2,352,128]{2,1,0:T(8,128)(2,1)S(1)} %add.19.after.mine), channel_id=1, source_target_pairs={{0,8},{4,12},{8,0},{12,4},{1,9},{5,13},{9,1},{13,5},{2,10},{6,14},... | collective-permute-start | bytes 540680 | tf_op jit(solution)/shard_map/ppermute | solution.py:33
  89.1 5.6 %collective-permute-start.37 = (bf16[2,352,128]{2,1,0:T(8,128)(2,1)S(1)}, bf16[2,352,128]{2,1,0:T(8,128)(2,1)S(1)}, u32[]{:S(2)}, u32[]{:S(2)}) collective-permute-start(bf16[2,352,128]{2,1,0:T(8,128)(2,1)S(1)} %add.20.after.mine), channel_id=1, source_target_pairs={{0,2},{2,0},{1,3},{3,1},{4,6},{6,4},{5,7},{7,5},{8,10},{10,8},{9,1... | collective-permute-start | bytes 540680 | tf_op jit(solution)/shard_map/ppermute | solution.py:33
  90.5 9.0 %collective-permute-start.36 = (bf16[2,224,128]{2,1,0:T(8,128)(2,1)S(1)}, bf16[2,224,128]{2,1,0:T(8,128)(2,1)S(1)}, u32[]{:S(2)}, u32[]{:S(2)}) collective-permute-start(bf16[2,224,128]{2,1,0:T(8,128)(2,1)S(1)} %get-tuple-element.81.after), channel_id=1, source_target_pairs={{0,4},{4,0},{8,12},{12,8},{1,5},{5,1},{9,13},{13,9},{2,6},{6,2},{1... | collective-permute-start | bytes 344072 | tf_op jit(solution)/shard_map/ppermute | solution.py:33
  91.7 10.1 %collective-permute-start.35 = (bf16[2,352,128]{2,1,0:T(8,128)(2,1)S(1)}, bf16[2,352,128]{2,1,0:T(8,128)(2,1)S(1)}, u32[]{:S(2)}, u32[]{:S(2)}) collective-permute-start(bf16[2,352,128]{2,1,0:T(8,128)(2,1)S(1)} %meet.3.after.near), channel_id=1, source_target_pairs={{0,4},{4,0},{8,12},{12,8},{1,5},{5,1},{9,13},{13,9},{2,6},{6,2},{1... | collective-permute-start | bytes 540680 | tf_op jit(solution)/shard_map/ppermute | solution.py:33
  94.7 11.9 %collective-permute-start.41 = (bf16[2,352,128]{2,1,0:T(8,128)(2,1)S(1)}, bf16[2,352,128]{2,1,0:T(8,128)(2,1)S(1)}, u32[]{:S(2)}, u32[]{:S(2)}) collective-permute-start(bf16[2,352,128]{2,1,0:T(8,128)(2,1)S(1)} %meet.4.after.near), channel_id=1, source_target_pairs={{0,8},{4,12},{8,0},{12,4},{1,9},{5,13},{9,1},{13,5},{2,10},{6,14},... | collective-permute-start | bytes 540680 | tf_op jit(solution)/shard_map/ppermute | solution.py:33
  99.5 8.3 %collective-permute-start.45 = (bf16[2,224,128]{2,1,0:T(8,128)(2,1)S(1)}, bf16[2,224,128]{2,1,0:T(8,128)(2,1)S(1)}, u32[]{:S(2)}, u32[]{:S(2)}) collective-permute-start(bf16[2,224,128]{2,1,0:T(8,128)(2,1)S(1)} %add.21.after.later.mine), channel_id=1, source_target_pairs={{0,8},{4,12},{8,0},{12,4},{1,9},{5,13},{9,1},{13,5},{2,10},{6,14},... | collective-permute-start | bytes 344072 | tf_op jit(solution)/shard_map/ppermute | solution.py:33
  101.9 12.1 %collective-permute-start.38 = (bf16[4,352,128]{2,1,0:T(8,128)(2,1)S(1)}, bf16[4,352,128]{2,1,0:T(8,128)(2,1)S(1)}, u32[]{:S(2)}, u32[]{:S(2)}) collective-permute-start(bf16[4,352,128]{2,1,0:T(8,128)(2,1)S(1)} %join.3.after.later.refs_0_), channel_id=1, source_target_pairs={{0,2},{2,0},{1,3},{3,1},{4,6},{6,4},{5,7},{7,5},{8,10},{10,8},{9,1... | collective-permute-start | bytes 1081352 | tf_op jit(solution)/shard_map/ppermute | solution.py:33
  107.8 6.2 %collective-permute-start.46 = (bf16[2,224,128]{2,1,0:T(8,128)(2,1)S(1)}, bf16[2,224,128]{2,1,0:T(8,128)(2,1)S(1)}, u32[]{:S(2)}, u32[]{:S(2)}) collective-permute-start(bf16[2,224,128]{2,1,0:T(8,128)(2,1)S(1)} %meet.5.near.after), channel_id=1, source_target_pairs={{0,4},{4,0},{8,12},{12,8},{1,5},{5,1},{9,13},{13,9},{2,6},{6,2},{1... | collective-permute-start | bytes 344072 | tf_op jit(solution)/shard_map/ppermute | solution.py:33
  107.9 10.0 %collective-permute-start.42 = (bf16[4,352,128]{2,1,0:T(8,128)(2,1)S(1)}, bf16[4,352,128]{2,1,0:T(8,128)(2,1)S(1)}, u32[]{:S(2)}, u32[]{:S(2)}) collective-permute-start(bf16[4,352,128]{2,1,0:T(8,128)(2,1)S(1)} %join.4.after.refs_4_), channel_id=1, source_target_pairs={{0,4},{4,0},{8,12},{12,8},{1,5},{5,1},{9,13},{13,9},{2,6},{6,2},{1... | collective-permute-start | bytes 1081352 | tf_op jit(solution)/shard_map/ppermute | solution.py:33
  109.9 8.5 %collective-permute-start.43 = (bf16[4,352,128]{2,1,0:T(8,128)(2,1)S(1)}, bf16[4,352,128]{2,1,0:T(8,128)(2,1)S(1)}, u32[]{:S(2)}, u32[]{:S(2)}) collective-permute-start(bf16[4,352,128]{2,1,0:T(8,128)(2,1)S(1)} %join.4.after.refs_4_), channel_id=1, source_target_pairs={{0,1},{1,0},{2,3},{3,2},{4,5},{5,4},{6,7},{7,6},{8,9},{9,8},{10,11... | collective-permute-start | bytes 1081352 | tf_op jit(solution)/shard_map/ppermute | solution.py:33
  114.0 6.1 %collective-permute-start.47 = (bf16[4,224,128]{2,1,0:T(8,128)(2,1)S(1)}, bf16[4,224,128]{2,1,0:T(8,128)(2,1)S(1)}, u32[]{:S(2)}, u32[]{:S(2)}) collective-permute-start(bf16[4,224,128]{2,1,0:T(8,128)(2,1)S(1)} %join.5.refs_8_), channel_id=1, source_target_pairs={{0,2},{2,0},{1,3},{3,1},{4,6},{6,4},{5,7},{7,5},{8,10},{10,8},{9,1... | collective-permute-start | bytes 688136 | tf_op jit(solution)/shard_map/ppermute | solution.py:33
  115.0 5.1 %collective-permute-start.39 = (bf16[4,352,128]{2,1,0:T(8,128)(2,1)S(1)}, bf16[4,352,128]{2,1,0:T(8,128)(2,1)S(1)}, u32[]{:S(2)}, u32[]{:S(2)}) collective-permute-start(bf16[4,352,128]{2,1,0:T(8,128)(2,1)S(1)} %join.3.after.later.refs_0_), channel_id=1, source_target_pairs={{0,1},{1,0},{2,3},{3,2},{4,5},{5,4},{6,7},{7,6},{8,9},{9,8},{10,11... | collective-permute-start | bytes 1081352 | tf_op jit(solution)/shard_map/ppermute | solution.py:33
  117.9 2.5 %collective-permute-start.44 = (bf16[4,352,128]{2,1,0:T(8,128)(2,1)S(1)}, bf16[4,352,128]{2,1,0:T(8,128)(2,1)S(1)}, u32[]{:S(2)}, u32[]{:S(2)}) collective-permute-start(bf16[4,352,128]{2,1,0:T(8,128)(2,1)S(1)} %collective-permute-done.42.refs_5_), channel_id=1, source_target_pairs={{0,1},{1,0},{2,3},{3,2},{4,5},{5,4},{6,7},{7,6},{8,9},{9,8},{10,11... | collective-permute-start | bytes 1081352 | tf_op jit(solution)/shard_map/ppermute | solution.py:33
  117.9 2.5 %collective-permute-start.40 = (bf16[4,352,128]{2,1,0:T(8,128)(2,1)S(1)}, bf16[4,352,128]{2,1,0:T(8,128)(2,1)S(1)}, u32[]{:S(2)}, u32[]{:S(2)}) collective-permute-start(bf16[4,352,128]{2,1,0:T(8,128)(2,1)S(1)} %collective-permute-done.38.later.refs_1_), channel_id=1, source_target_pairs={{0,1},{1,0},{2,3},{3,2},{4,5},{5,4},{6,7},{7,6},{8,9},{9,8},{10,11... | collective-permute-start | bytes 1081352 | tf_op jit(solution)/shard_map/ppermute | solution.py:33
  118.4 2.0 %collective-permute-start.48 = (bf16[4,224,128]{2,1,0:T(8,128)(2,1)S(1)}, bf16[4,224,128]{2,1,0:T(8,128)(2,1)S(1)}, u32[]{:S(2)}, u32[]{:S(2)}) collective-permute-start(bf16[4,224,128]{2,1,0:T(8,128)(2,1)S(1)} %join.5.refs_8_), channel_id=1, source_target_pairs={{0,1},{1,0},{2,3},{3,2},{4,5},{5,4},{6,7},{7,6},{8,9},{9,8},{10,11... | collective-permute-start | bytes 688136 | tf_op jit(solution)/shard_map/ppermute | solution.py:33
  120.1 1.5 %collective-permute-start.49 = (bf16[4,224,128]{2,1,0:T(8,128)(2,1)S(1)}, bf16[4,224,128]{2,1,0:T(8,128)(2,1)S(1)}, u32[]{:S(2)}, u32[]{:S(2)}) collective-permute-start(bf16[4,224,128]{2,1,0:T(8,128)(2,1)S(1)} %collective-permute-done.47.refs_9_), channel_id=1, source_target_pairs={{0,1},{1,0},{2,3},{3,2},{4,5},{5,4},{6,7},{7,6},{8,9},{9,8},{10,11... | collective-permute-start | bytes 688136 | tf_op jit(solution)/shard_map/ppermute | solution.py:33
  (19 other events, 38.1 us)

commit v6 on v5

--- a/solution.py
+++ b/solution.py
@@ -566,10 +566,15 @@
     third_got = swap(third_send, *across[0])
     c = Piece(across, third_got, third_keep)
     after = third_keep
-    for step in (a.second, b.second, c.first, a.meet, b.meet, c.second):
-        after = step(after)
+    after = a.second(after)
+    after = c.first(after)
+    after = b.second(after)
+    after = c.second(after)
+    after = a.meet(after)
+    after = b.meet(after)
     after = a.join(after, after)
-    after = c.meet(b.join(after, after))
+    after = c.meet(after)
+    after = b.join(after, after)
     c.join(after, a.blocks[1])
 
     def both_kinds(piece):

time: 126 us -> 123 us (0.976)
  waiting for transfers between devices: 51.6 us -> 47.6 us
    ppermute x36, waiting for transfers between devices: 39.7 us -> 35.7 us  [swap(): return lax.ppermute(array, axis, [(i, i ^ distance) for i in range(size)])]
  transfers between devices with their start and end apart: 50 -> 50, of which waited for: 24 -> 24; matrix products, arithmetic and copies ran while one was open for 0% -> 0% of each run, Pallas kernels for 21% -> 22%
where the time goes in v6:
time: 123 us; the launch traced here: 122 us
  waiting for transfers between devices  47.6 us (39%)
  starting transfers between devices  40.7 us (33%)
  Pallas kernels  30.6 us (25%)
  local copies, waits for them, and re-layouts  2.11 us (2%)
  between operations  1.23 us (1%)
    ppermute x36, waiting for transfers between devices, swap(): return lax.ppermute(array, axis, [(i, i ^ distance) for i in range(size)])  35.7 us
    pallas_call x39, Pallas kernels, kernel_call(): pl.pallas_call(body, out_shape=[jax.ShapeDtypeStruct(*out) for out in out...  23.6 us
    ppermute x14, starting transfers between devices, across_chips(): lax.ppermute(array, ('tr', 'cache'), [(i, i ^ distance) for i in range(ch...  22.8 us
    ppermute x36, starting transfers between devices, swap(): return lax.ppermute(array, axis, [(i, i ^ distance) for i in range(size)])  18 us
    ppermute x14, waiting for transfers between devices, across_chips(): lax.ppermute(array, ('tr', 'cache'), [(i, i ^ distance) for i in range(ch...  11.9 us
    pallas_call x1, Pallas kernels, beside(): pl.pallas_call(beside_kernel, out_shape=[shape((middle, inputs), BF16), s...  7.01 us
  transfers between devices with their start and end apart: 50, of which 24 were waited for; matrix products, arithmetic and copies ran while one was open for 0% of the time, Pallas kernels for 22%

profile of v6, /device:TPU:0, one launch (start us, length us, event | category | flops | bytes accessed | tf_op | source)
XLA Modules:
  0.0 122.3 jit_solution(4495505742514764789)
XLA Ops:
  0.7 0.7 copy-done.12
  2.5 0.8 collective-permute-done.got
  3.4 4.9 %collective-permute-start.1 = (s32[2,64]{1,0:T(2,128)S(1)}, s32[2,64]{1,0:T(2,128)S(1)}, u32[]{:S(2)}, u32[]{:S(2)}) collective-permute-start(s32[2,64]{1,0:T(2,128)S(1)} %get-tuple-element.48), channel_id=1, source_target_pairs={{0,10},{2,8},{4,14},{6,12},{8,2},{10,0},{12,6},{14,4},{1,11},{3,9}... | collective-permute-start | bytes 1544 | tf_op jit(solution)/shard_map/ppermute | solution.py:272
  8.5 3.6 %collective-permute-start.6 = (s32[2,64]{1,0:T(2,128)S(1)}, s32[2,64]{1,0:T(2,128)S(1)}, u32[]{:S(2)}, u32[]{:S(2)}) collective-permute-start(s32[2,64]{1,0:T(2,128)S(1)} %get-tuple-element.54), channel_id=1, source_target_pairs={{0,14},{2,12},{4,10},{6,8},{8,6},{10,4},{12,2},{14,0},{1,15},{3,13... | collective-permute-start | bytes 1544 | tf_op jit(solution)/shard_map/ppermute | solution.py:272
  12.6 2.0 %collective-permute-start.13 = (bf16[128,768]{1,0:T(8,128)(2,1)S(1)}, bf16[128,768]{1,0:T(8,128)(2,1)S(1)}, u32[]{:S(2)}, u32[]{:S(2)}) collective-permute-start(bf16[128,768]{1,0:T(8,128)(2,1)S(1)} %serve.8.after), channel_id=1, source_target_pairs={{0,10},{2,8},{4,14},{6,12},{8,2},{10,0},{12,6},{14,4},{1,11},{3,9}... | collective-permute-start | bytes 589832 | tf_op jit(solution)/shard_map/ppermute | solution.py:272
  14.6 3.3 %collective-permute-start.4 = (s32[2,64]{1,0:T(2,128)S(1)}, s32[2,64]{1,0:T(2,128)S(1)}, u32[]{:S(2)}, u32[]{:S(2)}) collective-permute-start(s32[2,64]{1,0:T(2,128)S(1)} %get-tuple-element.52), channel_id=1, source_target_pairs={{0,6},{2,4},{4,2},{6,0},{8,14},{10,12},{12,10},{14,8},{1,7},{3,5},... | collective-permute-start | bytes 1544 | tf_op jit(solution)/shard_map/ppermute | solution.py:272
  18.0 1.5 %collective-permute-start.3 = (s32[2,64]{1,0:T(2,128)S(1)}, s32[2,64]{1,0:T(2,128)S(1)}, u32[]{:S(2)}, u32[]{:S(2)}) collective-permute-start(s32[2,64]{1,0:T(2,128)S(1)} %get-tuple-element.51), channel_id=1, source_target_pairs={{0,2},{2,0},{4,6},{6,4},{8,10},{10,8},{12,14},{14,12},{1,3},{3,1},... | collective-permute-start | bytes 1544 | tf_op jit(solution)/shard_map/ppermute | solution.py:272
  20.5 2.5 %collective-permute-start.11 = (bf16[128,768]{1,0:T(8,128)(2,1)S(1)}, bf16[128,768]{1,0:T(8,128)(2,1)S(1)}, u32[]{:S(2)}, u32[]{:S(2)}) collective-permute-start(bf16[128,768]{1,0:T(8,128)(2,1)S(1)} %serve.10.after), channel_id=1, source_target_pairs={{0,14},{2,12},{4,10},{6,8},{8,6},{10,4},{12,2},{14,0},{1,15},{3,13... | collective-permute-start | bytes 589832 | tf_op jit(solution)/shard_map/ppermute | solution.py:272
  23.5 1.5 %collective-permute-start.9 = (bf16[128,768]{1,0:T(8,128)(2,1)S(1)}, bf16[128,768]{1,0:T(8,128)(2,1)S(1)}, u32[]{:S(2)}, u32[]{:S(2)}) collective-permute-start(bf16[128,768]{1,0:T(8,128)(2,1)S(1)} %serve.11.after), channel_id=1, source_target_pairs={{0,12},{2,14},{4,8},{6,10},{8,4},{10,6},{12,0},{14,2},{1,13},{3,15... | collective-permute-start | bytes 589832 | tf_op jit(solution)/shard_map/ppermute | solution.py:272
  26.7 7.0 %beside.1 = (bf16[512,1024]{1,0:T(8,128)(2,1)S(1)}, bf16[256,512]{1,0:T(8,128)(2,1)S(1)}, f32[512,2]{1,0:T(8,128)S(1)}, f32[256,1]{1,0:T(8,128)S(1)}, bf16[512,1...) custom-call(s32[16]{0:T(128)S(1)} %copy-done.15, s32[10,512]{1,0:T(8,128)S(1)} %bitcast.18, s32[1,512]{1,0:T(1,128)S(1)} %bitcast.20, ...), custom_call_target="tpu_custom_call" | custom-call | flops 10000000000 | bytes 10000000 | tf_op jit(solution)/shard_map/beside/pallas_call | solution.py:367
  33.7 2.5 %collective-permute-start.10 = (bf16[128,768]{1,0:T(8,128)(2,1)S(1)}, bf16[128,768]{1,0:T(8,128)(2,1)S(1)}, u32[]{:S(2)}, u32[]{:S(2)}) collective-permute-start(bf16[128,768]{1,0:T(8,128)(2,1)S(1)} %serve.12.after), channel_id=1, source_target_pairs={{0,6},{2,4},{4,2},{6,0},{8,14},{10,12},{12,10},{14,8},{1,7},{3,5},... | collective-permute-start | bytes 589832 | tf_op jit(solution)/shard_map/ppermute | solution.py:272
  37.2 1.4 %collective-permute-done.13.rows = bf16[128,768]{1,0:T(8,128)(2,1)S(1)} collective-permute-done((bf16[128,768]{1,0:T(8,128)(2,1)S(1)}, bf16[128,768]{1,0:T(8,128)(2,1)S(1)}, u32[]{:S(2)}, u32[]{:S(2)}) %collective-permute-start.13) | collective-permute-done | bytes 196640 | tf_op jit(solution)/shard_map/ppermute | solution.py:272
  39.1 2.7 %collective-permute-done.12.rows = bf16[128,768]{1,0:T(8,128)(2,1)S(1)} collective-permute-done((bf16[128,768]{1,0:T(8,128)(2,1)S(1)}, bf16[128,768]{1,0:T(8,128)(2,1)S(1)}, u32[]{:S(2)}, u32[]{:S(2)}) %collective-permute-start.12) | collective-permute-done | bytes 196640 | tf_op jit(solution)/shard_map/ppermute | solution.py:272
  41.9 4.2 %collective-permute-done.10.rows = bf16[128,768]{1,0:T(8,128)(2,1)S(1)} collective-permute-done((bf16[128,768]{1,0:T(8,128)(2,1)S(1)}, bf16[128,768]{1,0:T(8,128)(2,1)S(1)}, u32[]{:S(2)}, u32[]{:S(2)}) %collective-permute-start.10) | collective-permute-done | bytes 196640 | tf_op jit(solution)/shard_map/ppermute | solution.py:272
  46.6 1.6 %collective-permute-done.8.rows = bf16[128,768]{1,0:T(8,128)(2,1)S(1)} collective-permute-done((bf16[128,768]{1,0:T(8,128)(2,1)S(1)}, bf16[128,768]{1,0:T(8,128)(2,1)S(1)}, u32[]{:S(2)}, u32[]{:S(2)}) %collective-permute-start.8) | collective-permute-done | bytes 196640 | tf_op jit(solution)/shard_map/ppermute | solution.py:272
  48.2 2.0 %collective-permute-done.14.rows = bf16[128,768]{1,0:T(8,128)(2,1)S(1)} collective-permute-done((bf16[128,768]{1,0:T(8,128)(2,1)S(1)}, bf16[128,768]{1,0:T(8,128)(2,1)S(1)}, u32[]{:S(2)}, u32[]{:S(2)}) %collective-permute-start.14) | collective-permute-done | bytes 196640 | tf_op jit(solution)/shard_map/ppermute | solution.py:272
  52.5 1.9 %mean.1 = (bf16[512,768]{1,0:T(8,128)(2,1)S(1)}, bf16[512,768]{1,0:T(8,128)(2,1)S(1)}) custom-call(s32[3]{0:T(128)S(1)} %copy-done.1, bf16[128,768]{1,0:T(8,128)(2,1)S(1)} %serve.15.after.refs_0_, bf16[128,768]{1,0:T(8,128)(2,1)S(1)} %land.12.after.refs_1_, bf16[128,768]{1,0:T(8,128)(2,1)S(1)} %land.13.refs_2_.refs_18_, ...), custom_call_target="tpu_custom_call" | custom-call | flops 10000000000 | bytes 10000000 | tf_op jit(solution)/shard_map/mean/pallas_call | solution.py:46
  54.7 1.8 %hidden.2 = (bf16[512,512]{1,0:T(8,128)(2,1)S(1)}, bf16[512,512]{1,0:T(8,128)(2,1)S(1)}) custom-call(s32[3]{0:T(128)S(1)} %copy-done.1, bf16[512,768]{1,0:T(8,128)(2,1)S(1)} %get-tuple-element.58.mine.after, bf16[512,768]{1,0:T(8,128)(2,1)S(1)} %get-tuple-element.59.other, bf16[768,1024]{1,0:T(8,128)(2,1)S(1)} %copy-done.3, bf16[768,1024]{1,0:T(8,128)(2,1)S(1)} %copy-done.4, ...), custom_call_target="tpu_custom_call" | custom-call | flops 10000000000 | bytes 10000000 | tf_op jit(solution)/shard_map/hidden/pallas_call | solution.py:46
  56.8 1.8 %hidden.3 = (bf16[512,512]{1,0:T(8,128)(2,1)S(1)}, bf16[512,512]{1,0:T(8,128)(2,1)S(1)}) custom-call(s32[3]{0:T(128)S(1)} %copy-done.1, bf16[512,768]{1,0:T(8,128)(2,1)S(1)} %get-tuple-element.58.mine.after, bf16[512,768]{1,0:T(8,128)(2,1)S(1)} %get-tuple-element.59.other, bf16[768,1024]{1,0:T(8,128)(2,1)S(1)} %copy-done.3, bf16[768,1024]{1,0:T(8,128)(2,1)S(1)} %copy-done.4, ...), custom_call_target="tpu_custom_call" | custom-call | flops 10000000000 | bytes 10000000 | tf_op jit(solution)/shard_map/hidden/pallas_call | solution.py:46
  58.9 1.1 send_across.1.after
  60.1 0.7 collective-permute-start.26
  60.8 2.0 %send_along.1.after = bf16[4,352,128]{2,1,0:T(8,128)(2,1)S(1)} custom-call(s32[3]{0:T(128)S(1)} %copy-done.1, bf16[512,768]{1,0:T(8,128)(2,1)S(1)} %get-tuple-element.58.mine.after, bf16[512,768]{1,0:T(8,128)(2,1)S(1)} %collective-permute-done.23.got, bf16[512,512]{1,0:T(8,128)(2,1)S(1)} %get-tuple-element.66.after.grad, ...), custom_call_target="tpu_custom_call" | custom-call | flops 10000000000 | bytes 10000000 | tf_op jit(solution)/shard_map/send_along/pallas_call | solution.py:46
  62.8 1.2 collective-permute-start.31
  64.0 2.4 %keep.1 = (f32[4,352,128]{2,1,0:T(8,128)S(1)}, f32[4,352,128]{2,1,0:T(8,128)S(1)}) custom-call(s32[3]{0:T(128)S(1)} %copy-done.1, bf16[512,768]{1,0:T(8,128)(2,1)S(1)} %get-tuple-element.58.mine.after, bf16[512,768]{1,0:T(8,128)(2,1)S(1)} %collective-permute-done.23.got, bf16[512,512]{1,0:T(8,128)(2,1)S(1)} %get-tuple-element.66.after.grad, ...), custom_call_target="tpu_custom_call" | custom-call | flops 10000000000 | bytes 10000000 | tf_op jit(solution)/shard_map/keep/pallas_call | solution.py:46
  66.4 2.2 %top.1 = (f32[153,256]{1,0:T(8,128)}, bf16[256,512]{1,0:T(8,128)(2,1)S(1)}, bf16[256,512]{1,0:T(8,128)(2,1)S(1)}, bf16[256,512]{1,0:T(8,128)(2,1)S(1)}, bf16[256,512]{1,0:T(8,128)(2,1)S(1)}) custom-call(s32[3]{0:T(128)S(1)} %copy-done.1, bf16[512,512]{1,0:T(8,128)(2,1)S(1)} %get-tuple-element.62.near, bf16[512,512]{1,0:T(8,128)(2,1)S(1)} %get-tuple-element.63.far, ...), custom_call_target="tpu_custom_call" | custom-call | flops 10000000000 | bytes 10000000 | tf_op jit(solution)/shard_map/top/pallas_call | solution.py:46
  69.1 1.7 %collective-permute-done.26.got = bf16[4,352,128]{2,1,0:T(8,128)(2,1)S(1)} collective-permute-done((bf16[4,352,128]{2,1,0:T(8,128)(2,1)S(1)}, bf16[4,352,128]{2,1,0:T(8,128)(2,1)S(1)}, u32[]{:S(2)}, u32[]{:S(2)}) %collective-permute-start.26) | collective-permute-done | bytes 360480 | tf_op jit(solution)/shard_map/ppermute | solution.py:33
  70.8 0.9 copy-done.16
  71.7 1.2 collective-permute-start.27
  73.3 1.7 %collective-permute-start.35 = (bf16[2,352,128]{2,1,0:T(8,128)(2,1)S(1)}, bf16[2,352,128]{2,1,0:T(8,128)(2,1)S(1)}, u32[]{:S(2)}, u32[]{:S(2)}) collective-permute-start(bf16[2,352,128]{2,1,0:T(8,128)(2,1)S(1)} %get-tuple-element.77.after), channel_id=1, source_target_pairs={{0,8},{4,12},{8,0},{12,4},{1,9},{5,13},{9,1},{13,5},{2,10},{6,14},... | collective-permute-start | bytes 540680 | tf_op jit(solution)/shard_map/ppermute | solution.py:33
  75.0 1.9 %last.1 = (bf16[4,224,128]{2,1,0:T(8,128)(2,1)S(1)}, f32[4,224,128]{2,1,0:T(8,128)S(1)}) custom-call(s32[3]{0:T(128)S(1)} %copy-done.1, bf16[512,768]{1,0:T(8,128)(2,1)S(1)} %get-tuple-element.58.mine.after, bf16[512,768]{1,0:T(8,128)(2,1)S(1)} %collective-permute-done.23.got, bf16[512,512]{1,0:T(8,128)(2,1)S(1)} %get-tuple-element.66.after.grad, ...), custom_call_target="tpu_custom_call" | custom-call | flops 10000000000 | bytes 10000000 | tf_op jit(solution)/shard_map/last/pallas_call | solution.py:46
  76.9 1.1 collective-permute-start.33
  78.0 2.2 %collective-permute-done.27.got = bf16[2,352,128]{2,1,0:T(8,128)(2,1)S(1)} collective-permute-done((bf16[2,352,128]{2,1,0:T(8,128)(2,1)S(1)}, bf16[2,352,128]{2,1,0:T(8,128)(2,1)S(1)}, u32[]{:S(2)}, u32[]{:S(2)}) %collective-permute-start.27) | collective-permute-done | bytes 180256 | tf_op jit(solution)/shard_map/ppermute | solution.py:33
  80.7 2.6 %collective-permute-done.33.got = bf16[4,224,128]{2,1,0:T(8,128)(2,1)S(1)} collective-permute-done((bf16[4,224,128]{2,1,0:T(8,128)(2,1)S(1)}, bf16[4,224,128]{2,1,0:T(8,128)(2,1)S(1)}, u32[]{:S(2)}, u32[]{:S(2)}) %collective-permute-start.33) | collective-permute-done | bytes 229408 | tf_op jit(solution)/shard_map/ppermute | solution.py:33
  83.4 0.8 collective-permute-start.34
  84.2 4.9 %collective-permute-done.35.got = bf16[2,352,128]{2,1,0:T(8,128)(2,1)S(1)} collective-permute-done((bf16[2,352,128]{2,1,0:T(8,128)(2,1)S(1)}, bf16[2,352,128]{2,1,0:T(8,128)(2,1)S(1)}, u32[]{:S(2)}, u32[]{:S(2)}) %collective-permute-start.35) | collective-permute-done | bytes 180256 | tf_op jit(solution)/shard_map/ppermute | solution.py:33
  89.2 1.3 %collective-permute-start.37 = (bf16[2,352,128]{2,1,0:T(8,128)(2,1)S(1)}, bf16[2,352,128]{2,1,0:T(8,128)(2,1)S(1)}, u32[]{:S(2)}, u32[]{:S(2)}) collective-permute-start(bf16[2,352,128]{2,1,0:T(8,128)(2,1)S(1)} %add.20.after.mine), channel_id=1, source_target_pairs={{0,2},{2,0},{1,3},{3,1},{4,6},{6,4},{5,7},{7,5},{8,10},{10,8},{9,1... | collective-permute-start | bytes 540680 | tf_op jit(solution)/shard_map/ppermute | solution.py:33
  90.5 1.2 collective-permute-done.34.got
  91.8 2.4 %collective-permute-done.32.got = bf16[2,352,128]{2,1,0:T(8,128)(2,1)S(1)} collective-permute-done((bf16[2,352,128]{2,1,0:T(8,128)(2,1)S(1)}, bf16[2,352,128]{2,1,0:T(8,128)(2,1)S(1)}, u32[]{:S(2)}, u32[]{:S(2)}) %collective-permute-start.32) | collective-permute-done | bytes 180256 | tf_op jit(solution)/shard_map/ppermute | solution.py:33
  94.8 1.4 %collective-permute-start.41 = (bf16[2,352,128]{2,1,0:T(8,128)(2,1)S(1)}, bf16[2,352,128]{2,1,0:T(8,128)(2,1)S(1)}, u32[]{:S(2)}, u32[]{:S(2)}) collective-permute-start(bf16[2,352,128]{2,1,0:T(8,128)(2,1)S(1)} %meet.4.after.later.near), channel_id=1, source_target_pairs={{0,8},{4,12},{8,0},{12,4},{1,9},{5,13},{9,1},{13,5},{2,10},{6,14},... | collective-permute-start | bytes 540680 | tf_op jit(solution)/shard_map/ppermute | solution.py:33
  96.2 5.5 %collective-permute-done.36.far = bf16[2,352,128]{2,1,0:T(8,128)(2,1)S(1)} collective-permute-done((bf16[2,352,128]{2,1,0:T(8,128)(2,1)S(1)}, bf16[2,352,128]{2,1,0:T(8,128)(2,1)S(1)}, u32[]{:S(2)}, u32[]{:S(2)}) %collective-permute-start.36) | collective-permute-done | bytes 180256 | tf_op jit(solution)/shard_map/ppermute | solution.py:33
  101.7 1.2 collective-permute-start.38
  103.1 1.2 %collective-permute-done.41.far = bf16[2,352,128]{2,1,0:T(8,128)(2,1)S(1)} collective-permute-done((bf16[2,352,128]{2,1,0:T(8,128)(2,1)S(1)}, bf16[2,352,128]{2,1,0:T(8,128)(2,1)S(1)}, u32[]{:S(2)}, u32[]{:S(2)}) %collective-permute-start.41) | collective-permute-done | bytes 180256 | tf_op jit(solution)/shard_map/ppermute | solution.py:33
  104.3 0.8 collective-permute-start.43
  105.1 3.8 %collective-permute-done.46.far = bf16[2,224,128]{2,1,0:T(8,128)(2,1)S(1)} collective-permute-done((bf16[2,224,128]{2,1,0:T(8,128)(2,1)S(1)}, bf16[2,224,128]{2,1,0:T(8,128)(2,1)S(1)}, u32[]{:S(2)}, u32[]{:S(2)}) %collective-permute-start.46) | collective-permute-done | bytes 114720 | tf_op jit(solution)/shard_map/ppermute | solution.py:33
  109.2 1.2 collective-permute-start.47
  110.9 5.4 %collective-permute-done.43.refs_5_ = bf16[4,352,128]{2,1,0:T(8,128)(2,1)S(1)} collective-permute-done((bf16[4,352,128]{2,1,0:T(8,128)(2,1)S(1)}, bf16[4,352,128]{2,1,0:T(8,128)(2,1)S(1)}, u32[]{:S(2)}, u32[]{:S(2)}) %collective-permute-start.43) | collective-permute-done | bytes 360480 | tf_op jit(solution)/shard_map/ppermute | solution.py:33
  116.9 1.4 %collective-permute-done.48.refs_10_ = bf16[4,224,128]{2,1,0:T(8,128)(2,1)S(1)} collective-permute-done((bf16[4,224,128]{2,1,0:T(8,128)(2,1)S(1)}, bf16[4,224,128]{2,1,0:T(8,128)(2,1)S(1)}, u32[]{:S(2)}, u32[]{:S(2)}) %collective-permute-start.48) | collective-permute-done | bytes 229408 | tf_op jit(solution)/shard_map/ppermute | solution.py:33
  118.6 3.6 %place.1 = (bf16[768,1024]{1,0:T(8,128)(2,1)}, bf16[768,1024]{1,0:T(8,128)(2,1)}, bf16[153,1024]{1,0:T(8,128)(2,1)}, bf16[153,1024]{1,0:T(8,128)(2,1)}) custom-call(s32[3]{0:T(128)S(1)} %copy-done.1, bf16[4,352,128]{2,1,0:T(8,128)(2,1)S(1)} %join.3.after.refs_0_, bf16[4,352,128]{2,1,0:T(8,128)(2,1)S(1)} %collective-permute-done.38.later.refs_1_, ...), custom_call_target="tpu_custom_call" | custom-call | flops 10000000000 | bytes 10000000 | tf_op jit(solution)/shard_map/place/pallas_call | solution.py:46
  (127 shorter events, 14.6 us)
Async XLA Ops:
  3.4 8.8 %collective-permute-start.1 = (s32[2,64]{1,0:T(2,128)S(1)}, s32[2,64]{1,0:T(2,128)S(1)}, u32[]{:S(2)}, u32[]{:S(2)}) collective-permute-start(s32[2,64]{1,0:T(2,128)S(1)} %get-tuple-element.48), channel_id=1, source_target_pairs={{0,10},{2,8},{4,14},{6,12},{8,2},{10,0},{12,6},{14,4},{1,11},{3,9}... | collective-permute-start | bytes 1544 | tf_op jit(solution)/shard_map/ppermute | solution.py:272
  8.2 9.8 %collective-permute-start.7 = (s32[2,64]{1,0:T(2,128)S(1)}, s32[2,64]{1,0:T(2,128)S(1)}, u32[]{:S(2)}, u32[]{:S(2)}) collective-permute-start(s32[2,64]{1,0:T(2,128)S(1)} %get-tuple-element.55), channel_id=1, source_target_pairs={{0,8},{2,10},{4,12},{6,14},{8,0},{10,2},{12,4},{14,6},{1,9},{3,11}... | collective-permute-start | bytes 1544 | tf_op jit(solution)/shard_map/ppermute | solution.py:272
  8.5 11.4 %collective-permute-start.6 = (s32[2,64]{1,0:T(2,128)S(1)}, s32[2,64]{1,0:T(2,128)S(1)}, u32[]{:S(2)}, u32[]{:S(2)}) collective-permute-start(s32[2,64]{1,0:T(2,128)S(1)} %get-tuple-element.54), channel_id=1, source_target_pairs={{0,14},{2,12},{4,10},{6,8},{8,6},{10,4},{12,2},{14,0},{1,15},{3,13... | collective-permute-start | bytes 1544 | tf_op jit(solution)/shard_map/ppermute | solution.py:272
  12.1 8.4 %collective-permute-start.5 = (s32[2,64]{1,0:T(2,128)S(1)}, s32[2,64]{1,0:T(2,128)S(1)}, u32[]{:S(2)}, u32[]{:S(2)}) collective-permute-start(s32[2,64]{1,0:T(2,128)S(1)} %get-tuple-element.53), channel_id=1, source_target_pairs={{0,12},{2,14},{4,8},{6,10},{8,4},{10,6},{12,0},{14,2},{1,13},{3,15... | collective-permute-start | bytes 1544 | tf_op jit(solution)/shard_map/ppermute | solution.py:272
  12.6 26.0 %collective-permute-start.13 = (bf16[128,768]{1,0:T(8,128)(2,1)S(1)}, bf16[128,768]{1,0:T(8,128)(2,1)S(1)}, u32[]{:S(2)}, u32[]{:S(2)}) collective-permute-start(bf16[128,768]{1,0:T(8,128)(2,1)S(1)} %serve.8.after), channel_id=1, source_target_pairs={{0,10},{2,8},{4,14},{6,12},{8,2},{10,0},{12,6},{14,4},{1,11},{3,9}... | collective-permute-start | bytes 589832 | tf_op jit(solution)/shard_map/ppermute | solution.py:272
  14.6 8.9 %collective-permute-start.4 = (s32[2,64]{1,0:T(2,128)S(1)}, s32[2,64]{1,0:T(2,128)S(1)}, u32[]{:S(2)}, u32[]{:S(2)}) collective-permute-start(s32[2,64]{1,0:T(2,128)S(1)} %get-tuple-element.52), channel_id=1, source_target_pairs={{0,6},{2,4},{4,2},{6,0},{8,14},{10,12},{12,10},{14,8},{1,7},{3,5},... | collective-permute-start | bytes 1544 | tf_op jit(solution)/shard_map/ppermute | solution.py:272
  18.0 7.6 %collective-permute-start.3 = (s32[2,64]{1,0:T(2,128)S(1)}, s32[2,64]{1,0:T(2,128)S(1)}, u32[]{:S(2)}, u32[]{:S(2)}) collective-permute-start(s32[2,64]{1,0:T(2,128)S(1)} %get-tuple-element.51), channel_id=1, source_target_pairs={{0,2},{2,0},{4,6},{6,4},{8,10},{10,8},{12,14},{14,12},{1,3},{3,1},... | collective-permute-start | bytes 1544 | tf_op jit(solution)/shard_map/ppermute | solution.py:272
  20.0 21.9 %collective-permute-start.12 = (bf16[128,768]{1,0:T(8,128)(2,1)S(1)}, bf16[128,768]{1,0:T(8,128)(2,1)S(1)}, u32[]{:S(2)}, u32[]{:S(2)}) collective-permute-start(bf16[128,768]{1,0:T(8,128)(2,1)S(1)} %serve.9.after), channel_id=1, source_target_pairs={{0,8},{2,10},{4,12},{6,14},{8,0},{10,2},{12,4},{14,6},{1,9},{3,11}... | collective-permute-start | bytes 589832 | tf_op jit(solution)/shard_map/ppermute | solution.py:272
  20.5 21.3 %collective-permute-start.11 = (bf16[128,768]{1,0:T(8,128)(2,1)S(1)}, bf16[128,768]{1,0:T(8,128)(2,1)S(1)}, u32[]{:S(2)}, u32[]{:S(2)}) collective-permute-start(bf16[128,768]{1,0:T(8,128)(2,1)S(1)} %serve.10.after), channel_id=1, source_target_pairs={{0,14},{2,12},{4,10},{6,8},{8,6},{10,4},{12,2},{14,0},{1,15},{3,13... | collective-permute-start | bytes 589832 | tf_op jit(solution)/shard_map/ppermute | solution.py:272
  23.5 22.6 %collective-permute-start.9 = (bf16[128,768]{1,0:T(8,128)(2,1)S(1)}, bf16[128,768]{1,0:T(8,128)(2,1)S(1)}, u32[]{:S(2)}, u32[]{:S(2)}) collective-permute-start(bf16[128,768]{1,0:T(8,128)(2,1)S(1)} %serve.11.after), channel_id=1, source_target_pairs={{0,12},{2,14},{4,8},{6,10},{8,4},{10,6},{12,0},{14,2},{1,13},{3,15... | collective-permute-start | bytes 589832 | tf_op jit(solution)/shard_map/ppermute | solution.py:272
  25.7 8.0 %collective-permute-start.2 = (s32[2,64]{1,0:T(2,128)S(1)}, s32[2,64]{1,0:T(2,128)S(1)}, u32[]{:S(2)}, u32[]{:S(2)}) collective-permute-start(s32[2,64]{1,0:T(2,128)S(1)} %get-tuple-element.50), channel_id=1, source_target_pairs={{0,4},{2,6},{4,0},{6,2},{8,12},{10,14},{12,8},{14,10},{1,5},{3,7},... | collective-permute-start | bytes 1544 | tf_op jit(solution)/shard_map/ppermute | solution.py:272
  33.7 12.4 %collective-permute-start.10 = (bf16[128,768]{1,0:T(8,128)(2,1)S(1)}, bf16[128,768]{1,0:T(8,128)(2,1)S(1)}, u32[]{:S(2)}, u32[]{:S(2)}) collective-permute-start(bf16[128,768]{1,0:T(8,128)(2,1)S(1)} %serve.12.after), channel_id=1, source_target_pairs={{0,6},{2,4},{4,2},{6,0},{8,14},{10,12},{12,10},{14,8},{1,7},{3,5},... | collective-permute-start | bytes 589832 | tf_op jit(solution)/shard_map/ppermute | solution.py:272
  38.7 9.5 %collective-permute-start.8 = (bf16[128,768]{1,0:T(8,128)(2,1)S(1)}, bf16[128,768]{1,0:T(8,128)(2,1)S(1)}, u32[]{:S(2)}, u32[]{:S(2)}) collective-permute-start(bf16[128,768]{1,0:T(8,128)(2,1)S(1)} %serve.13.done), channel_id=1, source_target_pairs={{0,2},{2,0},{4,6},{6,4},{8,10},{10,8},{12,14},{14,12},{1,3},{3,1},... | collective-permute-start | bytes 589832 | tf_op jit(solution)/shard_map/ppermute | solution.py:272
  41.8 8.3 %collective-permute-start.14 = (bf16[128,768]{1,0:T(8,128)(2,1)S(1)}, bf16[128,768]{1,0:T(8,128)(2,1)S(1)}, u32[]{:S(2)}, u32[]{:S(2)}) collective-permute-start(bf16[128,768]{1,0:T(8,128)(2,1)S(1)} %serve.14.after), channel_id=1, source_target_pairs={{0,4},{2,6},{4,0},{6,2},{8,12},{10,14},{12,8},{14,10},{1,5},{3,7},... | collective-permute-start | bytes 589832 | tf_op jit(solution)/shard_map/ppermute | solution.py:272
  41.8 8.4 %collective-permute-start.15 = (bf16[128,768]{1,0:T(8,128)(2,1)S(1)}, bf16[128,768]{1,0:T(8,128)(2,1)S(1)}, u32[]{:S(2)}, u32[]{:S(2)}) collective-permute-start(bf16[128,768]{1,0:T(8,128)(2,1)S(1)} %serve.15.after.refs_0_), channel_id=1, source_target_pairs={{0,1},{1,0},{2,3},{3,2},{4,5},{5,4},{6,7},{7,6},{8,9},{9,8},{10,11... | collective-permute-start | bytes 589832 | tf_op jit(solution)/shard_map/ppermute | solution.py:33
  46.1 4.6 %collective-permute-start.22 = (bf16[128,768]{1,0:T(8,128)(2,1)S(1)}, bf16[128,768]{1,0:T(8,128)(2,1)S(1)}, u32[]{:S(2)}, u32[]{:S(2)}) collective-permute-start(bf16[128,768]{1,0:T(8,128)(2,1)S(1)} %land.9.after.refs_7_), channel_id=1, source_target_pairs={{0,1},{1,0},{2,3},{3,2},{4,5},{5,4},{6,7},{7,6},{8,9},{9,8},{10,11... | collective-permute-start | bytes 589832 | tf_op jit(solution)/shard_map/ppermute | solution.py:33
  46.1 4.7 %collective-permute-start.19 = (bf16[128,768]{1,0:T(8,128)(2,1)S(1)}, bf16[128,768]{1,0:T(8,128)(2,1)S(1)}, u32[]{:S(2)}, u32[]{:S(2)}) collective-permute-start(bf16[128,768]{1,0:T(8,128)(2,1)S(1)} %land.8.after.refs_4_), channel_id=1, source_target_pairs={{0,1},{1,0},{2,3},{3,2},{4,5},{5,4},{6,7},{7,6},{8,9},{9,8},{10,11... | collective-permute-start | bytes 589832 | tf_op jit(solution)/shard_map/ppermute | solution.py:33
  48.2 3.0 %collective-permute-start.20 = (bf16[128,768]{1,0:T(8,128)(2,1)S(1)}, bf16[128,768]{1,0:T(8,128)(2,1)S(1)}, u32[]{:S(2)}, u32[]{:S(2)}) collective-permute-start(bf16[128,768]{1,0:T(8,128)(2,1)S(1)} %land.7.after.refs_5_), channel_id=1, source_target_pairs={{0,1},{1,0},{2,3},{3,2},{4,5},{5,4},{6,7},{7,6},{8,9},{9,8},{10,11... | collective-permute-start | bytes 589832 | tf_op jit(solution)/shard_map/ppermute | solution.py:33
  50.2 1.7 %collective-permute-start.16 = (bf16[128,768]{1,0:T(8,128)(2,1)S(1)}, bf16[128,768]{1,0:T(8,128)(2,1)S(1)}, u32[]{:S(2)}, u32[]{:S(2)}) collective-permute-start(bf16[128,768]{1,0:T(8,128)(2,1)S(1)} %land.12.after.refs_1_), channel_id=1, source_target_pairs={{0,1},{1,0},{2,3},{3,2},{4,5},{5,4},{6,7},{7,6},{8,9},{9,8},{10,11... | collective-permute-start | bytes 589832 | tf_op jit(solution)/shard_map/ppermute | solution.py:33
  50.2 1.7 %collective-permute-start.17 = (bf16[128,768]{1,0:T(8,128)(2,1)S(1)}, bf16[128,768]{1,0:T(8,128)(2,1)S(1)}, u32[]{:S(2)}, u32[]{:S(2)}) collective-permute-start(bf16[128,768]{1,0:T(8,128)(2,1)S(1)} %land.13.refs_2_.refs_18_), channel_id=1, source_target_pairs={{0,1},{1,0},{2,3},{3,2},{4,5},{5,4},{6,7},{7,6},{8,9},{9,8},{10,11... | collective-permute-start | bytes 589832 | tf_op jit(solution)/shard_map/ppermute | solution.py:33
  50.8 1.7 %collective-permute-start.18 = (bf16[128,768]{1,0:T(8,128)(2,1)S(1)}, bf16[128,768]{1,0:T(8,128)(2,1)S(1)}, u32[]{:S(2)}, u32[]{:S(2)}) collective-permute-start(bf16[128,768]{1,0:T(8,128)(2,1)S(1)} %land.10.after.refs_3_), channel_id=1, source_target_pairs={{0,1},{1,0},{2,3},{3,2},{4,5},{5,4},{6,7},{7,6},{8,9},{9,8},{10,11... | collective-permute-start | bytes 589832 | tf_op jit(solution)/shard_map/ppermute | solution.py:33
  51.2 23.8 %collective-permute-start.28 = (bf16[256,160]{1,0:T(8,128)(2,1)S(1)}, bf16[256,160]{1,0:T(8,128)(2,1)S(1)}, u32[]{:S(2)}, u32[]{:S(2)}) collective-permute-start(bf16[256,160]{1,0:T(8,128)(2,1)S(1)} %get-tuple-element.72.cot), channel_id=1, source_target_pairs={{0,1},{1,0},{2,3},{3,2},{4,5},{5,4},{6,7},{7,6},{8,9},{9,8},{10,11... | collective-permute-start | bytes 245768 | tf_op jit(solution)/shard_map/ppermute | solution.py:33
  54.4 4.6 %collective-permute-start.23 = (bf16[512,768]{1,0:T(8,128)(2,1)S(1)}, bf16[512,768]{1,0:T(8,128)(2,1)S(1)}, u32[]{:S(2)}, u32[]{:S(2)}) collective-permute-start(bf16[512,768]{1,0:T(8,128)(2,1)S(1)} %get-tuple-element.59.other), channel_id=1, source_target_pairs={{0,1},{1,0},{2,3},{3,2},{4,5},{5,4},{6,7},{7,6},{8,9},{9,8},{10,11... | collective-permute-start | bytes 2359304 | tf_op jit(solution)/shard_map/ppermute | solution.py:33
  56.5 2.4 %collective-permute-start.25 = (bf16[512,512]{1,0:T(8,128)(2,1)S(1)}, bf16[512,512]{1,0:T(8,128)(2,1)S(1)}, u32[]{:S(2)}, u32[]{:S(2)}) collective-permute-start(bf16[512,512]{1,0:T(8,128)(2,1)S(1)} %get-tuple-element.61.after.grad.far), channel_id=1, source_target_pairs={{0,1},{1,0},{2,3},{3,2},{4,5},{5,4},{6,7},{7,6},{8,9},{9,8},{10,11... | collective-permute-start | bytes 1572872 | tf_op jit(solution)/shard_map/ppermute | solution.py:33
  58.6 2.1 %collective-permute-start.24 = (bf16[512,512]{1,0:T(8,128)(2,1)S(1)}, bf16[512,512]{1,0:T(8,128)(2,1)S(1)}, u32[]{:S(2)}, u32[]{:S(2)}) collective-permute-start(bf16[512,512]{1,0:T(8,128)(2,1)S(1)} %get-tuple-element.66.after.grad), channel_id=1, source_target_pairs={{0,1},{1,0},{2,3},{3,2},{4,5},{5,4},{6,7},{7,6},{8,9},{9,8},{10,11... | collective-permute-start | bytes 1572872 | tf_op jit(solution)/shard_map/ppermute | solution.py:33
  60.1 10.7 %collective-permute-start.26 = (bf16[4,352,128]{2,1,0:T(8,128)(2,1)S(1)}, bf16[4,352,128]{2,1,0:T(8,128)(2,1)S(1)}, u32[]{:S(2)}, u32[]{:S(2)}) collective-permute-start(bf16[4,352,128]{2,1,0:T(8,128)(2,1)S(1)} %send_across.1.after), channel_id=1, source_target_pairs={{0,2},{2,0},{1,3},{3,1},{4,6},{6,4},{5,7},{7,5},{8,10},{10,8},{9,1... | collective-permute-start | bytes 1081352 | tf_op jit(solution)/shard_map/ppermute | solution.py:33
  62.8 10.5 %collective-permute-start.31 = (bf16[4,352,128]{2,1,0:T(8,128)(2,1)S(1)}, bf16[4,352,128]{2,1,0:T(8,128)(2,1)S(1)}, u32[]{:S(2)}, u32[]{:S(2)}) collective-permute-start(bf16[4,352,128]{2,1,0:T(8,128)(2,1)S(1)} %send_along.1.after), channel_id=1, source_target_pairs={{0,4},{4,0},{8,12},{12,8},{1,5},{5,1},{9,13},{13,9},{2,6},{6,2},{1... | collective-permute-start | bytes 1081352 | tf_op jit(solution)/shard_map/ppermute | solution.py:33
  68.6 6.4 %collective-permute-start.29 = (bf16[256,512]{1,0:T(8,128)(2,1)S(1)}, bf16[256,512]{1,0:T(8,128)(2,1)S(1)}, u32[]{:S(2)}, u32[]{:S(2)}) collective-permute-start(bf16[256,512]{1,0:T(8,128)(2,1)S(1)} %get-tuple-element.74), channel_id=1, source_target_pairs={{0,1},{1,0},{2,3},{3,2},{4,5},{5,4},{6,7},{7,6},{8,9},{9,8},{10,11... | collective-permute-start | bytes 786440 | tf_op jit(solution)/shard_map/ppermute | solution.py:33
  68.6 6.4 %collective-permute-start.30 = (bf16[256,512]{1,0:T(8,128)(2,1)S(1)}, bf16[256,512]{1,0:T(8,128)(2,1)S(1)}, u32[]{:S(2)}, u32[]{:S(2)}) collective-permute-start(bf16[256,512]{1,0:T(8,128)(2,1)S(1)} %get-tuple-element.76), channel_id=1, source_target_pairs={{0,1},{1,0},{2,3},{3,2},{4,5},{5,4},{6,7},{7,6},{8,9},{9,8},{10,11... | collective-permute-start | bytes 786440 | tf_op jit(solution)/shard_map/ppermute | solution.py:33
  71.7 8.5 %collective-permute-start.27 = (bf16[2,352,128]{2,1,0:T(8,128)(2,1)S(1)}, bf16[2,352,128]{2,1,0:T(8,128)(2,1)S(1)}, u32[]{:S(2)}, u32[]{:S(2)}) collective-permute-start(bf16[2,352,128]{2,1,0:T(8,128)(2,1)S(1)} %get-tuple-element.70.after), channel_id=1, source_target_pairs={{0,4},{4,0},{8,12},{12,8},{1,5},{5,1},{9,13},{13,9},{2,6},{6,2},{1... | collective-permute-start | bytes 540680 | tf_op jit(solution)/shard_map/ppermute | solution.py:33
  73.3 15.8 %collective-permute-start.35 = (bf16[2,352,128]{2,1,0:T(8,128)(2,1)S(1)}, bf16[2,352,128]{2,1,0:T(8,128)(2,1)S(1)}, u32[]{:S(2)}, u32[]{:S(2)}) collective-permute-start(bf16[2,352,128]{2,1,0:T(8,128)(2,1)S(1)} %get-tuple-element.77.after), channel_id=1, source_target_pairs={{0,8},{4,12},{8,0},{12,4},{1,9},{5,13},{9,1},{13,5},{2,10},{6,14},... | collective-permute-start | bytes 540680 | tf_op jit(solution)/shard_map/ppermute | solution.py:33
  76.9 6.5 %collective-permute-start.33 = (bf16[4,224,128]{2,1,0:T(8,128)(2,1)S(1)}, bf16[4,224,128]{2,1,0:T(8,128)(2,1)S(1)}, u32[]{:S(2)}, u32[]{:S(2)}) collective-permute-start(bf16[4,224,128]{2,1,0:T(8,128)(2,1)S(1)} %get-tuple-element.79), channel_id=1, source_target_pairs={{0,2},{2,0},{1,3},{3,1},{4,6},{6,4},{5,7},{7,5},{8,10},{10,8},{9,1... | collective-permute-start | bytes 688136 | tf_op jit(solution)/shard_map/ppermute | solution.py:33
  80.3 13.9 %collective-permute-start.32 = (bf16[2,352,128]{2,1,0:T(8,128)(2,1)S(1)}, bf16[2,352,128]{2,1,0:T(8,128)(2,1)S(1)}, u32[]{:S(2)}, u32[]{:S(2)}) collective-permute-start(bf16[2,352,128]{2,1,0:T(8,128)(2,1)S(1)} %add.19.after.mine), channel_id=1, source_target_pairs={{0,8},{4,12},{8,0},{12,4},{1,9},{5,13},{9,1},{13,5},{2,10},{6,14},... | collective-permute-start | bytes 540680 | tf_op jit(solution)/shard_map/ppermute | solution.py:33
  83.4 8.2 %collective-permute-start.34 = (bf16[2,224,128]{2,1,0:T(8,128)(2,1)S(1)}, bf16[2,224,128]{2,1,0:T(8,128)(2,1)S(1)}, u32[]{:S(2)}, u32[]{:S(2)}) collective-permute-start(bf16[2,224,128]{2,1,0:T(8,128)(2,1)S(1)} %get-tuple-element.80.after), channel_id=1, source_target_pairs={{0,4},{4,0},{8,12},{12,8},{1,5},{5,1},{9,13},{13,9},{2,6},{6,2},{1... | collective-permute-start | bytes 344072 | tf_op jit(solution)/shard_map/ppermute | solution.py:33
  89.2 5.6 %collective-permute-start.37 = (bf16[2,352,128]{2,1,0:T(8,128)(2,1)S(1)}, bf16[2,352,128]{2,1,0:T(8,128)(2,1)S(1)}, u32[]{:S(2)}, u32[]{:S(2)}) collective-permute-start(bf16[2,352,128]{2,1,0:T(8,128)(2,1)S(1)} %add.20.after.mine), channel_id=1, source_target_pairs={{0,2},{2,0},{1,3},{3,1},{4,6},{6,4},{5,7},{7,5},{8,10},{10,8},{9,1... | collective-permute-start | bytes 540680 | tf_op jit(solution)/shard_map/ppermute | solution.py:33
  91.7 11.2 %collective-permute-start.42 = (bf16[2,224,128]{2,1,0:T(8,128)(2,1)S(1)}, bf16[2,224,128]{2,1,0:T(8,128)(2,1)S(1)}, u32[]{:S(2)}, u32[]{:S(2)}) collective-permute-start(bf16[2,224,128]{2,1,0:T(8,128)(2,1)S(1)} %add.21.after.mine), channel_id=1, source_target_pairs={{0,8},{4,12},{8,0},{12,4},{1,9},{5,13},{9,1},{13,5},{2,10},{6,14},... | collective-permute-start | bytes 344072 | tf_op jit(solution)/shard_map/ppermute | solution.py:33
  94.2 7.5 %collective-permute-start.36 = (bf16[2,352,128]{2,1,0:T(8,128)(2,1)S(1)}, bf16[2,352,128]{2,1,0:T(8,128)(2,1)S(1)}, u32[]{:S(2)}, u32[]{:S(2)}) collective-permute-start(bf16[2,352,128]{2,1,0:T(8,128)(2,1)S(1)} %meet.3.after.near), channel_id=1, source_target_pairs={{0,4},{4,0},{8,12},{12,8},{1,5},{5,1},{9,13},{13,9},{2,6},{6,2},{1... | collective-permute-start | bytes 540680 | tf_op jit(solution)/shard_map/ppermute | solution.py:33
  94.8 9.5 %collective-permute-start.41 = (bf16[2,352,128]{2,1,0:T(8,128)(2,1)S(1)}, bf16[2,352,128]{2,1,0:T(8,128)(2,1)S(1)}, u32[]{:S(2)}, u32[]{:S(2)}) collective-permute-start(bf16[2,352,128]{2,1,0:T(8,128)(2,1)S(1)} %meet.4.after.later.near), channel_id=1, source_target_pairs={{0,8},{4,12},{8,0},{12,4},{1,9},{5,13},{9,1},{13,5},{2,10},{6,14},... | collective-permute-start | bytes 540680 | tf_op jit(solution)/shard_map/ppermute | solution.py:33
  101.7 7.5 %collective-permute-start.38 = (bf16[4,352,128]{2,1,0:T(8,128)(2,1)S(1)}, bf16[4,352,128]{2,1,0:T(8,128)(2,1)S(1)}, u32[]{:S(2)}, u32[]{:S(2)}) collective-permute-start(bf16[4,352,128]{2,1,0:T(8,128)(2,1)S(1)} %join.3.after.refs_0_), channel_id=1, source_target_pairs={{0,2},{2,0},{1,3},{3,1},{4,6},{6,4},{5,7},{7,5},{8,10},{10,8},{9,1... | collective-permute-start | bytes 1081352 | tf_op jit(solution)/shard_map/ppermute | solution.py:33
  102.9 13.4 %collective-permute-start.39 = (bf16[4,352,128]{2,1,0:T(8,128)(2,1)S(1)}, bf16[4,352,128]{2,1,0:T(8,128)(2,1)S(1)}, u32[]{:S(2)}, u32[]{:S(2)}) collective-permute-start(bf16[4,352,128]{2,1,0:T(8,128)(2,1)S(1)} %join.3.after.refs_0_), channel_id=1, source_target_pairs={{0,1},{1,0},{2,3},{3,2},{4,5},{5,4},{6,7},{7,6},{8,9},{9,8},{10,11... | collective-permute-start | bytes 1081352 | tf_op jit(solution)/shard_map/ppermute | solution.py:33
  102.9 6.0 %collective-permute-start.46 = (bf16[2,224,128]{2,1,0:T(8,128)(2,1)S(1)}, bf16[2,224,128]{2,1,0:T(8,128)(2,1)S(1)}, u32[]{:S(2)}, u32[]{:S(2)}) collective-permute-start(bf16[2,224,128]{2,1,0:T(8,128)(2,1)S(1)} %meet.5.after.later.near), channel_id=1, source_target_pairs={{0,4},{4,0},{8,12},{12,8},{1,5},{5,1},{9,13},{13,9},{2,6},{6,2},{1... | collective-permute-start | bytes 344072 | tf_op jit(solution)/shard_map/ppermute | solution.py:33
  104.3 11.9 %collective-permute-start.43 = (bf16[4,352,128]{2,1,0:T(8,128)(2,1)S(1)}, bf16[4,352,128]{2,1,0:T(8,128)(2,1)S(1)}, u32[]{:S(2)}, u32[]{:S(2)}) collective-permute-start(bf16[4,352,128]{2,1,0:T(8,128)(2,1)S(1)} %join.4.after.refs_4_), channel_id=1, source_target_pairs={{0,4},{4,0},{8,12},{12,8},{1,5},{5,1},{9,13},{13,9},{2,6},{6,2},{1... | collective-permute-start | bytes 1081352 | tf_op jit(solution)/shard_map/ppermute | solution.py:33
  109.2 7.6 %collective-permute-start.47 = (bf16[4,224,128]{2,1,0:T(8,128)(2,1)S(1)}, bf16[4,224,128]{2,1,0:T(8,128)(2,1)S(1)}, u32[]{:S(2)}, u32[]{:S(2)}) collective-permute-start(bf16[4,224,128]{2,1,0:T(8,128)(2,1)S(1)} %join.5.refs_8_), channel_id=1, source_target_pairs={{0,2},{2,0},{1,3},{3,1},{4,6},{6,4},{5,7},{7,5},{8,10},{10,8},{9,1... | collective-permute-start | bytes 688136 | tf_op jit(solution)/shard_map/ppermute | solution.py:33
  110.4 6.5 %collective-permute-start.44 = (bf16[4,352,128]{2,1,0:T(8,128)(2,1)S(1)}, bf16[4,352,128]{2,1,0:T(8,128)(2,1)S(1)}, u32[]{:S(2)}, u32[]{:S(2)}) collective-permute-start(bf16[4,352,128]{2,1,0:T(8,128)(2,1)S(1)} %join.4.after.refs_4_), channel_id=1, source_target_pairs={{0,1},{1,0},{2,3},{3,2},{4,5},{5,4},{6,7},{7,6},{8,9},{9,8},{10,11... | collective-permute-start | bytes 1081352 | tf_op jit(solution)/shard_map/ppermute | solution.py:33
  110.4 7.9 %collective-permute-start.40 = (bf16[4,352,128]{2,1,0:T(8,128)(2,1)S(1)}, bf16[4,352,128]{2,1,0:T(8,128)(2,1)S(1)}, u32[]{:S(2)}, u32[]{:S(2)}) collective-permute-start(bf16[4,352,128]{2,1,0:T(8,128)(2,1)S(1)} %collective-permute-done.38.later.refs_1_), channel_id=1, source_target_pairs={{0,1},{1,0},{2,3},{3,2},{4,5},{5,4},{6,7},{7,6},{8,9},{9,8},{10,11... | collective-permute-start | bytes 1081352 | tf_op jit(solution)/shard_map/ppermute | solution.py:33
  116.3 2.0 %collective-permute-start.45 = (bf16[4,352,128]{2,1,0:T(8,128)(2,1)S(1)}, bf16[4,352,128]{2,1,0:T(8,128)(2,1)S(1)}, u32[]{:S(2)}, u32[]{:S(2)}) collective-permute-start(bf16[4,352,128]{2,1,0:T(8,128)(2,1)S(1)} %collective-permute-done.43.refs_5_), channel_id=1, source_target_pairs={{0,1},{1,0},{2,3},{3,2},{4,5},{5,4},{6,7},{7,6},{8,9},{9,8},{10,11... | collective-permute-start | bytes 1081352 | tf_op jit(solution)/shard_map/ppermute | solution.py:33
  116.3 2.0 %collective-permute-start.48 = (bf16[4,224,128]{2,1,0:T(8,128)(2,1)S(1)}, bf16[4,224,128]{2,1,0:T(8,128)(2,1)S(1)}, u32[]{:S(2)}, u32[]{:S(2)}) collective-permute-start(bf16[4,224,128]{2,1,0:T(8,128)(2,1)S(1)} %join.5.refs_8_), channel_id=1, source_target_pairs={{0,1},{1,0},{2,3},{3,2},{4,5},{5,4},{6,7},{7,6},{8,9},{9,8},{10,11... | collective-permute-start | bytes 688136 | tf_op jit(solution)/shard_map/ppermute | solution.py:33
  116.8 1.8 %collective-permute-start.49 = (bf16[4,224,128]{2,1,0:T(8,128)(2,1)S(1)}, bf16[4,224,128]{2,1,0:T(8,128)(2,1)S(1)}, u32[]{:S(2)}, u32[]{:S(2)}) collective-permute-start(bf16[4,224,128]{2,1,0:T(8,128)(2,1)S(1)} %collective-permute-done.47.refs_9_), channel_id=1, source_target_pairs={{0,1},{1,0},{2,3},{3,2},{4,5},{5,4},{6,7},{7,6},{8,9},{9,8},{10,11... | collective-permute-start | bytes 688136 | tf_op jit(solution)/shard_map/ppermute | solution.py:33
  (19 other events, 38.1 us)
